TPU v7x, 32 devices: a whole 2x2x4 slice. The times are simulated.
32 devices in a mesh: dp: 2 (over y), seq: 4 (over z), tensor: 4 (over x, core).
Axes of the slice: x: 2, y: 2, z: 4, core: 2. Of those that a mesh axis runs over, the one named last changes fastest.
Arguments:
- residual: bfloat16 [4, 2048, 1024], P('dp', 'seq'), may hold values from -6 to 6
- block_order: int32 [4, 8], P('dp'), may hold values from 0 to 7, each once within a row
- projections: bfloat16 [3, 1024, 1024], P(None, None, 'tensor'), may hold values from -0.25 to 0.25
- offsets: float32 [3, 1024], P(None, 'tensor'), may hold values from -0.9 to 0.9
- mixing: bfloat16 [1024, 1024], P('tensor'), may hold values from -1.5 to 1.5
- baseline: float32 [1024], replicated, may hold values from -1.8 to 1.8
- expand: bfloat16 [1024, 4096], P(None, 'tensor'), may hold values from -0.1875 to 0.1875
- thresholds: float32 [4096], P('tensor'), may hold values from -3 to 3
- contract: bfloat16 [4096, 1024], P('tensor'), may hold values from -0.09375 to 0.09375
- norm_scale: float32 [2, 1024], replicated, may hold values from 0.1 to 1.9
- norm_shift: float32 [2, 1024], replicated, may hold values from -1.8 to 1.8
- cotangent: bfloat16 [4, 2048, 1024], P('dp', 'seq'), may hold values from -6 to 6
Outputs:
- layer_output: bfloat16 [4, 2048, 1024], P('dp', 'seq')
- grad_residual: bfloat16 [4, 2048, 1024], P('dp', 'seq')
- grad_projections: float32 [3, 1024, 1024], P(None, None, 'tensor')
- grad_offsets: float32 [3, 1024], P(None, 'tensor')
- grad_mixing: float32 [1024, 1024], P('tensor')
- grad_baseline: float32 [1024], replicated
- grad_expand: float32 [1024, 4096], P(None, 'tensor')
- grad_thresholds: float32 [4096], P('tensor')
- grad_contract: float32 [4096, 1024], P('tensor')
- grad_scale: float32 [2, 1024], replicated
- grad_shift: float32 [2, 1024], replicated
Inputs may be any that keep to these rules, and one draw needn't show every extreme that they name: Each row of block_order holds every number of 0 to 7 once.
All inputs are finite; a program needn't handle non-finite values.
Results may differ from a plain program's by a relative error of at most 0.017.
Values may be sent and summed in bfloat16 or wider, within the bound.
No kernel may reach another device: no remote copies, remote signals or barrier semaphores. Data moves between devices by JAX's collectives and lax.ppermute only.
A program may use at most 320 MiB of HBM per device.

v0:
```python
import jax
import jax.numpy as jnp
from jax import lax
from jax.sharding import PartitionSpec as P

HEAD_DIM = 64
ROT = 16


norm_eps = 1e-05
masked_value = -1e30


def normalize(values):
    centred = values - jnp.mean(values, axis=-1, keepdims=True)
    inverse = lax.rsqrt(jnp.mean(centred * centred, axis=-1, keepdims=True) + norm_eps)
    return (centred * inverse, inverse)


def norm_back(upstream, normed, inverse):
    return inverse * (
        upstream
        - jnp.mean(upstream, axis=-1, keepdims=True)
        - normed * jnp.mean(upstream * normed, axis=-1, keepdims=True)
    )


def rotate(values, positions, rot_dims, direction):
    half_dims = rot_dims // 2
    freqs = 10000.0 ** (-jnp.arange(half_dims, dtype=jnp.float32) * 2.0 / rot_dims)
    angles = positions.astype(jnp.float32)[:, :, None] * freqs
    cosine = jnp.cos(angles)[:, :, None, :]
    sine = direction * jnp.sin(angles)[:, :, None, :]
    first = values[..., :half_dims]
    second = values[..., half_dims:rot_dims]
    return jnp.concatenate(
        [first * cosine - second * sine, second * cosine + first * sine, values[..., rot_dims:]],
        axis=-1,
    )


def gelu_exact(values):
    return jax.nn.gelu(values, approximate=False)


def weights_from(queries, keys, query_places, key_places, log_total, score_scale):
    scores = (
        jnp.einsum("sqhe,skhe->shqk", queries, keys, preferred_element_type=jnp.float32)
        * score_scale
    )
    causal = key_places[:, None, None, :] <= query_places[:, None, :, None]
    return jnp.where(causal, jnp.exp(scores - log_total[..., None]), 0.0)


def on_device(
    residual,
    block_order,
    projections,
    offsets,
    mixing,
    baseline,
    expand,
    thresholds,
    contract,
    norm_scale,
    norm_shift,
    cotangent,
):
    seq_count, local_rows, model_width = residual.shape
    local_width = mixing.shape[0]
    head_count = local_width // HEAD_DIM
    group_size = lax.axis_size("seq")
    full_length = local_rows * group_size
    block_len = full_length // block_order.shape[1]
    score_scale = HEAD_DIM ** (-0.5)
    split_shape = (seq_count, local_rows, head_count, HEAD_DIM)
    full_shape = (seq_count, full_length, head_count, HEAD_DIM)
    all_places = (
        block_order[:, :, None] * block_len + jnp.arange(block_len, dtype=jnp.int32)[None, None, :]
    ).reshape(seq_count, full_length)
    own_places = lax.dynamic_slice_in_dim(
        all_places, lax.axis_index("seq") * local_rows, local_rows, 1
    )
    inputs = residual.astype(jnp.float32)
    normed, inverse = normalize(inputs)
    attn_in = (normed * norm_scale[0] + norm_shift[0]).astype(jnp.bfloat16)
    feed_in = (normed * norm_scale[1] + norm_shift[1]).astype(jnp.bfloat16)
    linear = (
        jnp.einsum("srd,ide->isre", attn_in, projections, preferred_element_type=jnp.float32)
        + offsets[:, None, None, :]
    )
    queries = rotate(linear[0].reshape(split_shape), own_places, ROT, 1.0).astype(jnp.bfloat16)
    keys = rotate(linear[1].reshape(split_shape), own_places, ROT, 1.0).astype(jnp.bfloat16)
    values = linear[2].astype(jnp.bfloat16)
    key_flat = keys.reshape(seq_count, local_rows, local_width)
    gathered_keys, gathered_values = (
        lax.all_gather(key_flat, "seq", axis=1, tiled=True),
        lax.all_gather(values, "seq", axis=1, tiled=True),
    )
    all_keys = gathered_keys.reshape(full_shape)
    all_values = gathered_values.reshape(full_shape)
    scores = (
        jnp.einsum("sqhe,skhe->shqk", queries, all_keys, preferred_element_type=jnp.float32)
        * score_scale
    )
    causal = all_places[:, None, None, :] <= own_places[:, None, :, None]
    masked = jnp.where(causal, scores, masked_value)
    row_top = jnp.max(masked, axis=-1)
    log_total = row_top + jnp.log(jnp.sum(jnp.exp(masked - row_top[..., None]), axis=-1))
    probs = jnp.where(causal, jnp.exp(scores - log_total[..., None]), 0.0)
    attended = jnp.einsum(
        "shqk,skhe->sqhe",
        probs.astype(jnp.bfloat16),
        all_values,
        preferred_element_type=jnp.float32,
    )
    attended_low = attended.reshape(seq_count, local_rows, local_width).astype(jnp.bfloat16)
    hidden = (
        jnp.einsum("srd,df->srf", feed_in, expand, preferred_element_type=jnp.float32) + thresholds
    )
    activated = gelu_exact(hidden).astype(jnp.bfloat16)
    partial_out = (
        jnp.einsum("srh,hd->srd", attended_low, mixing, preferred_element_type=jnp.float32)
        + jnp.einsum("srf,fd->srd", activated, contract, preferred_element_type=jnp.float32)
    ).astype(jnp.bfloat16)
    branch_total = lax.psum(partial_out.astype(jnp.float32).astype(jnp.bfloat16), "tensor").astype(
        jnp.float32
    )
    layer_output = (inputs + branch_total + baseline).astype(jnp.bfloat16)
    upstream = cotangent.astype(jnp.float32)
    grad_baseline = jnp.sum(upstream, axis=(0, 1))
    grad_mixing = jnp.einsum(
        "srh,srd->hd", attended_low, cotangent, preferred_element_type=jnp.float32
    )
    grad_contract = jnp.einsum(
        "srf,srd->fd", activated, cotangent, preferred_element_type=jnp.float32
    )
    grad_attended = jnp.einsum(
        "srd,hd->srh", cotangent, mixing, preferred_element_type=jnp.float32
    ).astype(jnp.bfloat16)
    grad_activated = jnp.einsum(
        "srd,fd->srf", cotangent, contract, preferred_element_type=jnp.float32
    )
    grad_hidden = jax.vjp(gelu_exact, hidden)[1](grad_activated)[0].astype(jnp.bfloat16)
    grad_expand = jnp.einsum(
        "srd,srf->df", feed_in, grad_hidden, preferred_element_type=jnp.float32
    )
    grad_thresholds = jnp.sum(grad_hidden.astype(jnp.float32), axis=(0, 1))
    grad_feed_in = jnp.einsum(
        "srf,df->srd", grad_hidden, expand, preferred_element_type=jnp.float32
    ).astype(jnp.bfloat16)
    grad_heads = grad_attended.reshape(split_shape)
    probs_again = weights_from(queries, all_keys, own_places, all_places, log_total, score_scale)
    dots = jnp.einsum("sqhe,skhe->shqk", grad_heads, all_values, preferred_element_type=jnp.float32)
    row_dots = jnp.sum(probs_again * dots, axis=-1)
    slopes = (score_scale * probs_again * (dots - row_dots[..., None])).astype(jnp.bfloat16)
    grad_queries = jnp.einsum(
        "shqk,skhe->sqhe", slopes, all_keys, preferred_element_type=jnp.float32
    )
    key_terms = jnp.einsum(
        "shqk,sqhe->skhe", slopes, queries, preferred_element_type=jnp.float32
    ).reshape(seq_count, full_length, local_width)
    value_terms = jnp.einsum(
        "shqk,sqhe->skhe",
        probs_again.astype(jnp.bfloat16),
        grad_heads,
        preferred_element_type=jnp.float32,
    ).reshape(seq_count, full_length, local_width)
    summed_keys, summed_values = (
        lax.psum_scatter(
            key_terms.astype(jnp.bfloat16), "seq", scatter_dimension=1, tiled=True
        ).astype(jnp.float32),
        lax.psum_scatter(
            value_terms.astype(jnp.bfloat16), "seq", scatter_dimension=1, tiled=True
        ).astype(jnp.float32),
    )
    grad_keys = summed_keys.reshape(split_shape)
    grad_values = summed_values.reshape(split_shape)
    flat_shape = (seq_count, local_rows, local_width)
    grad_linear = jnp.stack(
        [
            rotate(grad_queries, own_places, ROT, -1.0).reshape(flat_shape),
            rotate(grad_keys, own_places, ROT, -1.0).reshape(flat_shape),
            grad_values.reshape(flat_shape),
        ]
    ).astype(jnp.bfloat16)
    grad_projections = jnp.einsum(
        "srd,isre->ide", attn_in, grad_linear, preferred_element_type=jnp.float32
    )
    grad_offsets = jnp.sum(grad_linear.astype(jnp.float32), axis=(1, 2))
    grad_attn_in = jnp.einsum(
        "isre,ide->srd", grad_linear, projections, preferred_element_type=jnp.float32
    ).astype(jnp.bfloat16)
    input_attn, input_feed = (
        lax.psum(grad_attn_in.astype(jnp.float32).astype(jnp.bfloat16), "tensor").astype(
            jnp.float32
        ),
        lax.psum(grad_feed_in.astype(jnp.float32).astype(jnp.bfloat16), "tensor").astype(
            jnp.float32
        ),
    )
    grad_scale = jnp.stack(
        [jnp.sum(input_attn * normed, axis=(0, 1)), jnp.sum(input_feed * normed, axis=(0, 1))]
    )
    grad_shift = jnp.stack([jnp.sum(input_attn, axis=(0, 1)), jnp.sum(input_feed, axis=(0, 1))])
    combined = input_attn * norm_scale[0] + input_feed * norm_scale[1]
    grad_residual = (upstream + norm_back(combined, normed, inverse)).astype(jnp.bfloat16)
    (
        grad_projections,
        grad_offsets,
        grad_mixing,
        grad_baseline,
        grad_expand,
        grad_thresholds,
        grad_contract,
        grad_scale,
        grad_shift,
    ) = lax.psum(
        (
            grad_projections,
            grad_offsets,
            grad_mixing,
            grad_baseline,
            grad_expand,
            grad_thresholds,
            grad_contract,
            grad_scale,
            grad_shift,
        ),
        ("dp", "seq"),
    )
    return (
        layer_output,
        grad_residual,
        grad_projections,
        grad_offsets,
        grad_mixing,
        grad_baseline,
        grad_expand,
        grad_thresholds,
        grad_contract,
        grad_scale,
        grad_shift,
    )


def solution(mesh):
    in_specs = (
        P("dp", "seq", None),
        P("dp", None),
        P(None, None, "tensor"),
        P(None, "tensor"),
        P("tensor", None),
        P(),
        P(None, "tensor"),
        P("tensor"),
        P("tensor", None),
        P(),
        P(),
        P("dp", "seq", None),
    )
    out_specs = (
        P("dp", "seq", None),
        P("dp", "seq", None),
        P(None, None, "tensor"),
        P(None, "tensor"),
        P("tensor", None),
        P(),
        P(None, "tensor"),
        P("tensor"),
        P("tensor", None),
        P(),
        P(),
    )
    return jax.shard_map(
        on_device, mesh=mesh, in_specs=in_specs, out_specs=out_specs, check_vma=False
    )
```

profile of v0, /device:TPU:0, one launch (start us, length us, event | category | flops | bytes accessed | tf_op | source)
XLA Modules:
  0.0 828.6 jit_solution(7756911481575855506)
XLA Ops:
  7.3 0.5 multiply_power_fusion
  7.8 2.3 convert_reduce_fusion.2
  10.2 2.3 fusion.14
  12.5 0.6 fusion.57
  13.1 0.6 fusion.58
  13.7 0.6 copy-done.30
  14.3 2.2 add_bitcast_fusion
  16.6 1.7 copy-done.12
  18.2 1.2 fusion.56
  19.4 0.1 broadcast_bitcast_fusion
  19.5 0.6 copy.40
  20.1 0.6 copy.41
  20.7 1.2 slice.120
  21.9 0.7 broadcast_add_fusion
  22.6 0.6 fusion.54
  23.2 1.5 broadcast_multiply_fusion
  24.7 0.6 copy-done.17
  25.3 1.7 subtract_convert_fusion.3
  27.0 0.8 pad_maximum_fusion.2
  27.9 2.1 slice.118
  30.0 0.5 reduce-scatter.3.cloned.1.call-start
  30.6 3.1 broadcast_compare_fusion
  33.7 2.4 convolution_convert_fusion.3
  36.2 7.2 fusion.44
  43.3 33.4 %all-gather.4.cloned.1.call-done = bf16[2,2048,256]{1,2,0:T(8,128)(2,1)} async-done(((bf16[2,512,256]{1,2,0:T(8,128)(2,1)}), bf16[2,2048,256]{1,2,0:T(8,128)(2,1)}) %all-gather.4.cloned.1.call-update) | async-done | bytes 2097168 | tf_op jit(solution)/shard_map/all_gather | solution.py:97
  76.7 16.6 %select_reduce_fusion = (f32[2,4,512]{2,1,0:T(4,128)S(1)}, f32[2,4,512,2048]{3,2,1,0:T(8,128)}) fusion(pred[2,512,2048]{2,1,0:T(8,128)(4,1)} %broadcast_compare_fusion, bf16[2,2048,4,64]{1,3,2,0:T(8,128)(2,1)} %bitcast.111, bf16[2,512,4,48]{1,3,2,0:T(8,128)(2,1)S(1)} %slice.121, bf16[2,512,4,8]{1,3,2,0:T(8,128)(2,1)} %get-tuple-element.56, ...), kind=kOutput, calls=%fused_computation.4 | convolution fusion | flops 1100476416 | bytes 38289408 | tf_op jit(solution)/shard_map/sqhe,skhe->shqk/dot_general | solution.py:103
  93.3 15.1 %exponential_reduce_fusion = f32[2,4,512]{2,1,0:T(4,128)S(1)} fusion(f32[2,4,512,2048]{3,2,1,0:T(8,128)} %get-tuple-element.72, f32[2,4,512]{2,1,0:T(4,128)S(1)} %get-tuple-element.71, pred[2,512,2048]{2,1,0:T(8,128)(4,1)S(1)} %copy-done.1), kind=kLoop, calls=%fused_computation.3 | loop fusion | flops 33550336 | bytes 35684352 | tf_op jit(solution)/shard_map/reduce_sum | solution.py:109
  108.5 15.1 %all-gather.6.cloned.1.call-done = bf16[1,2,2048,256]{2,3,0,1:T(8,128)(2,1)} async-done(((bf16[1,2,512,256]{2,3,0,1:T(8,128)(2,1)}), bf16[1,2,2048,256]{2,3,0,1:T(8,128)(2,1)}) %all-gather.6.cloned.1.call-update) | async-done | bytes 2097168 | tf_op jit(solution)/shard_map/all_gather | solution.py:98
  123.6 27.1 %multiply_reduce_fusion = (f32[2,4,512]{2,1,0:T(4,128)}, f32[2,4,512,2048]{3,2,1,0:T(8,128)}) fusion(f32[2,4,512,2048]{3,2,1,0:T(8,128)} %get-tuple-element.72, f32[2,4,512]{2,1,0:T(4,128)S(1)} %bitcast.121, pred[2,512,2048]{2,1,0:T(8,128)(4,1)} %broadcast_compare_fusion, bf16[2,512,4,64]{1,3,2,0:T(8,128)(2,1)S(1)} %bitcast.125, ...), kind=kOutput, calls=%fused_computation.1 | convolution fusion | flops 1115680768 | bytes 71860224 | tf_op jit(solution)/shard_map/sqhe,skhe->shqk/dot_general | solution.py:154
  150.6 28.6 %multiply_convert_fusion = bf16[2,4,512,2048]{3,2,1,0:T(8,128)(2,1)} fusion(f32[2,4,512,2048]{3,2,1,0:T(8,128)} %get-tuple-element.74, f32[2,4,512,2048]{3,2,1,0:T(8,128)} %get-tuple-element.72, f32[2,4,512]{2,1,0:T(4,128)} %get-tuple-element.73, f32[2,4,512]{2,1,0:T(4,128)S(1)} %bitcast.122, pred[2,512,2048]{2,1,0:T(8,128)(4,1)} %broadcast_compare_fusion), kind=kLoop, calls=%fused_computation | loop fusion | flops 58720256 | bytes 86016000 | tf_op jit(solution)/shard_map/convert_element_type | solution.py:156
  179.2 10.2 %convolution_convert_fusion.1 = bf16[2,4,64,2048]{3,2,1,0:T(8,128)(2,1)} fusion(bf16[2,4,512,2048]{3,2,1,0:T(8,128)(2,1)} %multiply_convert_fusion, bf16[2,512,4,48]{1,3,2,0:T(8,128)(2,1)S(1)} %slice.121, bf16[2,512,4,8]{1,3,2,0:T(8,128)(2,1)} %get-tuple-element.56, bf16[2,512,4,8]{1,3,2,0:T(8,128)(2,1)} %get-tuple-element.55), kind=kOutput, calls=%fused_computation.65 | convolution fusion | flops 1076363264 | bytes 19398656 | tf_op jit(solution)/shard_map/shqk,sqhe->skhe/dot_general | solution.py:160
  189.5 11.2 %multiply_convert_fusion.1 = (bf16[2,512,1024]{2,1,0:T(8,128)(2,1)S(1)}, f32[2,512,1024]{2,1,0:T(8,128)S(1)}) fusion(f32[2,512,1024]{2,1,0:T(8,128)} %get-tuple-element.70, f32[1024]{0:T(1024)} %param.19, u8[512,1024]{1,0:T(8,128)(4,1)} %get-tuple-element.27, u8[512,1024]{1,0:T(8,128)(4,1)S(1)} %get-tuple-element.26), kind=kLoop, calls=%fused_computation.48 | loop fusion | flops 74448896 | bytes 11538432 | tf_op jit(solution)/shard_map/convert_element_type | solution.py:121
  200.8 4.4 fusion.30
  205.2 5.6 convert_reduce_fusion.4
  210.8 15.7 %convolution_convert_fusion = bf16[2,4,64,2048]{3,2,1,0:T(8,128)(2,1)} fusion(bf16[2,512,4,64]{1,3,2,0:T(8,128)(2,1)S(1)} %bitcast.126, f32[2,4,512,2048]{3,2,1,0:T(8,128)} %get-tuple-element.72, f32[2,4,512]{2,1,0:T(4,128)S(1)} %bitcast.123, pred[2,512,2048]{2,1,0:T(8,128)(4,1)} %broadcast_compare_fusion), kind=kOutput, calls=%fused_computation.64 | convolution fusion | flops 1108344832 | bytes 38289408 | tf_op jit(solution)/shard_map/shqk,sqhe->skhe/dot_general | solution.py:163
  226.5 3.9 copy.25
  230.4 0.4 all-reduce.8.cloned.1.call-start
  230.9 5.3 fusion.36
  236.2 12.0 %convolution_bitcast_fusion.4 = f32[2,512,4,64]{1,3,2,0:T(8,128)S(1)} fusion(bf16[2,2048,4,64]{1,3,2,0:T(8,128)(2,1)} %bitcast.112, bf16[2,4,512,2048]{3,2,1,0:T(8,128)(2,1)} %multiply_convert_fusion), kind=kOutput, calls=%fused_computation.83 | convolution fusion | flops 1073741824 | bytes 19922944 | tf_op jit(solution)/shard_map/shqk,skhe->sqhe/dot_general | solution.py:157
  248.2 16.2 %convolution_convert_fusion.2 = bf16[2,4,64,512]{3,2,1,0:T(8,128)(2,1)} fusion(bf16[2,2048,4,64]{1,3,2,0:T(8,128)(2,1)} %bitcast.114, f32[2,4,512,2048]{3,2,1,0:T(8,128)} %get-tuple-element.72, f32[2,4,512]{2,1,0:T(4,128)S(1)} %bitcast.124, pred[2,512,2048]{2,1,0:T(8,128)(4,1)} %broadcast_compare_fusion), kind=kOutput, calls=%fused_computation.84 | convolution fusion | flops 1107558400 | bytes 38289408 | tf_op jit(solution)/shard_map/shqk,skhe->sqhe/dot_general | solution.py:111
  264.4 4.6 add_convert_fusion.1
  269.0 1.2 reshape.124
  270.2 1.0 slice.97
  271.2 0.8 subtract_convert_fusion.1
  272.1 0.9 pad_maximum_fusion.3
  273.0 0.2 copy.26
  273.2 1.2 copy.27
  274.4 3.8 reduce-scatter.5.cloned.1.call-done
  278.2 4.7 bitcast_convert_fusion
  283.0 0.2 all-reduce.6.cloned.1.call-start
  283.2 6.8 convolution_bitcast_fusion
  290.1 4.8 convolution_bitcast_fusion.1
  294.9 1.7 convolution_bitcast_fusion.3
  296.6 3.8 convolution_bitcast_fusion.2
  300.5 1.3 convert_reduce_fusion.5
  301.8 100.7 %all-reduce.8.cloned.1.call-done = (bf16[2,512,1024]{2,1,0:T(8,128)(2,1)}, bf16[2,512,1024]{2,1,0:T(8,128)(2,1)}, bf16[2,512,1024]{2,1,0:T(8,128)(2,1)}) async-done(((bf16[2,512,1024]{2,1,0:T(8,128)(2,1)}, bf16[2,512,1024]{2,1,0:T(8,128)(2,1)}, bf16[2,512,1024]{2,1,0:T(8,128)(2,1)}), (bf16[2,512,1024]{2,1,0:T(8,128)(2,1)}, bf16[2,512,1024]{2,1,0:T(8,128)(2,1)}, ...) | async-done | bytes 6291472 | tf_op jit(solution)/shard_map/psum | solution.py:126
  402.4 5.3 fusion.20
  407.8 5.9 convert_reduce_fusion.3
  413.7 40.6 %all-reduce = (f32[3,256]{1,0:T(4,128)}, f32[1024]{0:T(1024)}, f32[1024]{0:T(1024)}, f32[2,1024]{1,0:T(2,128)}, f32[2,1024]{1,0:T(2,128)}) all-reduce(f32[3,256]{1,0:T(4,128)S(1)} %convert_reduce_fusion.5, f32[1024]{0:T(1024)S(1)} %get-tuple-element.48, ...), channel_id=1, replica_groups=mesh['dp'=2,'seq'=4,'tensor'=4] {'dp','seq'}, use_global_device_ids=true, to_apply=%region_14.15 | all-reduce | flops 6912 | bytes 55296 | tf_op jit(solution)/shard_map/psum | solution.py:218
  454.3 355.6 %all-reduce.6.cloned.1.call-done = (f32[3,1024,256]{1,2,0:T(8,128)}, f32[256,1024]{1,0:T(8,128)}, f32[1024,1024]{1,0:T(8,128)}, f32[1024,1024]{1,0:T(8,128)}) async-done(((f32[3,1024,256]{1,2,0:T(8,128)}, f32[256,1024]{1,0:T(8,128)}, f32[1024,1024]{1,0:T(8,128)}, f32[1024,1024]{1,0:T(8,128)}), (f32[3,1024,256]{1,2,0:T(8,128)}, f32[256,1024]{1,0:T(8,128)}, f32[1024,1024]{1,0:T(8,128)}, ...) | async-done | bytes 12582928 | tf_op jit(solution)/shard_map/psum | solution.py:218
  810.0 3.6 copy.31
  813.6 1.0 copy.49
  814.6 4.9 copy.50
  819.5 2.0 copy.51
  (94 shorter events, 0.6 us)
Async XLA Ops:
  7.2 29.0 %copy-start = (bf16[1024,1024]{1,0:T(8,128)(2,1)S(1)}, bf16[1024,1024]{1,0:T(8,128)(2,1)}, u32[]{:S(2)}) copy-start(bf16[1024,1024]{1,0:T(8,128)(2,1)} %param.18) | copy-start | bytes 6291460
  7.2 5.3 copy-start.25
  7.2 5.9 copy-start.26
  7.2 7.1 copy-start.36
  7.2 69.5 %all-gather.4.cloned.1.call-start = ((), (), s32[]{:S(2)}) async-start(), calls=%async_computation.2 | async-start | bytes 2621440 | tf_op jit(solution)/shard_map/all_gather | solution.py:97
  7.3 7.0 copy-start.2
  7.3 7.0 copy-start.35
  10.1 6.4 copy-start.18
  12.5 4.1 copy-start.20
  13.1 3.5 copy-start.22
  13.7 0.6 copy-start.30
  16.5 1.7 copy-start.12
  18.2 1.2 copy-start.33
  24.7 0.6 copy-start.17
  27.8 95.7 %all-gather.6.cloned.1.call-start = ((), (), s32[]{:S(2)}) async-start(), calls=%async_computation.5 | async-start | bytes 2621440 | tf_op jit(solution)/shard_map/all_gather | solution.py:98
  30.0 239.0 %reduce-scatter.3.cloned.1.call-start = ((), (), s32[]{:S(2)}) async-start(), calls=%async_computation.3 | async-start | bytes 2621440 | tf_op jit(solution)/shard_map/reduce_scatter | solution.py:170
  30.5 5.6 copy-start.3
  76.7 16.6 %copy-start.1 = (pred[2,512,2048]{2,1,0:T(8,128)(4,1)S(1)}, pred[2,512,2048]{2,1,0:T(8,128)(4,1)}, u32[]{:S(2)}) copy-start(pred[2,512,2048]{2,1,0:T(8,128)(4,1)} %broadcast_compare_fusion) | copy-start | bytes 6291460
  189.4 88.8 %reduce-scatter.5.cloned.1.call-start = ((), (), s32[]{:S(2)}) async-start(), calls=%async_computation.4 | async-start | bytes 2621440 | tf_op jit(solution)/shard_map/reduce_scatter | solution.py:173
  189.5 11.3 %copy-start.34 = (bf16[1024,1024]{1,0:T(8,128)(2,1)S(1)}, bf16[1024,1024]{1,0:T(8,128)(2,1)}, u32[]{:S(2)}) copy-start(bf16[1024,1024]{1,0:T(8,128)(2,1)} %param.20) | copy-start | bytes 6291460
  200.7 4.4 copy-start.14
  200.7 4.4 copy-start.6
  200.8 4.4 copy-start.11
  200.8 4.4 copy-start.27
  230.4 172.0 %all-reduce.8.cloned.1.call-start = ((), (), s32[]{:S(2)}) async-start(), calls=%async_computation.7 | async-start | bytes 12582912 | tf_op jit(solution)/shard_map/psum | solution.py:126
  283.0 7.1 copy-start.19
  283.0 7.1 copy-start.21
  283.0 7.0 copy-start.24
  283.0 7.0 copy-start.32
  283.0 527.0 %all-reduce.6.cloned.1.call-start = ((), (), s32[]{:S(2)}) async-start(), calls=%async_computation.6 | async-start | bytes 25165824 | tf_op jit(solution)/shard_map/psum | solution.py:218
  283.2 6.8 copy-start.4
  283.2 6.8 copy-start.37
  290.1 4.8 copy-start.7
  290.1 4.8 copy-start.13
  290.1 6.5 copy-start.16
  290.1 6.5 copy-start.23
  290.1 6.5 copy-start.31
  300.4 107.3 %copy-start.28 = (f32[1024]{0:T(1024)S(1)}, f32[1024]{0:T(1024)}, u32[]{:S(2)}) copy-start(f32[1024]{0:T(1024)} %param.17) | copy-start | bytes 12292
  402.4 5.4 copy-start.5
  402.4 5.4 copy-start.8
  402.4 5.4 copy-start.9
  407.8 5.9 copy-start.29
  810.0 3.6 copy-start.15
  814.6 4.9 copy-start.10
Sparse Core Ops, SparseCore 0:
  28.0 48.7 all-gather.3
  78.9 44.6 all-gather.5
  189.6 42.5 reduce-scatter.2
  235.0 43.1 reduce-scatter.4
  283.1 119.3 all-reduce.7
  408.2 401.7 all-reduce.5
where the time goes:
time: 833 us; the launch traced here: 829 us
  waiting for transfers between devices  509 us (61%)
  matrix products  151 us (18%)
  other arithmetic  83.9 us (10%)
  blocking collectives  40.6 us (5%)
  local copies, waits for them, and re-layouts  28 us (3%)
  between operations  14.8 us (2%)
    psum x1, waiting for transfers between devices, on_device(): lax.psum((grad_projections, grad_offsets, grad_mixing, grad_baseline, gra...  356 us
    psum x1, waiting for transfers between devices, on_device(): lax.psum(partial_out.astype(jnp.float32).astype(jnp.bfloat16), 'tensor')  101 us
    psum x1, blocking collectives, on_device(): lax.psum((grad_projections, grad_offsets, grad_mixing, grad_baseline, gra...  40.6 us
    all_gather x1, waiting for transfers between devices, on_device(): lax.all_gather(key_flat, 'seq', axis=1, tiled=True)  33.4 us
    convert_element_type x1, other arithmetic, on_device(): (score_scale * probs_again * (dots - row_dots[..., None])).astype(jnp.bfl...  28.6 us
    dot_general x1, matrix products, on_device(): jnp.einsum('sqhe,skhe->shqk', grad_heads, all_values, preferred_element_t...  27.1 us
  transfers between devices with their start and end apart: 6, of which 5 were waited for; matrix products, arithmetic and copies ran while one was open for 19% of the time, Pallas kernels for 0%

commit v1 on v0

v1 whole, which is shorter than its diff:
```python
import functools

import jax
import jax.numpy as jnp
import numpy as np
from jax import lax
from jax.experimental import pallas as pl
from jax.experimental.pallas import tpu as pltpu
from jax.sharding import PartitionSpec as P

HEAD_DIM = 64
ROT = 16
LANES = 128

norm_eps = 1e-05
masked_value = -1e30
low = jnp.bfloat16
wide = jnp.float32


def dot_nn(a, b):
    return lax.dot_general(a, b, (((1,), (0,)), ((), ())), preferred_element_type=wide)


def dot_nt(a, b):
    return lax.dot_general(a, b, (((1,), (1,)), ((), ())), preferred_element_type=wide)


def rotary_tables(length):
    half = ROT // 2
    freqs = np.float32(10000.0) ** (-np.arange(half, dtype=np.float32) * 2.0 / ROT)
    angles = np.arange(length, dtype=np.float32)[:, None] * freqs.astype(np.float32)
    cosine = np.ones((length, HEAD_DIM), np.float32)
    sine = np.zeros((length, HEAD_DIM), np.float32)
    cosine[:, :half] = np.cos(angles)
    cosine[:, half:ROT] = np.cos(angles)
    sine[:, :half] = -np.sin(angles)
    sine[:, half:ROT] = np.sin(angles)
    return np.tile(cosine, (1, LANES // HEAD_DIM)), np.tile(sine, (1, LANES // HEAD_DIM))


def rotate_lanes(x, cosine, sine):
    width = x.shape[1]
    if width < LANES:
        x = jnp.concatenate([x, x], axis=1)
    lane = lax.broadcasted_iota(jnp.int32, x.shape, 1) % HEAD_DIM
    partner = jnp.where(
        lane < ROT // 2, pltpu.roll(x, LANES - ROT // 2, 1), pltpu.roll(x, ROT // 2, 1)
    )
    return (x * cosine + partner * sine)[:, :width]


def project_kernel(
    places, res, cot, proj, offs, mix, scale, shift, cosine, sine, out, attn_out, feed_out
):
    x = res[0].astype(wide)
    centred = x - jnp.mean(x, axis=1, keepdims=True)
    inverse = lax.rsqrt(jnp.mean(centred * centred, axis=1, keepdims=True) + norm_eps)
    normed = centred * inverse
    attn_in = (normed * scale[0:1] + shift[0:1]).astype(low)
    attn_out[0] = attn_in
    feed_out[0] = (normed * scale[1:2] + shift[1:2]).astype(low)
    parts, width = out.shape[0], out.shape[4]
    for i in range(3):
        linear = dot_nn(attn_in, proj[i]) + offs[i : i + 1]
        if i < 2:
            linear = jnp.concatenate(
                [
                    rotate_lanes(linear[:, c : c + LANES], cosine[...], sine[...])
                    for c in range(0, linear.shape[1], LANES)
                ],
                axis=1,
            )
        linear = linear.astype(low)
        for w in range(parts):
            out[w, i, 0] = linear[:, w * width : (w + 1) * width]
    grad = dot_nt(cot[0], mix[...]).astype(low)
    for w in range(parts):
        out[w, 3, 0] = grad[:, w * width : (w + 1) * width]


def project(residual, cotangent, places, projections, offsets, mixing, scale, shift, tables, dims):
    blocks, span, model = residual.shape
    n, per_device, width = dims
    local = projections.shape[2]
    parts = local // width
    whole = lambda *shape: pl.BlockSpec(shape, lambda t, p: (0,) * len(shape))
    token = pl.BlockSpec((1, span, model), lambda t, p: (t, 0, 0))
    table = pl.BlockSpec((span, LANES), lambda t, p: (p[t], 0))
    return pl.pallas_call(
        project_kernel,
        grid_spec=pltpu.PrefetchScalarGridSpec(
            num_scalar_prefetch=1,
            grid=(blocks,),
            in_specs=[
                token,
                token,
                whole(3, model, local),
                whole(3, local),
                whole(local, model),
                whole(2, model),
                whole(2, model),
                table,
                table,
            ],
            out_specs=[
                pl.BlockSpec(
                    (parts, 4, 1, span, width),
                    lambda t, p: (t // per_device, 0, t % per_device, 0, 0),
                ),
                token,
                token,
            ],
        ),
        out_shape=[
            jax.ShapeDtypeStruct((n, 4, per_device, span, width), low),
            jax.ShapeDtypeStruct((blocks, span, model), low),
            jax.ShapeDtypeStruct((blocks, span, model), low),
        ],
        compiler_params=pltpu.CompilerParams(vmem_limit_bytes=40 * 2**20),
    )(places, residual, cotangent, projections, offsets, mixing, scale, shift, *tables)


def attention_kernel(n, per_device, slots, *refs):
    received, refs = refs[:n], refs[n:]
    cosine, sine = refs[0], refs[1]
    outs_o, refs = refs[2 : 2 + n], refs[2 + n :]
    outs_d, refs = refs[:n], refs[n:]
    xs, ys_o, ys_d, k_turned, v_turned, strip, dk_sum, dv_sum, sems = refs
    blocks = n * per_device
    span, width = xs.shape[3], xs.shape[4]
    heads = width // HEAD_DIM
    scale = HEAD_DIM ** (-0.5)
    to_log2 = scale * float(np.log2(np.e))

    copies = [pltpu.make_async_copy(received[k], xs.at[k], sems.at[k]) for k in range(n)]
    for copy in copies:
        copy.start()
    dk_sum[...] = jnp.zeros_like(dk_sum)
    dv_sum[...] = jnp.zeros_like(dv_sum)
    for copy in copies:
        copy.wait()

    def place(j):
        slot = slots[j]
        return slot // per_device, slot % per_device

    def turn(j, _):
        a, b = place(j)
        k_turned[j] = xs[a, 1, b].astype(wide).T.astype(low)
        v_turned[j] = xs[a, 2, b].astype(wide).T.astype(low)
        return 0

    lax.fori_loop(0, blocks, turn, 0)

    lane_head = lax.broadcasted_iota(jnp.int32, (span, width), 1) // HEAD_DIM

    def stacked(x):
        if heads == 1:
            return x
        return jnp.concatenate(
            [jnp.where(lane_head == h, x, jnp.zeros_like(x)) for h in range(heads)], axis=0
        )

    def head_rows(h):
        return slice(h * HEAD_DIM, (h + 1) * HEAD_DIM)

    def head_cols(h):
        return slice(h * span, (h + 1) * span)

    shape = (span, heads * span)
    allowed = lax.broadcasted_iota(jnp.int32, shape, 0) <= (
        lax.broadcasted_iota(jnp.int32, shape, 1) % span
    )

    def query_block(i, _):
        a, b = place(i)
        q, g = xs[a, 0, b], xs[a, 3, b]
        q_all, g_all = stacked(q), stacked(g)
        g_turned = g.astype(wide).T

        own = jnp.where(allowed, dot_nt(xs[a, 1, b], q_all), masked_value)
        strip[i] = own
        top = jnp.max(own, axis=0, keepdims=True)

        def scores(j, top):
            c, d = place(j)
            s = dot_nt(xs[c, 1, d], q_all)
            strip[j] = s
            return jnp.maximum(top, jnp.max(s, axis=0, keepdims=True))

        top = lax.fori_loop(0, i, scores, top)

        def weigh(j, carry):
            total, outs = carry
            p = jnp.exp2((strip[j] - top) * to_log2)
            strip[j] = p
            p_low = p.astype(low)
            return total + jnp.sum(p, axis=0, keepdims=True), tuple(
                outs[h] + dot_nn(v_turned[j, head_rows(h)], p_low[:, head_cols(h)])
                for h in range(heads)
            )

        zeros = tuple(jnp.zeros((HEAD_DIM, span), wide) for _ in range(heads))
        total, outs = lax.fori_loop(
            0, i + 1, weigh, (jnp.zeros((1, heads * span), wide), zeros)
        )
        recip = 1.0 / total
        outs = [outs[h] * recip[:, head_cols(h)] for h in range(heads)]
        row_dots = jnp.concatenate(
            [
                jnp.sum(outs[h] * g_turned[head_rows(h)], axis=0, keepdims=True)
                for h in range(heads)
            ],
            axis=1,
        )
        ys_o[a, b] = jnp.concatenate(outs, axis=0).T.astype(low)
        slope_scale = scale * recip
        slope_shift = slope_scale * row_dots

        def back(j, dq):
            c, d = place(j)
            p = strip[j]
            dots = dot_nt(xs[c, 2, d], g_all)
            slopes = (p * (dots * slope_scale - slope_shift)).astype(low)
            dv_sum[j] += dot_nn((p * recip).astype(low), g_all)
            dk_sum[j] += dot_nn(slopes, q_all)
            return tuple(
                dq[h] + dot_nn(k_turned[j, head_rows(h)], slopes[:, head_cols(h)])
                for h in range(heads)
            )

        dq = lax.fori_loop(0, i + 1, back, zeros)
        dq = jnp.concatenate(dq, axis=0).T
        rows = pl.ds(pl.multiple_of(i * span, span), span)
        ys_d[a, 0, b] = rotate_lanes(dq, cosine[rows], -sine[rows]).astype(low)
        return 0

    lax.fori_loop(0, blocks, query_block, 0)

    def finish(j, _):
        a, b = place(j)
        rows = pl.ds(pl.multiple_of(j * span, span), span)
        ys_d[a, 1, b] = rotate_lanes(dk_sum[j], cosine[rows], -sine[rows]).astype(low)
        ys_d[a, 2, b] = dv_sum[j].astype(low)
        return 0

    lax.fori_loop(0, blocks, finish, 0)
    copies = [pltpu.make_async_copy(ys_o.at[k], outs_o[k], sems.at[k]) for k in range(n)]
    copies += [pltpu.make_async_copy(ys_d.at[k], outs_d[k], sems.at[n + k]) for k in range(n)]
    for copy in copies:
        copy.start()
    for copy in copies:
        copy.wait()


def attention(received, slots, tables, per_device):
    n = len(received)
    _, _, span, width = received[0].shape
    blocks = n * per_device
    heads = width // HEAD_DIM
    anywhere = pl.BlockSpec(memory_space=pl.ANY)
    vmem = pl.BlockSpec(memory_space=pltpu.VMEM)
    pairs = blocks * (blocks + 1) // 2 * heads * span * span
    results = pl.pallas_call(
        functools.partial(attention_kernel, n, per_device),
        in_specs=[pl.BlockSpec(memory_space=pltpu.SMEM)] + [anywhere] * n + [vmem] * 2,
        out_specs=[anywhere] * (2 * n),
        out_shape=[jax.ShapeDtypeStruct((per_device, span, width), low)] * n
        + [jax.ShapeDtypeStruct((3, per_device, span, width), low)] * n,
        scratch_shapes=[
            pltpu.VMEM((n, 4, per_device, span, width), low),
            pltpu.VMEM((n, per_device, span, width), low),
            pltpu.VMEM((n, 3, per_device, span, width), low),
            pltpu.VMEM((blocks, width, span), low),
            pltpu.VMEM((blocks, width, span), low),
            pltpu.VMEM((blocks, span, heads * span), wide),
            pltpu.VMEM((blocks, span, width), wide),
            pltpu.VMEM((blocks, span, width), wide),
            pltpu.SemaphoreType.DMA((2 * n,)),
        ],
        compiler_params=pltpu.CompilerParams(vmem_limit_bytes=40 * 2**20),
        cost_estimate=pl.CostEstimate(
            flops=12 * pairs * 256, bytes_accessed=8 * 2**20, transcendentals=pairs
        ),
    )(slots, *received, *tables)
    return results[:n], results[n:]


def steps_over(*axes):
    steps = []
    for axis in axes:
        size = lax.axis_size(axis)
        bit = 1
        while bit < size:
            steps.append((axis, [(s, s ^ bit) for s in range(size)], bit))
            bit *= 2
    return steps


def side_of(axis, bit):
    return (lax.axis_index(axis) // bit) % 2


def reduce_rows(x, steps):
    for axis, perm, bit in steps:
        half = x.shape[0] // 2
        side = side_of(axis, bit)
        sent = lax.dynamic_slice_in_dim(x, (1 - side) * half, half, 0).astype(low)
        kept = lax.dynamic_slice_in_dim(x, side * half, half, 0)
        got = lax.ppermute(sent, axis, perm)
        x = kept.astype(wide) + got.astype(wide)
    return x


def spread_rows(x, steps):
    for axis, perm, bit in reversed(steps):
        got = lax.ppermute(x, axis, perm)
        side = side_of(axis, bit)
        x = jnp.where(
            side == 0, jnp.concatenate([x, got], axis=0), jnp.concatenate([got, x], axis=0)
        )
    return x


def own_rows(x, steps):
    for axis, _, bit in steps:
        half = x.shape[0] // 2
        x = lax.dynamic_slice_in_dim(x, side_of(axis, bit) * half, half, 0)
    return x


def sum_small(x, steps):
    for axis, perm, _ in steps:
        x = x + lax.ppermute(x, axis, perm)
    return x


def gelu_exact(values):
    return jax.nn.gelu(values, approximate=False)


def on_device(
    residual,
    block_order,
    projections,
    offsets,
    mixing,
    baseline,
    expand,
    thresholds,
    contract,
    norm_scale,
    norm_shift,
    cotangent,
):
    seq_count, local_rows, model = residual.shape
    local = mixing.shape[0]
    n = lax.axis_size("seq")
    me = lax.axis_index("seq")
    blocks = block_order.shape[1]
    length = local_rows * n
    span = length // blocks
    per_device = blocks // n
    width = seq_count * local // n
    parts = local // width
    tokens = seq_count * local_rows
    tables = [jnp.asarray(t) for t in rotary_tables(length)]

    own_blocks = lax.dynamic_slice_in_dim(block_order, me * per_device, per_device, 1).reshape(-1)
    as_blocks = (seq_count * per_device, span, model)
    sends, attn_in, feed_in = project(
        residual.reshape(as_blocks),
        cotangent.reshape(as_blocks),
        own_blocks,
        projections,
        offsets,
        mixing,
        norm_scale,
        norm_shift,
        tables,
        (n, per_device, width),
    )
    received = [lax.dynamic_index_in_dim(sends, me, 0, keepdims=False)]
    for k in range(1, n):
        part = lax.dynamic_index_in_dim(sends, (me + k) % n, 0, keepdims=False)
        received.append(lax.ppermute(part, "seq", [(s, (s + k) % n) for s in range(n)]))

    own_order = lax.dynamic_index_in_dim(block_order, me // parts, 0, keepdims=False)
    stored = jnp.arange(blocks, dtype=jnp.int32)
    slot_of = ((me - stored // per_device) % n) * per_device + stored % per_device
    slots = jnp.sum(
        jnp.where(own_order[None, :] == stored[:, None], slot_of[None, :], 0), axis=1
    ).astype(jnp.int32)

    attn_in = attn_in.reshape(tokens, model)
    feed_in = feed_in.reshape(tokens, model)
    upstream_low = cotangent.reshape(tokens, model)
    hidden = dot_nn(feed_in, expand) + thresholds
    activated = gelu_exact(hidden).astype(low)
    grad_activated = dot_nt(upstream_low, contract)
    grad_hidden = jax.vjp(gelu_exact, hidden)[1](grad_activated)[0].astype(low)
    feed_out = dot_nn(activated, contract)
    grad_contract = lax.dot_general(
        activated, upstream_low, (((0,), (0,)), ((), ())), preferred_element_type=wide
    )
    grad_expand = lax.dot_general(
        feed_in, grad_hidden, (((0,), (0,)), ((), ())), preferred_element_type=wide
    )
    feed_part = dot_nt(grad_hidden, expand)
    grad_thresholds = jnp.sum(grad_hidden.astype(wide), axis=0)
    grad_baseline = jnp.sum(upstream_low.astype(wide), axis=0)

    batch_steps = steps_over("dp", "seq")
    tensor_steps = steps_over("tensor")

    def total_rows(x):
        return spread_rows(reduce_rows(x, batch_steps).astype(low), batch_steps).astype(wide)

    grad_contract = total_rows(grad_contract)
    grad_expand = total_rows(grad_expand)

    outs_o, outs_d = attention(received, slots, tables, per_device)

    def returned(pieces, lead):
        full = jnp.zeros((n,) + pieces[0].shape, low)
        for k in range(n):
            piece = pieces[k]
            if k:
                piece = lax.ppermute(piece, "seq", [(s, (s - k) % n) for s in range(n)])
            full = lax.dynamic_update_index_in_dim(full, piece, (me + k) % n, 0)
        full = full.reshape((seq_count, parts, lead, per_device, span, width))
        return full.transpose(2, 0, 3, 4, 1, 5).reshape(lead, tokens, local)

    attended = returned(outs_o, 1)[0]
    grad_linear = returned(outs_d, 3)

    partial_out = dot_nn(attended, mixing) + feed_out
    grad_mixing = lax.dot_general(
        attended, upstream_low, (((0,), (0,)), ((), ())), preferred_element_type=wide
    )
    flat_residual = residual.reshape(tokens, model)
    branch_total = reduce_rows(partial_out, tensor_steps)
    shard_in = own_rows(flat_residual, tensor_steps).astype(wide)
    layer_output = spread_rows(
        (shard_in + branch_total + baseline).astype(low), tensor_steps
    ).reshape(residual.shape)

    grad_projections = jnp.stack(
        [
            lax.dot_general(
                attn_in, grad_linear[i], (((0,), (0,)), ((), ())), preferred_element_type=wide
            )
            for i in range(3)
        ]
    )
    grad_offsets = jnp.sum(grad_linear.astype(wide), axis=1)
    attn_part = sum(dot_nt(grad_linear[i], projections[i]) for i in range(3))

    inputs = flat_residual.astype(wide)
    centred = inputs - jnp.mean(inputs, axis=-1, keepdims=True)
    inverse = lax.rsqrt(jnp.mean(centred * centred, axis=-1, keepdims=True) + norm_eps)
    normed = centred * inverse
    upstream_part = attn_part * norm_scale[0] + feed_part * norm_scale[1]
    small_all = jnp.stack(
        [
            jnp.sum(attn_part * normed, axis=0),
            jnp.sum(feed_part * normed, axis=0),
            jnp.sum(attn_part, axis=0),
            jnp.sum(feed_part, axis=0),
        ]
    )
    combined = reduce_rows(upstream_part, tensor_steps)
    normed_own = own_rows(normed, tensor_steps)
    inverse_own = own_rows(inverse, tensor_steps)
    grad_own = own_rows(upstream_low, tensor_steps).astype(wide) + inverse_own * (
        combined
        - jnp.mean(combined, axis=-1, keepdims=True)
        - normed_own * jnp.mean(combined * normed_own, axis=-1, keepdims=True)
    )
    grad_residual = spread_rows(grad_own.astype(low), tensor_steps).reshape(residual.shape)

    grad_projections = total_rows(grad_projections.reshape(3 * model, local)).reshape(
        3, model, local
    )
    grad_mixing = total_rows(grad_mixing)
    small_all = sum_small(small_all, tensor_steps)
    small = jnp.concatenate(
        [
            small_all.reshape(-1),
            grad_offsets.reshape(-1),
            grad_thresholds,
            grad_baseline,
        ]
    )
    small = sum_small(small, batch_steps)
    sizes = [2 * model, 2 * model, 3 * local, thresholds.shape[0], model]
    grad_scale, grad_shift, grad_offsets, grad_thresholds, grad_baseline = jnp.split(
        small, np.cumsum(sizes)[:-1]
    )
    return (
        layer_output,
        grad_residual,
        grad_projections,
        grad_offsets.reshape(3, local),
        grad_mixing,
        grad_baseline,
        grad_expand,
        grad_thresholds,
        grad_contract,
        grad_scale.reshape(2, model),
        grad_shift.reshape(2, model),
    )


def solution(mesh):
    in_specs = (
        P("dp", "seq", None),
        P("dp", None),
        P(None, None, "tensor"),
        P(None, "tensor"),
        P("tensor", None),
        P(),
        P(None, "tensor"),
        P("tensor"),
        P("tensor", None),
        P(),
        P(),
        P("dp", "seq", None),
    )
    out_specs = (
        P("dp", "seq", None),
        P("dp", "seq", None),
        P(None, None, "tensor"),
        P(None, "tensor"),
        P("tensor", None),
        P(),
        P(None, "tensor"),
        P("tensor"),
        P("tensor", None),
        P(),
        P(),
    )
    return jax.shard_map(
        on_device, mesh=mesh, in_specs=in_specs, out_specs=out_specs, check_vma=False
    )
```

time: 833 us -> 398 us (0.48)
  waiting for transfers between devices: 509 us -> 160 us
  matrix products: 151 us -> 47.6 us
  starting transfers between devices: 1.29 us -> 64.1 us
  Pallas kernels: 0 us -> 45.1 us
  blocking collectives: 40.6 us -> 0 us
  other arithmetic: 83.9 us -> 45 us
  between operations: 14.8 us -> 2.22 us
    psum x2 -> x0, waiting for transfers between devices: 456 us -> none  [the longest x1 356 us: on_device(): lax.psum((grad_projections, grad_offsets, grad_mixing, grad_baseline, gra...]
    ppermute x0 -> x46, waiting for transfers between devices: none -> 160 us  [the longest x16 87.4 us: spread_rows(): got = lax.ppermute(x, axis, perm)]
    dot_general x18 -> x14, matrix products: 151 us -> 47.6 us  [the longest x5 25 us: dot_nt(): lax.dot_general(a, b, (((1,), (1,)), ((), ())), preferred_element_type=wide)]
    ppermute x0 -> x46, starting transfers between devices: none -> 64.1 us  [the longest x16 20.9 us: spread_rows(): got = lax.ppermute(x, axis, perm)]
    all_gather x2 -> x0, waiting for transfers between devices: 48.5 us -> none  [the longest x1 33.4 us: on_device(): lax.all_gather(key_flat, 'seq', axis=1, tiled=True)]
    pallas_call x0 -> x2, Pallas kernels: none -> 45.1 us  [the longest x1 39.2 us: attention(): pl.pallas_call(functools.partial(attention_kernel, n, per_device), in_spe...]
    psum x1 -> x0, blocking collectives: 40.6 us -> none  [on_device(): lax.psum((grad_projections, grad_offsets, grad_mixing, grad_baseline, gra...]
    reduce_sum x6, other arithmetic: 32.2 us -> 5.42 us  [the longest x1 2.08 us: on_device(): centred = inputs - jnp.mean(inputs, axis=-1, keepdims=True)]
  transfers between devices with their start and end apart: 6 -> 46, of which waited for: 5 -> 18; matrix products, arithmetic and copies ran while one was open for 19% -> 26% of each run, Pallas kernels for 0% -> 10%
where the time goes in v1:
time: 398 us; the launch traced here: 393 us
  waiting for transfers between devices  160 us (40%)
  starting transfers between devices  64.1 us (16%)
  matrix products  47.6 us (12%)
  Pallas kernels  45.1 us (11%)
  other arithmetic  45 us (11%)
  local copies, waits for them, and re-layouts  29.1 us (7%)
    ppermute x16, waiting for transfers between devices, spread_rows(): got = lax.ppermute(x, axis, perm)  87.4 us
    ppermute x16, waiting for transfers between devices, reduce_rows(): got = lax.ppermute(sent, axis, perm)  40.6 us
    pallas_call x1, Pallas kernels, attention(): pl.pallas_call(functools.partial(attention_kernel, n, per_device), in_spe...  39.2 us
    dot_general x5, matrix products, dot_nt(): lax.dot_general(a, b, (((1,), (1,)), ((), ())), preferred_element_type=wide)  25 us
    ppermute x6, waiting for transfers between devices, returned(): piece = lax.ppermute(piece, 'seq', [(s, (s - k) % n) for s in range(n)])  21.3 us
    ppermute x16, starting transfers between devices, spread_rows(): got = lax.ppermute(x, axis, perm)  20.9 us
    ppermute x6, starting transfers between devices, returned(): piece = lax.ppermute(piece, 'seq', [(s, (s - k) % n) for s in range(n)])  19.9 us
    unnamed x82, local copies, waits for them, and re-layouts  13.6 us
  transfers between devices with their start and end apart: 46, of which 18 were waited for; matrix products, arithmetic and copies ran while one was open for 26% of the time, Pallas kernels for 10%

profile of v1, /device:TPU:0, one launch (start us, length us, event | category | flops | bytes accessed | tf_op | source)
XLA Modules:
  0.0 393.0 jit_solution(13907800028926546614)
XLA Ops:
  1.7 1.6 copy-done.2
  10.3 5.9 %shard_map.221 = (bf16[4,4,2,256,128]{4,3,2,1,0:T(8,128)(2,1)S(1)}, bf16[4,256,1024]{2,1,0:T(8,128)(2,1)S(1)}, bf16[4,256,1024]{2,1,0:T(8,128)(2,1)S(1)}) custom-call(s32[4]{0:T(128)S(1)} %reshape.191.places, bf16[4,256,1024]{2,1,0:T(8,128)(2,1)S(1)} %bitcast.137, bf16[4,256,1024]{2,1,0:T(8,128)(2,1)} %bitcast.144, bf16[3,1024,256]{2,1,0:T(8,128)(2,1)S(1)} %copy-done.5, ...), custom_call_target="tpu_custom_call" | custom-call | tf_op jit(solution)/shard_map/pallas_call | solution.py:90
  18.7 3.0 collective-permute-start
  21.7 2.6 collective-permute-start.1
  25.6 4.7 %fusion.52 = f32[1024,1024]{1,0:T(8,128)S(1)} fusion(bf16[1024,1024]{1,0:T(8,128)(2,1)} %bitcast.142, bf16[1024,1024]{1,0:T(8,128)(2,1)} %param.20), kind=kOutput, calls=%fused_computation.160 | convolution fusion | flops 2147483648 | bytes 8388608 | tf_op jit(solution)/shard_map/dot_general | solution.py:22
  30.4 13.5 %convert_reduce_fusion.2 = (f32[1024]{0:T(1024)S(1)}, bf16[1024,1024]{1,0:T(8,128)(2,1)S(1)}, f32[1024,1024]{1,0:T(8,128)}) fusion(f32[1024,1024]{1,0:T(8,128)S(1)} %fusion.52, f32[1024]{0:T(1024)S(1)} %copy-done.35, bf16[1024,1024]{1,0:T(8,128)(2,1)S(1)} %bitcast.146, bf16[1024,1024]{1,0:T(8,128)(2,1)S(1)} %copy-done), kind=kOutput, calls=%fused_computation.7 | convolution fusion | flops 2226125824 | bytes 14688256 | tf_op jit(solution)/shard_map/dot_general | solution.py:26
  45.2 4.4 %fusion.55 = f32[1024,1024]{1,0:T(8,128)} fusion(bf16[1024,1024]{1,0:T(8,128)(2,1)S(1)} %bitcast.143, bf16[1024,1024]{1,0:T(8,128)(2,1)S(1)} %get-tuple-element.42), kind=kOutput, calls=%fused_computation.163 | convolution fusion | flops 2147483648 | bytes 8388608 | tf_op jit(solution)/shard_map/dot_general | solution.py:407
  49.7 2.8 dynamic-slice_convert_fusion.1
  52.4 1.5 collective-permute-start.34
  53.9 4.7 %multiply_convert_fusion = bf16[1024,1024]{1,0:T(8,128)(2,1)S(1)} fusion(f32[1024,1024]{1,0:T(8,128)} %get-tuple-element.43, f32[1024,1024]{1,0:T(8,128)} %copy-done.28, f32[1024]{0:T(1024)S(1)} %copy-done.35), kind=kLoop, calls=%fused_computation.14 | loop fusion | flops 4194304 | bytes 10489856 | tf_op jit(solution)/shard_map/convert_element_type | solution.py:400
  58.7 2.5 fusion.56
  63.5 4.4 %fusion.53 = f32[1024,1024]{1,0:T(8,128)} fusion(bf16[1024,1024]{1,0:T(8,128)(2,1)S(1)} %multiply_convert_fusion, bf16[1024,1024]{1,0:T(8,128)(2,1)S(1)} %copy-done), kind=kOutput, calls=%fused_computation.161 | convolution fusion | flops 2147483648 | bytes 8388608 | tf_op jit(solution)/shard_map/dot_general | solution.py:22
  67.9 2.1 convert_reduce_fusion
  70.1 2.0 convert_reduce_fusion.1
  73.2 4.7 %fusion.54 = f32[1024,1024]{1,0:T(8,128)S(1)} fusion(bf16[1024,1024]{1,0:T(8,128)(2,1)} %copy-done.38, bf16[1024,1024]{1,0:T(8,128)(2,1)} %param.20), kind=kOutput, calls=%fused_computation.162 | convolution fusion | flops 2147483648 | bytes 8388608 | tf_op jit(solution)/shard_map/dot_general | solution.py:26
  78.0 39.2 %shard_map.222 = (bf16[2,256,128]{2,1,0:T(8,128)(2,1)S(1)}, bf16[2,256,128]{2,1,0:T(8,128)(2,1)S(1)}, bf16[2,256,128]{2,1,0:T(8,128)(2,1)S(1)}, bf16[2,256,128]{...) custom-call(s32[8]{0:T(128)S(1)} %select_reduce_fusion.slots, ...), custom_call_target="tpu_custom_call" | custom-call | flops 14495514624 | bytes 8388608 | tf_op jit(solution)/shard_map/pallas_call | solution.py:265
  117.7 1.7 collective-permute-start.4
  120.1 2.9 collective-permute-done.3
  123.1 2.8 collective-permute-start.10
  125.9 6.2 %collective-permute-done.4 = bf16[2,256,128]{2,1,0:T(8,128)(2,1)S(1)} collective-permute-done((bf16[2,256,128]{2,1,0:T(8,128)(2,1)S(1)}, bf16[2,256,128]{2,1,0:T(8,128)(2,1)S(1)}, u32[]{:S(2)}, u32[]{:S(2)}) %collective-permute-start.4) | collective-permute-done | bytes 131104 | tf_op jit(solution)/shard_map/ppermute | solution.py:430
  132.1 14.7 %collective-permute-start.12 = (bf16[3,2,256,128]{3,2,1,0:T(8,128)(2,1)S(1)}, bf16[3,2,256,128]{3,2,1,0:T(8,128)(2,1)S(1)}, u32[]{:S(2)}, u32[]{:S(2)}) collective-permute-start(bf16[3,2,256,128]{3,2,1,0:T(8,128)(2,1)S(1)} %get-tuple-element.31), channel_id=1, source_target_pairs={{0,4},{4,8},{8,12},{12,0},{1,5},{5,9},{9,13},{13,1},{2,6},{6,10},{... | collective-permute-start | bytes 1179656 | tf_op jit(solution)/shard_map/ppermute | solution.py:430
  149.8 1.6 dynamic-slice_convert_fusion.3
  151.5 12.2 %collective-permute-done.11 = bf16[3,2,256,128]{3,2,1,0:T(8,128)(2,1)S(1)} collective-permute-done((bf16[3,2,256,128]{3,2,1,0:T(8,128)(2,1)S(1)}, bf16[3,2,256,128]{3,2,1,0:T(8,128)(2,1)S(1)}, u32[]{:S(2)}, u32[]{:S(2)}) %collective-permute-start.11) | collective-permute-done | bytes 393248 | tf_op jit(solution)/shard_map/ppermute | solution.py:430
  168.2 1.7 convolution_bitcast_fusion.1
  169.9 1.7 convolution_bitcast_fusion
  171.6 5.3 %multiply_reduce_fusion.1 = (f32[1024]{0:T(1024)S(1)}, f32[1024]{0:T(1024)S(1)}, f32[1024]{0:T(1024)S(1)}, f32[1024]{0:T(1024)S(1)}, f32[1024,1024]{1,0:T(8,128)}, /*index=5*/f32[1024,1024]{1,0:T(8,128)}) fusion(f32[1024]{0:T(1024)S(1)} %bitcast.179, f32[1024]{0:T(1024)S(1)} %bitcast.180, bf16[2,512,1024]{2,1,0:T(8,128)(2,1)S(1)} %copy-done.4, ...), kind=kOutput, calls=%fused_computation.9 | convolution fusion | flops 551546880 | bytes 24150016 | tf_op jit(solution)/shard_map/dot_general | solution.py:26
  177.0 1.7 convolution_bitcast_fusion.2
  179.1 1.6 collective-permute-start.24
  180.8 2.1 collective-permute-done.24
  184.3 2.1 pad_maximum_fusion
  187.1 3.8 collective-permute-done.26
  191.4 4.2 %collective-permute-done.27 = f32[6912]{0:T(1024)S(1)} collective-permute-done((f32[6912]{0:T(1024)S(1)}, f32[6912]{0:T(1024)S(1)}, u32[]{:S(2)}, u32[]{:S(2)}) %collective-permute-start.27) | collective-permute-done | bytes 27680 | tf_op jit(solution)/shard_map/ppermute | solution.py:335
  196.3 2.0 convert_add_fusion.1
  199.8 1.7 convert_add_fusion
  202.3 2.2 collective-permute-start.31
  204.5 19.5 %collective-permute-done.31 = bf16[32,1024]{1,0:T(8,128)(2,1)S(1)} collective-permute-done((bf16[32,1024]{1,0:T(8,128)(2,1)S(1)}, bf16[32,1024]{1,0:T(8,128)(2,1)S(1)}, u32[]{:S(2)}, u32[]{:S(2)}) %collective-permute-start.31) | collective-permute-done | bytes 65568 | tf_op jit(solution)/shard_map/ppermute | solution.py:318
  224.8 3.9 collective-permute-start.32
  229.2 3.0 collective-permute-start.42
  232.1 1.7 convert_add_fusion.3
  233.9 8.9 %collective-permute-done.17 = bf16[1536,256]{1,0:T(8,128)(2,1)S(1)} collective-permute-done((bf16[1536,256]{1,0:T(8,128)(2,1)S(1)}, bf16[1536,256]{1,0:T(8,128)(2,1)S(1)}, u32[]{:S(2)}, u32[]{:S(2)}) %collective-permute-start.17) | collective-permute-done | bytes 786464 | tf_op jit(solution)/shard_map/ppermute | solution.py:311
  242.8 1.5 collective-permute-start.7
  244.5 4.2 %collective-permute-done.36 = bf16[128,1024]{1,0:T(8,128)(2,1)S(1)} collective-permute-done((bf16[128,1024]{1,0:T(8,128)(2,1)S(1)}, bf16[128,1024]{1,0:T(8,128)(2,1)S(1)}, u32[]{:S(2)}, u32[]{:S(2)}) %collective-permute-start.36) | collective-permute-done | bytes 262176 | tf_op jit(solution)/shard_map/ppermute | solution.py:311
  248.8 4.5 %collective-permute-done.42 = bf16[128,1024]{1,0:T(8,128)(2,1)S(1)} collective-permute-done((bf16[128,1024]{1,0:T(8,128)(2,1)S(1)}, bf16[128,1024]{1,0:T(8,128)(2,1)S(1)}, u32[]{:S(2)}, u32[]{:S(2)}) %collective-permute-start.42) | collective-permute-done | bytes 262176 | tf_op jit(solution)/shard_map/ppermute | solution.py:311
  253.3 3.0 collective-permute-start.43
  256.9 15.9 %collective-permute-done.37 = bf16[128,1024]{1,0:T(8,128)(2,1)S(1)} collective-permute-done((bf16[128,1024]{1,0:T(8,128)(2,1)S(1)}, bf16[128,1024]{1,0:T(8,128)(2,1)S(1)}, u32[]{:S(2)}, u32[]{:S(2)}) %collective-permute-start.37) | collective-permute-done | bytes 262176 | tf_op jit(solution)/shard_map/ppermute | solution.py:318
  272.8 1.5 collective-permute-start.14
  274.5 2.9 collective-permute-done.43
  277.5 2.1 collective-permute-start.44
  280.5 23.0 %collective-permute-done.19 = bf16[384,256]{1,0:T(8,128)(2,1)S(1)} collective-permute-done((bf16[384,256]{1,0:T(8,128)(2,1)S(1)}, bf16[384,256]{1,0:T(8,128)(2,1)S(1)}, u32[]{:S(2)}, u32[]{:S(2)}) %collective-permute-start.19) | collective-permute-done | bytes 196640 | tf_op jit(solution)/shard_map/ppermute | solution.py:311
  303.4 1.5 collective-permute-start.8
  305.0 3.4 collective-permute-start.20
  308.8 1.6 add_convert_fusion.1
  310.4 5.4 %collective-permute-done.20 = bf16[384,256]{1,0:T(8,128)(2,1)S(1)} collective-permute-done((bf16[384,256]{1,0:T(8,128)(2,1)S(1)}, bf16[384,256]{1,0:T(8,128)(2,1)S(1)}, u32[]{:S(2)}, u32[]{:S(2)}) %collective-permute-start.20) | collective-permute-done | bytes 196640 | tf_op jit(solution)/shard_map/ppermute | solution.py:318
  317.1 1.6 collective-permute-start.39
  326.3 1.5 collective-permute-start.33
  329.8 1.6 maximum_select_fusion.5
  331.5 1.6 maximum_select_fusion.6
  333.1 38.2 %collective-permute-done.33 = bf16[128,1024]{1,0:T(8,128)(2,1)S(1)} collective-permute-done((bf16[128,1024]{1,0:T(8,128)(2,1)S(1)}, bf16[128,1024]{1,0:T(8,128)(2,1)S(1)}, u32[]{:S(2)}, u32[]{:S(2)}) %collective-permute-start.33) | collective-permute-done | bytes 262176 | tf_op jit(solution)/shard_map/ppermute | solution.py:318
  372.4 4.5 %fusion.8 = f32[1024,1024]{1,0:T(8,128)} fusion(bf16[512,1024]{1,0:T(8,128)(2,1)} %collective-permute-done.39, bf16[512,1024]{1,0:T(8,128)(2,1)S(1)} %maximum_select_fusion.7, pred[]{:T(512)S(6)} %eq.102), kind=kLoop, calls=%fused_computation.34 | loop fusion | flops 10485760 | bytes 6291457 | tf_op jit(solution)/shard_map/convert_element_type | solution.py:418
  376.9 4.5 %fusion.9 = f32[1024,1024]{1,0:T(8,128)} fusion(bf16[512,1024]{1,0:T(8,128)(2,1)} %collective-permute-done.45, bf16[512,1024]{1,0:T(8,128)(2,1)S(1)} %maximum_select_fusion.8, pred[]{:T(512)S(6)} %eq.102), kind=kLoop, calls=%fused_computation.36 | loop fusion | flops 10485760 | bytes 6291457 | tf_op jit(solution)/shard_map/convert_element_type | solution.py:418
  381.5 4.3 %collective-permute-done.22 = bf16[1536,256]{1,0:T(8,128)(2,1)S(1)} collective-permute-done((bf16[1536,256]{1,0:T(8,128)(2,1)S(1)}, bf16[1536,256]{1,0:T(8,128)(2,1)S(1)}, u32[]{:S(2)}, u32[]{:S(2)}) %collective-permute-start.22) | collective-permute-done | bytes 786464 | tf_op jit(solution)/shard_map/ppermute | solution.py:318
  386.2 1.9 convert.1
  388.1 2.3 maximum_select_fusion
  390.5 2.3 maximum_select_fusion.1
  (223 shorter events, 47.3 us)
Async XLA Ops:
  0.6 29.7 %copy-start = (bf16[1024,1024]{1,0:T(8,128)(2,1)S(1)}, bf16[1024,1024]{1,0:T(8,128)(2,1)}, u32[]{:S(2)}) copy-start(bf16[1024,1024]{1,0:T(8,128)(2,1)} %param.22) | copy-start | bytes 6291460
  18.7 59.3 %collective-permute-start = (bf16[4,2,256,128]{3,2,1,0:T(8,128)(2,1)}, bf16[4,2,256,128]{3,2,1,0:T(8,128)(2,1)S(1)}, u32[]{:S(2)}, u32[]{:S(2)}) collective-permute-start(bf16[4,2,256,128]{3,2,1,0:T(8,128)(2,1)} %get-tuple-element.48), channel_id=1, source_target_pairs={{0,4},{4,8},{8,12},{12,0},{1,5},{5,9},{9,13},{13,1},{2,6},{6,10},{... | collective-permute-start | bytes 1572872 | tf_op jit(solution)/shard_map/ppermute | solution.py:387
  21.7 56.3 %collective-permute-start.1 = (bf16[4,2,256,128]{3,2,1,0:T(8,128)(2,1)}, bf16[4,2,256,128]{3,2,1,0:T(8,128)(2,1)}, u32[]{:S(2)}, u32[]{:S(2)}) collective-permute-start(bf16[4,2,256,128]{3,2,1,0:T(8,128)(2,1)} %get-tuple-element.47), channel_id=1, source_target_pairs={{0,8},{4,12},{8,0},{12,4},{1,9},{5,13},{9,1},{13,5},{2,10},{6,14},... | collective-permute-start | bytes 1572872 | tf_op jit(solution)/shard_map/ppermute | solution.py:387
  24.3 53.7 %collective-permute-start.2 = (bf16[4,2,256,128]{3,2,1,0:T(8,128)(2,1)}, bf16[4,2,256,128]{3,2,1,0:T(8,128)(2,1)}, u32[]{:S(2)}, u32[]{:S(2)}) collective-permute-start(bf16[4,2,256,128]{3,2,1,0:T(8,128)(2,1)} %get-tuple-element.46), channel_id=1, source_target_pairs={{0,12},{4,0},{8,4},{12,8},{1,13},{5,1},{9,5},{13,9},{2,14},{6,2},{... | collective-permute-start | bytes 1572872 | tf_op jit(solution)/shard_map/ppermute | solution.py:387
  25.6 4.7 %copy-start.21 = (bf16[2,512,1024]{2,1,0:T(8,128)(2,1)S(1)}, bf16[2,512,1024]{2,1,0:T(8,128)(2,1)}, u32[]{:S(2)}) copy-start(bf16[2,512,1024]{2,1,0:T(8,128)(2,1)} %param.25) | copy-start | bytes 6291460
  25.6 4.7 %copy-start.35 = (f32[1024]{0:T(1024)S(1)}, f32[1024]{0:T(1024)}, u32[]{:S(2)}) copy-start(f32[1024]{0:T(1024)} %param.21) | copy-start | bytes 12292
  30.3 13.6 %copy-start.28 = (f32[1024,1024]{1,0:T(8,128)}, f32[1024,1024]{1,0:T(8,128)S(1)}, u32[]{:S(2)}) copy-start(f32[1024,1024]{1,0:T(8,128)S(1)} %fusion.52) | copy-start | bytes 12582916
  30.4 14.9 %copy-start.20 = (bf16[4,256,1024]{2,1,0:T(8,128)(2,1)S(1)}, bf16[4,256,1024]{2,1,0:T(8,128)(2,1)}, u32[]{:S(2)}) copy-start(bf16[4,256,1024]{2,1,0:T(8,128)(2,1)} %copy-done.19) | copy-start | bytes 6291460
  52.4 143.8 %collective-permute-start.34 = (bf16[512,1024]{1,0:T(8,128)(2,1)}, bf16[512,1024]{1,0:T(8,128)(2,1)}, u32[]{:S(2)}, u32[]{:S(2)}) collective-permute-start(bf16[512,1024]{1,0:T(8,128)(2,1)} %dynamic-slice_convert_fusion.1), channel_id=1, source_target_pairs={{0,16},{16,0},{1,17},{17,1},{2,18},{18,2},{3,19},{19,3},{4,20},{20... | collective-permute-start | bytes 3145736 | tf_op jit(solution)/shard_map/ppermute | solution.py:311
  53.9 4.7 %copy-start.22 = (bf16[2,512,1024]{2,1,0:T(8,128)(2,1)S(1)}, bf16[2,512,1024]{2,1,0:T(8,128)(2,1)}, u32[]{:S(2)}) copy-start(bf16[2,512,1024]{2,1,0:T(8,128)(2,1)} %param.25) | copy-start | bytes 6291460
  62.5 7.5 %copy-start.14 = (f32[2,1024]{1,0:T(2,128)S(1)}, f32[2,1024]{1,0:T(2,128)}, u32[]{:S(2)}) copy-start(f32[2,1024]{1,0:T(2,128)} %scale.1) | copy-start | bytes 24580
  62.5 137.3 %collective-permute-start.40 = (bf16[512,1024]{1,0:T(8,128)(2,1)}, bf16[512,1024]{1,0:T(8,128)(2,1)}, u32[]{:S(2)}, u32[]{:S(2)}) collective-permute-start(bf16[512,1024]{1,0:T(8,128)(2,1)} %dynamic-slice_convert_fusion), channel_id=1, source_target_pairs={{0,16},{16,0},{1,17},{17,1},{2,18},{18,2},{3,19},{19,3},{4,20},{20... | collective-permute-start | bytes 3145736 | tf_op jit(solution)/shard_map/ppermute | solution.py:311
  73.2 4.8 %copy-start.10 = (f32[2048,128]{1,0:T(8,128)S(1)}, f32[2048,128]{1,0:T(8,128)}, u32[]{:S(2)}) copy-start(f32[2048,128]{1,0:T(8,128)} %constant.460.clone.cosine.refs_4_) | copy-start | bytes 3145732
  73.2 4.8 %copy-start.12 = (f32[2048,128]{1,0:T(8,128)S(1)}, f32[2048,128]{1,0:T(8,128)}, u32[]{:S(2)}) copy-start(f32[2048,128]{1,0:T(8,128)} %constant.461.clone.sine.refs_5_) | copy-start | bytes 3145732
  117.2 30.2 %copy-start.8 = (bf16[256,1024]{1,0:T(8,128)(2,1)S(1)}, bf16[256,1024]{1,0:T(8,128)(2,1)}, u32[]{:S(2)}) copy-start(bf16[256,1024]{1,0:T(8,128)(2,1)} %mix.1) | copy-start | bytes 1572868
  117.2 30.2 %copy-start.29 = (f32[1024,1024]{1,0:T(8,128)S(1)}, f32[1024,1024]{1,0:T(8,128)}, u32[]{:S(2)}) copy-start(f32[1024,1024]{1,0:T(8,128)} %fusion.53) | copy-start | bytes 12582916
  117.2 5.9 %collective-permute-start.3 = (bf16[2,256,128]{2,1,0:T(8,128)(2,1)S(1)}, bf16[2,256,128]{2,1,0:T(8,128)(2,1)S(1)}, u32[]{:S(2)}, u32[]{:S(2)}) collective-permute-start(bf16[2,256,128]{2,1,0:T(8,128)(2,1)S(1)} %get-tuple-element.24), channel_id=1, source_target_pairs={{0,12},{4,0},{8,4},{12,8},{1,13},{5,1},{9,5},{13,9},{2,14},{6,2},{... | collective-permute-start | bytes 393224 | tf_op jit(solution)/shard_map/ppermute | solution.py:430
  117.7 14.4 %collective-permute-start.4 = (bf16[2,256,128]{2,1,0:T(8,128)(2,1)S(1)}, bf16[2,256,128]{2,1,0:T(8,128)(2,1)S(1)}, u32[]{:S(2)}, u32[]{:S(2)}) collective-permute-start(bf16[2,256,128]{2,1,0:T(8,128)(2,1)S(1)} %get-tuple-element.25), channel_id=1, source_target_pairs={{0,8},{4,12},{8,0},{12,4},{1,9},{5,13},{9,1},{13,5},{2,10},{6,14},... | collective-permute-start | bytes 393224 | tf_op jit(solution)/shard_map/ppermute | solution.py:430
  119.4 12.7 %collective-permute-start.5 = (bf16[2,256,128]{2,1,0:T(8,128)(2,1)S(1)}, bf16[2,256,128]{2,1,0:T(8,128)(2,1)S(1)}, u32[]{:S(2)}, u32[]{:S(2)}) collective-permute-start(bf16[2,256,128]{2,1,0:T(8,128)(2,1)S(1)} %get-tuple-element.26), channel_id=1, source_target_pairs={{0,4},{4,8},{8,12},{12,0},{1,5},{5,9},{9,13},{13,1},{2,6},{6,10},{... | collective-permute-start | bytes 393224 | tf_op jit(solution)/shard_map/ppermute | solution.py:430
  123.1 28.3 %collective-permute-start.10 = (bf16[3,2,256,128]{3,2,1,0:T(8,128)(2,1)S(1)}, bf16[3,2,256,128]{3,2,1,0:T(8,128)(2,1)S(1)}, u32[]{:S(2)}, u32[]{:S(2)}) collective-permute-start(bf16[3,2,256,128]{3,2,1,0:T(8,128)(2,1)S(1)} %get-tuple-element.29), channel_id=1, source_target_pairs={{0,12},{4,0},{8,4},{12,8},{1,13},{5,1},{9,5},{13,9},{2,14},{6,2},{... | collective-permute-start | bytes 1179656 | tf_op jit(solution)/shard_map/ppermute | solution.py:430
  132.1 31.5 %collective-permute-start.11 = (bf16[3,2,256,128]{3,2,1,0:T(8,128)(2,1)S(1)}, bf16[3,2,256,128]{3,2,1,0:T(8,128)(2,1)S(1)}, u32[]{:S(2)}, u32[]{:S(2)}) collective-permute-start(bf16[3,2,256,128]{3,2,1,0:T(8,128)(2,1)S(1)} %get-tuple-element.30), channel_id=1, source_target_pairs={{0,8},{4,12},{8,0},{12,4},{1,9},{5,13},{9,1},{13,5},{2,10},{6,14},... | collective-permute-start | bytes 1179656 | tf_op jit(solution)/shard_map/ppermute | solution.py:430
  132.1 32.3 %collective-permute-start.12 = (bf16[3,2,256,128]{3,2,1,0:T(8,128)(2,1)S(1)}, bf16[3,2,256,128]{3,2,1,0:T(8,128)(2,1)S(1)}, u32[]{:S(2)}, u32[]{:S(2)}) collective-permute-start(bf16[3,2,256,128]{3,2,1,0:T(8,128)(2,1)S(1)} %get-tuple-element.31), channel_id=1, source_target_pairs={{0,4},{4,8},{8,12},{12,0},{1,5},{5,9},{9,13},{13,1},{2,6},{6,10},{... | collective-permute-start | bytes 1179656 | tf_op jit(solution)/shard_map/ppermute | solution.py:430
  151.4 77.8 %collective-permute-start.6 = (bf16[512,1024]{1,0:T(8,128)(2,1)}, bf16[512,1024]{1,0:T(8,128)(2,1)}, u32[]{:S(2)}, u32[]{:S(2)}) collective-permute-start(bf16[512,1024]{1,0:T(8,128)(2,1)} %dynamic-slice_convert_fusion.3), channel_id=1, source_target_pairs={{0,1},{1,0},{2,3},{3,2},{4,5},{5,4},{6,7},{7,6},{8,9},{9,8},{10,11... | collective-permute-start | bytes 3145736 | tf_op jit(solution)/shard_map/ppermute | solution.py:311
  163.6 15.1 %collective-permute-start.28 = (bf16[128,1024]{1,0:T(8,128)(2,1)S(1)}, bf16[128,1024]{1,0:T(8,128)(2,1)S(1)}, u32[]{:S(2)}, u32[]{:S(2)}) collective-permute-start(bf16[128,1024]{1,0:T(8,128)(2,1)S(1)} %dynamic-slice_convert_fusion.12), channel_id=1, source_target_pairs={{0,16},{16,0},{1,17},{17,1},{2,18},{18,2},{3,19},{19,3},{4,20},{20... | collective-permute-start | bytes 786440 | tf_op jit(solution)/shard_map/ppermute | solution.py:311
  176.9 2.1 collective-permute-start.23
  179.1 3.8 collective-permute-start.24
  180.7 14.9 %collective-permute-start.29 = (bf16[64,1024]{1,0:T(8,128)(2,1)S(1)}, bf16[64,1024]{1,0:T(8,128)(2,1)S(1)}, u32[]{:S(2)}, u32[]{:S(2)}) collective-permute-start(bf16[64,1024]{1,0:T(8,128)(2,1)S(1)} %dynamic-slice_convert_fusion.14), channel_id=1, source_target_pairs={{0,4},{4,0},{8,12},{12,8},{1,5},{5,1},{9,13},{13,9},{2,6},{6,2},{1... | collective-permute-start | bytes 393224 | tf_op jit(solution)/shard_map/ppermute | solution.py:311
  182.9 8.3 %copy-start.26 = (f32[1024,1024]{1,0:T(8,128)S(1)}, f32[1024,1024]{1,0:T(8,128)}, u32[]{:S(2)}) copy-start(f32[1024,1024]{1,0:T(8,128)} %get-tuple-element.44) | copy-start | bytes 12582916
  182.9 3.9 %collective-permute-start.25 = (f32[6912]{0:T(1024)S(1)}, f32[6912]{0:T(1024)S(1)}, u32[]{:S(2)}, u32[]{:S(2)}) collective-permute-start(f32[6912]{0:T(1024)S(1)} %pad_maximum_fusion.1), channel_id=1, source_target_pairs={{0,16},{16,0},{1,17},{17,1},{2,18},{18,2},{3,19},{19,3},{4,20},{20... | collective-permute-start | bytes 82952 | tf_op jit(solution)/shard_map/ppermute | solution.py:335
  186.4 9.9 %copy-start.30 = (f32[1024,1024]{1,0:T(8,128)S(1)}, f32[1024,1024]{1,0:T(8,128)}, u32[]{:S(2)}) copy-start(f32[1024,1024]{1,0:T(8,128)} %fusion.55) | copy-start | bytes 12582916
  186.9 3.9 %collective-permute-start.26 = (f32[6912]{0:T(1024)S(1)}, f32[6912]{0:T(1024)S(1)}, u32[]{:S(2)}, u32[]{:S(2)}) collective-permute-start(f32[6912]{0:T(1024)S(1)} %fusion.45), channel_id=1, source_target_pairs={{0,4},{4,0},{8,12},{12,8},{1,5},{5,1},{9,13},{13,9},{2,6},{6,2},{1... | collective-permute-start | bytes 82952 | tf_op jit(solution)/shard_map/ppermute | solution.py:335
  190.8 4.8 %collective-permute-start.27 = (f32[6912]{0:T(1024)S(1)}, f32[6912]{0:T(1024)S(1)}, u32[]{:S(2)}, u32[]{:S(2)}) collective-permute-start(f32[6912]{0:T(1024)S(1)} %add.412), channel_id=1, source_target_pairs={{0,8},{4,12},{8,0},{12,4},{1,9},{5,13},{9,1},{13,5},{2,10},{6,14},... | collective-permute-start | bytes 82952 | tf_op jit(solution)/shard_map/ppermute | solution.py:335
  195.6 57.7 %collective-permute-start.13 = (bf16[512,1024]{1,0:T(8,128)(2,1)S(1)}, bf16[512,1024]{1,0:T(8,128)(2,1)S(1)}, u32[]{:S(2)}, u32[]{:S(2)}) collective-permute-start(bf16[512,1024]{1,0:T(8,128)(2,1)S(1)} %dynamic-slice_convert_fusion.2), channel_id=1, source_target_pairs={{0,1},{1,0},{2,3},{3,2},{4,5},{5,4},{6,7},{7,6},{8,9},{9,8},{10,11... | collective-permute-start | bytes 3145736 | tf_op jit(solution)/shard_map/ppermute | solution.py:311
  195.7 6.6 %collective-permute-start.30 = (bf16[32,1024]{1,0:T(8,128)(2,1)S(1)}, bf16[32,1024]{1,0:T(8,128)(2,1)S(1)}, u32[]{:S(2)}, u32[]{:S(2)}) collective-permute-start(bf16[32,1024]{1,0:T(8,128)(2,1)S(1)} %dynamic-slice_convert_fusion.15), channel_id=1, source_target_pairs={{0,8},{4,12},{8,0},{12,4},{1,9},{5,13},{9,1},{13,5},{2,10},{6,14},... | collective-permute-start | bytes 196616 | tf_op jit(solution)/shard_map/ppermute | solution.py:311
  198.3 26.4 %collective-permute-start.35 = (bf16[256,1024]{1,0:T(8,128)(2,1)S(1)}, bf16[256,1024]{1,0:T(8,128)(2,1)S(1)}, u32[]{:S(2)}, u32[]{:S(2)}) collective-permute-start(bf16[256,1024]{1,0:T(8,128)(2,1)S(1)} %dynamic-slice_convert_fusion.6), channel_id=1, source_target_pairs={{0,4},{4,0},{8,12},{12,8},{1,5},{5,1},{9,13},{13,9},{2,6},{6,2},{1... | collective-permute-start | bytes 1572872 | tf_op jit(solution)/shard_map/ppermute | solution.py:311
  201.5 27.3 %collective-permute-start.41 = (bf16[256,1024]{1,0:T(8,128)(2,1)S(1)}, bf16[256,1024]{1,0:T(8,128)(2,1)S(1)}, u32[]{:S(2)}, u32[]{:S(2)}) collective-permute-start(bf16[256,1024]{1,0:T(8,128)(2,1)S(1)} %dynamic-slice_convert_fusion.5), channel_id=1, source_target_pairs={{0,4},{4,0},{8,12},{12,8},{1,5},{5,1},{9,13},{13,9},{2,6},{6,2},{1... | collective-permute-start | bytes 1572872 | tf_op jit(solution)/shard_map/ppermute | solution.py:311
  202.3 21.7 %collective-permute-start.31 = (bf16[32,1024]{1,0:T(8,128)(2,1)S(1)}, bf16[32,1024]{1,0:T(8,128)(2,1)S(1)}, u32[]{:S(2)}, u32[]{:S(2)}) collective-permute-start(bf16[32,1024]{1,0:T(8,128)(2,1)S(1)} %add_convert_fusion.6), channel_id=1, source_target_pairs={{0,8},{4,12},{8,0},{12,4},{1,9},{5,13},{9,1},{13,5},{2,10},{6,14},... | collective-permute-start | bytes 196616 | tf_op jit(solution)/shard_map/ppermute | solution.py:318
  224.0 18.8 %collective-permute-start.17 = (bf16[1536,256]{1,0:T(8,128)(2,1)S(1)}, bf16[1536,256]{1,0:T(8,128)(2,1)S(1)}, u32[]{:S(2)}, u32[]{:S(2)}) collective-permute-start(bf16[1536,256]{1,0:T(8,128)(2,1)S(1)} %dynamic-slice_convert_fusion.4), channel_id=1, source_target_pairs={{0,16},{16,0},{1,17},{17,1},{2,18},{18,2},{3,19},{19,3},{4,20},{20... | collective-permute-start | bytes 2359304 | tf_op jit(solution)/shard_map/ppermute | solution.py:311
  224.7 4.4 %copy-start.33 = (bf16[64,1024]{1,0:T(8,128)(2,1)}, bf16[64,1024]{1,0:T(8,128)(2,1)S(1)}, u32[]{:S(2)}) copy-start(bf16[64,1024]{1,0:T(8,128)(2,1)S(1)} %maximum_select_fusion.15) | copy-start | bytes 393220
  224.8 7.4 %copy-start.25 = (f32[1024,1024]{1,0:T(8,128)S(1)}, f32[1024,1024]{1,0:T(8,128)}, u32[]{:S(2)}) copy-start(f32[1024,1024]{1,0:T(8,128)} %copy-done.24) | copy-start | bytes 12582916
  224.8 94.4 %collective-permute-start.32 = (bf16[64,1024]{1,0:T(8,128)(2,1)S(1)}, bf16[64,1024]{1,0:T(8,128)(2,1)S(1)}, u32[]{:S(2)}, u32[]{:S(2)}) collective-permute-start(bf16[64,1024]{1,0:T(8,128)(2,1)S(1)} %maximum_select_fusion.15), channel_id=1, source_target_pairs={{0,4},{4,0},{8,12},{12,8},{1,5},{5,1},{9,13},{13,9},{2,6},{6,2},{1... | collective-permute-start | bytes 393224 | tf_op jit(solution)/shard_map/ppermute | solution.py:318
  228.8 19.9 %collective-permute-start.36 = (bf16[128,1024]{1,0:T(8,128)(2,1)S(1)}, bf16[128,1024]{1,0:T(8,128)(2,1)S(1)}, u32[]{:S(2)}, u32[]{:S(2)}) collective-permute-start(bf16[128,1024]{1,0:T(8,128)(2,1)S(1)} %dynamic-slice_convert_fusion.11), channel_id=1, source_target_pairs={{0,8},{4,12},{8,0},{12,4},{1,9},{5,13},{9,1},{13,5},{2,10},{6,14},... | collective-permute-start | bytes 786440 | tf_op jit(solution)/shard_map/ppermute | solution.py:311
  229.2 24.1 %collective-permute-start.42 = (bf16[128,1024]{1,0:T(8,128)(2,1)S(1)}, bf16[128,1024]{1,0:T(8,128)(2,1)S(1)}, u32[]{:S(2)}, u32[]{:S(2)}) collective-permute-start(bf16[128,1024]{1,0:T(8,128)(2,1)S(1)} %dynamic-slice_convert_fusion.10), channel_id=1, source_target_pairs={{0,8},{4,12},{8,0},{12,4},{1,9},{5,13},{9,1},{13,5},{2,10},{6,14},... | collective-permute-start | bytes 786440 | tf_op jit(solution)/shard_map/ppermute | solution.py:311
  242.8 36.9 %collective-permute-start.7 = (bf16[256,1024]{1,0:T(8,128)(2,1)S(1)}, bf16[256,1024]{1,0:T(8,128)(2,1)S(1)}, u32[]{:S(2)}, u32[]{:S(2)}) collective-permute-start(bf16[256,1024]{1,0:T(8,128)(2,1)S(1)} %dynamic-slice_convert_fusion.8), channel_id=1, source_target_pairs={{0,2},{1,3},{2,0},{3,1},{4,6},{5,7},{6,4},{7,5},{8,10},{9,11},{10,... | collective-permute-start | bytes 1572872 | tf_op jit(solution)/shard_map/ppermute | solution.py:311
  248.7 28.8 %collective-permute-start.18 = (bf16[768,256]{1,0:T(8,128)(2,1)S(1)}, bf16[768,256]{1,0:T(8,128)(2,1)S(1)}, u32[]{:S(2)}, u32[]{:S(2)}) collective-permute-start(bf16[768,256]{1,0:T(8,128)(2,1)S(1)} %dynamic-slice_convert_fusion.9), channel_id=1, source_target_pairs={{0,4},{4,0},{8,12},{12,8},{1,5},{5,1},{9,13},{13,9},{2,6},{6,2},{1... | collective-permute-start | bytes 1179656 | tf_op jit(solution)/shard_map/ppermute | solution.py:311
  253.2 19.6 %collective-permute-start.37 = (bf16[128,1024]{1,0:T(8,128)(2,1)S(1)}, bf16[128,1024]{1,0:T(8,128)(2,1)S(1)}, u32[]{:S(2)}, u32[]{:S(2)}) collective-permute-start(bf16[128,1024]{1,0:T(8,128)(2,1)S(1)} %add_convert_fusion.4), channel_id=1, source_target_pairs={{0,8},{4,12},{8,0},{12,4},{1,9},{5,13},{9,1},{13,5},{2,10},{6,14},... | collective-permute-start | bytes 786440 | tf_op jit(solution)/shard_map/ppermute | solution.py:318
  253.3 24.0 %collective-permute-start.43 = (bf16[128,1024]{1,0:T(8,128)(2,1)S(1)}, bf16[128,1024]{1,0:T(8,128)(2,1)S(1)}, u32[]{:S(2)}, u32[]{:S(2)}) collective-permute-start(bf16[128,1024]{1,0:T(8,128)(2,1)S(1)} %add_convert_fusion.3), channel_id=1, source_target_pairs={{0,8},{4,12},{8,0},{12,4},{1,9},{5,13},{9,1},{13,5},{2,10},{6,14},... | collective-permute-start | bytes 786440 | tf_op jit(solution)/shard_map/ppermute | solution.py:318
  256.8 23.4 %copy-start.36 = (f32[1024]{0:T(1024)S(1)}, f32[1024]{0:T(1024)}, u32[]{:S(2)}) copy-start(f32[1024]{0:T(1024)} %param.19) | copy-start | bytes 12292
  272.8 32.1 %collective-permute-start.14 = (bf16[256,1024]{1,0:T(8,128)(2,1)S(1)}, bf16[256,1024]{1,0:T(8,128)(2,1)S(1)}, u32[]{:S(2)}, u32[]{:S(2)}) collective-permute-start(bf16[256,1024]{1,0:T(8,128)(2,1)S(1)} %dynamic-slice_convert_fusion.7), channel_id=1, source_target_pairs={{0,2},{1,3},{2,0},{3,1},{4,6},{5,7},{6,4},{7,5},{8,10},{9,11},{10,... | collective-permute-start | bytes 1572872 | tf_op jit(solution)/shard_map/ppermute | solution.py:311
  277.3 39.2 %collective-permute-start.38 = (bf16[256,1024]{1,0:T(8,128)(2,1)S(1)}, bf16[256,1024]{1,0:T(8,128)(2,1)S(1)}, u32[]{:S(2)}, u32[]{:S(2)}) collective-permute-start(bf16[256,1024]{1,0:T(8,128)(2,1)S(1)} %maximum_select_fusion.11), channel_id=1, source_target_pairs={{0,4},{4,0},{8,12},{12,8},{1,5},{5,1},{9,13},{13,9},{2,6},{6,2},{1... | collective-permute-start | bytes 1572872 | tf_op jit(solution)/shard_map/ppermute | solution.py:318
  277.5 30.9 %copy-start.27 = (f32[1024,1024]{1,0:T(8,128)S(1)}, f32[1024,1024]{1,0:T(8,128)}, u32[]{:S(2)}) copy-start(f32[1024,1024]{1,0:T(8,128)} %get-tuple-element.45) | copy-start | bytes 12582916
  277.5 39.6 %collective-permute-start.44 = (bf16[256,1024]{1,0:T(8,128)(2,1)S(1)}, bf16[256,1024]{1,0:T(8,128)(2,1)S(1)}, u32[]{:S(2)}, u32[]{:S(2)}) collective-permute-start(bf16[256,1024]{1,0:T(8,128)(2,1)S(1)} %maximum_select_fusion.12), channel_id=1, source_target_pairs={{0,4},{4,0},{8,12},{12,8},{1,5},{5,1},{9,13},{13,9},{2,6},{6,2},{1... | collective-permute-start | bytes 1572872 | tf_op jit(solution)/shard_map/ppermute | solution.py:318
  279.7 23.7 %collective-permute-start.19 = (bf16[384,256]{1,0:T(8,128)(2,1)S(1)}, bf16[384,256]{1,0:T(8,128)(2,1)S(1)}, u32[]{:S(2)}, u32[]{:S(2)}) collective-permute-start(bf16[384,256]{1,0:T(8,128)(2,1)S(1)} %dynamic-slice_convert_fusion.13), channel_id=1, source_target_pairs={{0,8},{4,12},{8,0},{12,4},{1,9},{5,13},{9,1},{13,5},{2,10},{6,14},... | collective-permute-start | bytes 589832 | tf_op jit(solution)/shard_map/ppermute | solution.py:311
  303.4 25.7 %collective-permute-start.8 = (bf16[256,1024]{1,0:T(8,128)(2,1)S(1)}, bf16[256,1024]{1,0:T(8,128)(2,1)}, u32[]{:S(2)}, u32[]{:S(2)}) collective-permute-start(bf16[256,1024]{1,0:T(8,128)(2,1)S(1)} %add_convert_fusion.2), channel_id=1, source_target_pairs={{0,2},{1,3},{2,0},{3,1},{4,6},{5,7},{6,4},{7,5},{8,10},{9,11},{10,... | collective-permute-start | bytes 1572872 | tf_op jit(solution)/shard_map/ppermute | solution.py:318
  305.0 10.8 %collective-permute-start.20 = (bf16[384,256]{1,0:T(8,128)(2,1)S(1)}, bf16[384,256]{1,0:T(8,128)(2,1)S(1)}, u32[]{:S(2)}, u32[]{:S(2)}) collective-permute-start(bf16[384,256]{1,0:T(8,128)(2,1)S(1)} %add_convert_fusion.5), channel_id=1, source_target_pairs={{0,8},{4,12},{8,0},{12,4},{1,9},{5,13},{9,1},{13,5},{2,10},{6,14},... | collective-permute-start | bytes 589832 | tf_op jit(solution)/shard_map/ppermute | solution.py:318
  315.8 15.6 %collective-permute-start.15 = (bf16[256,1024]{1,0:T(8,128)(2,1)S(1)}, bf16[256,1024]{1,0:T(8,128)(2,1)}, u32[]{:S(2)}, u32[]{:S(2)}) collective-permute-start(bf16[256,1024]{1,0:T(8,128)(2,1)S(1)} %add_convert_fusion.1), channel_id=1, source_target_pairs={{0,2},{1,3},{2,0},{3,1},{4,6},{5,7},{6,4},{7,5},{8,10},{9,11},{10,... | collective-permute-start | bytes 1572872 | tf_op jit(solution)/shard_map/ppermute | solution.py:318
  316.5 9.8 %collective-permute-start.21 = (bf16[768,256]{1,0:T(8,128)(2,1)S(1)}, bf16[768,256]{1,0:T(8,128)(2,1)}, u32[]{:S(2)}, u32[]{:S(2)}) collective-permute-start(bf16[768,256]{1,0:T(8,128)(2,1)S(1)} %maximum_select_fusion.13), channel_id=1, source_target_pairs={{0,4},{4,0},{8,12},{12,8},{1,5},{5,1},{9,13},{13,9},{2,6},{6,2},{1... | collective-permute-start | bytes 1179656 | tf_op jit(solution)/shard_map/ppermute | solution.py:318
  317.1 55.4 %collective-permute-start.39 = (bf16[512,1024]{1,0:T(8,128)(2,1)S(1)}, bf16[512,1024]{1,0:T(8,128)(2,1)}, u32[]{:S(2)}, u32[]{:S(2)}) collective-permute-start(bf16[512,1024]{1,0:T(8,128)(2,1)S(1)} %maximum_select_fusion.7), channel_id=1, source_target_pairs={{0,16},{16,0},{1,17},{17,1},{2,18},{18,2},{3,19},{19,3},{4,20},{20... | collective-permute-start | bytes 3145736 | tf_op jit(solution)/shard_map/ppermute | solution.py:318
  319.9 57.0 %collective-permute-start.45 = (bf16[512,1024]{1,0:T(8,128)(2,1)S(1)}, bf16[512,1024]{1,0:T(8,128)(2,1)}, u32[]{:S(2)}, u32[]{:S(2)}) collective-permute-start(bf16[512,1024]{1,0:T(8,128)(2,1)S(1)} %maximum_select_fusion.8), channel_id=1, source_target_pairs={{0,16},{16,0},{1,17},{17,1},{2,18},{18,2},{3,19},{19,3},{4,20},{20... | collective-permute-start | bytes 3145736 | tf_op jit(solution)/shard_map/ppermute | solution.py:318
  326.3 45.0 %collective-permute-start.33 = (bf16[128,1024]{1,0:T(8,128)(2,1)S(1)}, bf16[128,1024]{1,0:T(8,128)(2,1)S(1)}, u32[]{:S(2)}, u32[]{:S(2)}) collective-permute-start(bf16[128,1024]{1,0:T(8,128)(2,1)S(1)} %maximum_select_fusion.14), channel_id=1, source_target_pairs={{0,16},{16,0},{1,17},{17,1},{2,18},{18,2},{3,19},{19,3},{4,20},{20... | collective-permute-start | bytes 786440 | tf_op jit(solution)/shard_map/ppermute | solution.py:318
  329.2 56.6 %collective-permute-start.22 = (bf16[1536,256]{1,0:T(8,128)(2,1)S(1)}, bf16[1536,256]{1,0:T(8,128)(2,1)S(1)}, u32[]{:S(2)}, u32[]{:S(2)}) collective-permute-start(bf16[1536,256]{1,0:T(8,128)(2,1)S(1)} %maximum_select_fusion.9), channel_id=1, source_target_pairs={{0,16},{16,0},{1,17},{17,1},{2,18},{18,2},{3,19},{19,3},{4,20},{20... | collective-permute-start | bytes 2359304 | tf_op jit(solution)/shard_map/ppermute | solution.py:318
  331.4 56.7 %collective-permute-start.9 = (bf16[512,1024]{1,0:T(8,128)(2,1)S(1)}, bf16[512,1024]{1,0:T(8,128)(2,1)S(1)}, u32[]{:S(2)}, u32[]{:S(2)}) collective-permute-start(bf16[512,1024]{1,0:T(8,128)(2,1)S(1)} %maximum_select_fusion.5), channel_id=1, source_target_pairs={{0,1},{1,0},{2,3},{3,2},{4,5},{5,4},{6,7},{7,6},{8,9},{9,8},{10,11... | collective-permute-start | bytes 3145736 | tf_op jit(solution)/shard_map/ppermute | solution.py:318
  371.3 19.1 %collective-permute-start.16 = (bf16[512,1024]{1,0:T(8,128)(2,1)S(1)}, bf16[512,1024]{1,0:T(8,128)(2,1)S(1)}, u32[]{:S(2)}, u32[]{:S(2)}) collective-permute-start(bf16[512,1024]{1,0:T(8,128)(2,1)S(1)} %maximum_select_fusion.6), channel_id=1, source_target_pairs={{0,1},{1,0},{2,3},{3,2},{4,5},{5,4},{6,7},{7,6},{8,9},{9,8},{10,11... | collective-permute-start | bytes 3145736 | tf_op jit(solution)/shard_map/ppermute | solution.py:318
  388.1 4.7 %copy-start.1 = (bf16[1024,1024]{1,0:T(8,128)(2,1)S(1)}, bf16[1024,1024]{1,0:T(8,128)(2,1)}, u32[]{:S(2)}) copy-start(bf16[1024,1024]{1,0:T(8,128)(2,1)} %param.22) | copy-start | bytes 6291460
  (21 other events, 38.5 us)

commit v2 on v1

v2 whole, which is shorter than its diff:
```python
import functools

import jax
import jax.numpy as jnp
import numpy as np
from jax import lax
from jax.experimental import pallas as pl
from jax.experimental.pallas import tpu as pltpu
from jax.sharding import PartitionSpec as P

HEAD_DIM = 64
ROT = 16
LANES = 128

norm_eps = 1e-05
masked_value = -1e30
low = jnp.bfloat16
wide = jnp.float32


def dot_nn(a, b):
    return lax.dot_general(a, b, (((1,), (0,)), ((), ())), preferred_element_type=wide)


def dot_nt(a, b):
    return lax.dot_general(a, b, (((1,), (1,)), ((), ())), preferred_element_type=wide)


def rotary_tables(length):
    half = ROT // 2
    freqs = np.float32(10000.0) ** (-np.arange(half, dtype=np.float32) * 2.0 / ROT)
    angles = np.arange(length, dtype=np.float32)[:, None] * freqs.astype(np.float32)
    cosine = np.ones((length, HEAD_DIM), np.float32)
    sine = np.zeros((length, HEAD_DIM), np.float32)
    cosine[:, :half] = np.cos(angles)
    cosine[:, half:ROT] = np.cos(angles)
    sine[:, :half] = -np.sin(angles)
    sine[:, half:ROT] = np.sin(angles)
    return np.tile(cosine, (1, LANES // HEAD_DIM)), np.tile(sine, (1, LANES // HEAD_DIM))


def rotate_lanes(x, cosine, sine):
    width = x.shape[1]
    if width < LANES:
        x = jnp.concatenate([x, x], axis=1)
    lane = lax.broadcasted_iota(jnp.int32, x.shape, 1) % HEAD_DIM
    partner = jnp.where(
        lane < ROT // 2, pltpu.roll(x, LANES - ROT // 2, 1), pltpu.roll(x, ROT // 2, 1)
    )
    return (x * cosine + partner * sine)[:, :width]


def half_lanes(shape):
    return lax.broadcasted_iota(jnp.int32, shape, 1) < HEAD_DIM


def swap_halves(x):
    return pltpu.roll(x, HEAD_DIM, 1)


def pack_heads(first, second):
    packed = []
    for c in range(0, first.shape[1], LANES):
        x, y = first[:, c : c + LANES], second[:, c : c + LANES]
        lower = half_lanes(x.shape)
        packed.append(jnp.where(lower, x, swap_halves(y)))
        packed.append(jnp.where(lower, swap_halves(x), y))
    return packed


def unpack_heads(packed):
    first, second = [], []
    for h in range(0, len(packed), 2):
        x, y = packed[h], packed[h + 1]
        lower = half_lanes(x.shape)
        first.append(jnp.where(lower, x, swap_halves(y)))
        second.append(jnp.where(lower, swap_halves(x), y))
    return jnp.concatenate(first, axis=1), jnp.concatenate(second, axis=1)


def normalize_block(x):
    centred = x - jnp.mean(x, axis=1, keepdims=True)
    inverse = lax.rsqrt(jnp.mean(centred * centred, axis=1, keepdims=True) + norm_eps)
    return centred * inverse


def project_kernel(
    places, res, cot, proj, offs, mix, scale, shift, cosine, sine, out, attn_out, feed_out
):
    normed = normalize_block(res[0].astype(wide))
    attn_in = (normed * scale[0:1] + shift[0:1]).astype(low)
    attn_out[0] = attn_in
    feed_out[0] = (normed * scale[1:2] + shift[1:2]).astype(low)
    rows = []
    for i in range(3):
        linear = dot_nn(attn_in, proj[i]) + offs[i : i + 1]
        if i < 2:
            linear = jnp.concatenate(
                [
                    rotate_lanes(linear[:, c : c + LANES], cosine[...], sine[...])
                    for c in range(0, linear.shape[1], LANES)
                ],
                axis=1,
            )
        rows.append(linear)
    rows.append(dot_nt(cot[0], mix[...]))
    for kind in range(2):
        for h, x in enumerate(pack_heads(rows[2 * kind], rows[2 * kind + 1])):
            out[h, kind, 0] = x.astype(low)


def project(residual, cotangent, places, projections, offsets, mixing, scale, shift, tables, dims):
    blocks, span, model = residual.shape
    seq_count, per_device, heads = dims
    local = projections.shape[2]
    whole = lambda *shape: pl.BlockSpec(shape, lambda t, p: (0,) * len(shape))
    token = pl.BlockSpec((1, span, model), lambda t, p: (t, 0, 0))
    table = pl.BlockSpec((span, LANES), lambda t, p: (p[t], 0))
    return pl.pallas_call(
        project_kernel,
        grid_spec=pltpu.PrefetchScalarGridSpec(
            num_scalar_prefetch=1,
            grid=(blocks,),
            in_specs=[
                token,
                token,
                whole(3, model, local),
                whole(3, local),
                whole(local, model),
                whole(2, model),
                whole(2, model),
                table,
                table,
            ],
            out_specs=[
                pl.BlockSpec(
                    (heads, 2, 1, span, LANES),
                    lambda t, p: (t // per_device, 0, t % per_device, 0, 0),
                ),
                token,
                token,
            ],
        ),
        out_shape=[
            jax.ShapeDtypeStruct((seq_count * heads, 2, per_device, span, LANES), low),
            jax.ShapeDtypeStruct((blocks, span, model), low),
            jax.ShapeDtypeStruct((blocks, span, model), low),
        ],
        compiler_params=pltpu.CompilerParams(vmem_limit_bytes=58 * 2**20),
        cost_estimate=pl.CostEstimate(
            flops=8 * blocks * span * model * local, bytes_accessed=12 * 2**20, transcendentals=0
        ),
    )(places, residual, cotangent, projections, offsets, mixing, scale, shift, *tables)


def feed_kernel(feed, cot, expand, thresholds, contract, act, grad, out, part, sums):
    hidden = dot_nn(feed[...], expand[...]) + thresholds[...]
    normal = 0.5 + 0.5 * lax.erf(hidden * float(np.sqrt(0.5)))
    density = jnp.exp(-0.5 * hidden * hidden) * float(1.0 / np.sqrt(2.0 * np.pi))
    activated = (hidden * normal).astype(low)
    act[...] = activated
    slope = normal + hidden * density
    grad_hidden = (dot_nt(cot[...], contract[...]) * slope).astype(low)
    grad[...] = grad_hidden
    out[...] = dot_nn(activated, contract[...])
    part[...] = dot_nt(grad_hidden, expand[...])

    @pl.when(pl.program_id(0) == 0)
    def _():
        sums[...] = jnp.zeros_like(sums)

    sums[0:1] += jnp.sum(grad_hidden.astype(wide), axis=0, keepdims=True)
    sums[1:2] += jnp.sum(cot[...].astype(wide), axis=0, keepdims=True)


def feed_forward(feed_in, upstream, expand, thresholds, contract, span):
    tokens, model = feed_in.shape
    units = expand.shape[1]
    whole = lambda *shape: pl.BlockSpec(shape, lambda t: (0,) * len(shape))
    rows = lambda columns: pl.BlockSpec((span, columns), lambda t: (t, 0))
    return pl.pallas_call(
        feed_kernel,
        grid=(tokens // span,),
        in_specs=[
            rows(model),
            rows(model),
            whole(model, units),
            whole(1, units),
            whole(units, model),
        ],
        out_specs=[rows(units), rows(units), rows(model), rows(model), whole(8, units)],
        out_shape=[
            jax.ShapeDtypeStruct((tokens, units), low),
            jax.ShapeDtypeStruct((tokens, units), low),
            jax.ShapeDtypeStruct((tokens, model), wide),
            jax.ShapeDtypeStruct((tokens, model), wide),
            jax.ShapeDtypeStruct((8, units), wide),
        ],
        compiler_params=pltpu.CompilerParams(vmem_limit_bytes=58 * 2**20),
        cost_estimate=pl.CostEstimate(
            flops=8 * tokens * model * units,
            bytes_accessed=20 * 2**20,
            transcendentals=2 * tokens * units,
        ),
    )(feed_in, upstream, expand, thresholds.reshape(1, units), contract)


def attention_kernel(n, per_device, slots, *refs):
    received, refs = refs[:n], refs[n:]
    cosine, sine = refs[0], refs[1]
    outs, refs = refs[2 : 2 + n], refs[2 + n :]
    xs, ys, k_lo, q_lo, v_hi, g_hi, k_turned, v_turned, strip, sums, sems = refs
    blocks = n * per_device
    span = xs.shape[3]
    tiles, big = strip.shape[0], strip.shape[1]
    ratio = big // span
    scale = HEAD_DIM ** (-0.5)
    to_log2 = scale * float(np.log2(np.e))

    copies = [pltpu.make_async_copy(received[k], xs.at[k], sems.at[k]) for k in range(n)]
    for copy in copies:
        copy.start()
    sums[...] = jnp.zeros_like(sums)
    for copy in copies:
        copy.wait()

    def place(j):
        slot = slots[j]
        return slot // per_device, slot % per_device

    def rows_of(u, size):
        return pl.ds(pl.multiple_of(u * size, size), size)

    lower = half_lanes((span, LANES))

    def order(j, _):
        a, b = place(j)
        rows = rows_of(j, span)
        x, y = xs[a, 0, b].astype(wide), xs[a, 1, b].astype(wide)
        k_lo[rows] = swap_halves(x).astype(low)
        q_lo[rows] = jnp.where(lower, x, 0.0).astype(low)
        v_hi[rows] = swap_halves(y).astype(low)
        g_hi[rows] = jnp.where(lower, 0.0, y).astype(low)
        return 0

    lax.fori_loop(0, blocks, order, 0)

    def turn(u, _):
        rows = rows_of(u, big)
        k_turned[u] = k_lo[rows].astype(wide).T[:HEAD_DIM].astype(low)
        v_turned[u] = v_hi[rows].astype(wide).T[HEAD_DIM:].astype(low)
        return 0

    lax.fori_loop(0, tiles, turn, 0)
    allowed = lax.broadcasted_iota(jnp.int32, (big, big), 0) <= lax.broadcasted_iota(
        jnp.int32, (big, big), 1
    )
    lower_big = half_lanes((big, LANES))

    def query_tile(u, _):
        own = rows_of(u, big)
        q, g = q_lo[own], g_hi[own]
        g_turned = g.astype(wide).T[HEAD_DIM:]

        s = jnp.where(allowed, dot_nt(k_lo[own], q), masked_value)
        strip[u] = s
        top = jnp.max(s, axis=0, keepdims=True)

        def scores(j, top):
            s = dot_nt(k_lo[rows_of(j, big)], q)
            strip[j] = s
            return jnp.maximum(top, jnp.max(s, axis=0, keepdims=True))

        top = lax.fori_loop(0, u, scores, top)

        def weigh(j, carry):
            total, out = carry
            p = jnp.exp2((strip[j] - top) * to_log2)
            strip[j] = p
            return total + jnp.sum(p, axis=0, keepdims=True), out + dot_nn(
                v_turned[j], p.astype(low)
            )

        zeros = jnp.zeros((HEAD_DIM, big), wide)
        total, out = lax.fori_loop(0, u + 1, weigh, (jnp.zeros((1, big), wide), zeros))
        recip = 1.0 / total
        out = out * recip
        slope_scale = scale * recip
        slope_shift = slope_scale * jnp.sum(out * g_turned, axis=0, keepdims=True)

        def back(j, dq):
            p = strip[j]
            dots = dot_nt(v_hi[rows_of(j, big)], g)
            slopes = (p * (dots * slope_scale - slope_shift)).astype(low)
            sums[j] += dot_nn(slopes, q) + dot_nn((p * recip).astype(low), g)
            return dq + dot_nn(k_turned[j], slopes)

        dq = lax.fori_loop(0, u + 1, back, zeros)
        packed = jnp.concatenate([out, dq], axis=0).T
        packed = jnp.where(lower_big, packed, rotate_lanes(packed, cosine[own], -sine[own]))
        packed = packed.astype(low)
        for t in range(ratio):
            a, b = place(u * ratio + t)
            ys[a, 0, b] = packed[t * span : (t + 1) * span]
        return 0

    lax.fori_loop(0, tiles, query_tile, 0)

    def finish(u, _):
        own = rows_of(u, big)
        x = sums[u]
        packed = jnp.where(lower_big, rotate_lanes(x, cosine[own], -sine[own]), x).astype(low)
        for t in range(ratio):
            a, b = place(u * ratio + t)
            ys[a, 1, b] = packed[t * span : (t + 1) * span]
        return 0

    lax.fori_loop(0, tiles, finish, 0)
    copies = [pltpu.make_async_copy(ys.at[k], outs[k], sems.at[k]) for k in range(n)]
    for copy in copies:
        copy.start()
    for copy in copies:
        copy.wait()


def attention(received, slots, tables, per_device):
    n = len(received)
    span = received[0].shape[2]
    blocks = n * per_device
    length = blocks * span
    big = span * (2 if blocks % 2 == 0 else 1)
    tiles = length // big
    anywhere = pl.BlockSpec(memory_space=pl.ANY)
    vmem = pl.BlockSpec(memory_space=pltpu.VMEM)
    pairs = tiles * (tiles + 1) // 2 * big * big
    turned = pltpu.VMEM((length, LANES), low)
    return pl.pallas_call(
        functools.partial(attention_kernel, n, per_device),
        in_specs=[pl.BlockSpec(memory_space=pltpu.SMEM)] + [anywhere] * n + [vmem] * 2,
        out_specs=[anywhere] * n,
        out_shape=[jax.ShapeDtypeStruct(received[0].shape, low)] * n,
        scratch_shapes=[
            pltpu.VMEM((n,) + received[0].shape, low),
            pltpu.VMEM((n,) + received[0].shape, low),
            turned,
            turned,
            turned,
            turned,
            pltpu.VMEM((tiles, HEAD_DIM, big), low),
            pltpu.VMEM((tiles, HEAD_DIM, big), low),
            pltpu.VMEM((tiles, big, big), wide),
            pltpu.VMEM((tiles, big, LANES), wide),
            pltpu.SemaphoreType.DMA((n,)),
        ],
        compiler_params=pltpu.CompilerParams(vmem_limit_bytes=40 * 2**20),
        cost_estimate=pl.CostEstimate(
            flops=12 * pairs * 512, bytes_accessed=8 * 2**20, transcendentals=pairs
        ),
    )(slots, *received, *tables)


def close_kernel(
    back, mix, proj, out, part, res, scale, both, attended_out, linear_out, sums, offs
):
    heads = back.shape[0]
    model = res.shape[2]
    normed = normalize_block(res[0].astype(wide))
    kinds = []
    for kind in range(2):
        kinds += unpack_heads([back[h, kind, 0].astype(wide) for h in range(heads)])
    attended, linear = kinds[0].astype(low), [x.astype(low) for x in kinds[1:]]
    attended_out[...] = attended
    both[:, :model] = (dot_nn(attended, mix[...]) + out[...]).astype(low)
    attn_part = sum(dot_nt(linear[i], proj[i]) for i in range(3))
    feed_part = part[...]
    both[:, model:] = (attn_part * scale[0:1] + feed_part * scale[1:2]).astype(low)

    @pl.when(pl.program_id(0) == 0)
    def _():
        sums[...] = jnp.zeros_like(sums)
        offs[...] = jnp.zeros_like(offs)

    for i in range(3):
        linear_out[i] = linear[i]
        offs[i : i + 1] += jnp.sum(kinds[1 + i].astype(low).astype(wide), axis=0, keepdims=True)
    for i, x in enumerate([attn_part * normed, feed_part * normed, attn_part, feed_part]):
        sums[i : i + 1] += jnp.sum(x, axis=0, keepdims=True)


def close(back, mixing, projections, out, part, residual, scale, first):
    heads, _, per_device, span, _ = back.shape
    local, model = mixing.shape
    whole = lambda *shape: pl.BlockSpec(shape, lambda t: (0,) * len(shape))
    rows = lambda columns: pl.BlockSpec((span, columns), lambda t: (t, 0))
    later = lambda columns: pl.BlockSpec((span, columns), lambda t: (first + t, 0))
    count = per_device * span
    return pl.pallas_call(
        close_kernel,
        grid=(per_device,),
        in_specs=[
            pl.BlockSpec((heads, 2, 1, span, LANES), lambda t: (0, 0, t, 0, 0)),
            whole(local, model),
            whole(3, model, local),
            later(model),
            later(model),
            pl.BlockSpec((1, span, model), lambda t: (first + t, 0, 0)),
            whole(2, model),
        ],
        out_specs=[
            rows(2 * model),
            rows(local),
            pl.BlockSpec((3, span, local), lambda t: (0, t, 0)),
            whole(8, model),
            whole(8, local),
        ],
        out_shape=[
            jax.ShapeDtypeStruct((count, 2 * model), low),
            jax.ShapeDtypeStruct((count, local), low),
            jax.ShapeDtypeStruct((3, count, local), low),
            jax.ShapeDtypeStruct((8, model), wide),
            jax.ShapeDtypeStruct((8, local), wide),
        ],
        compiler_params=pltpu.CompilerParams(vmem_limit_bytes=58 * 2**20),
        cost_estimate=pl.CostEstimate(
            flops=8 * count * model * local, bytes_accessed=12 * 2**20, transcendentals=0
        ),
    )(back, mixing, projections, out, part, residual, scale)


def steps_over(*axes):
    steps = []
    for axis in axes:
        size = lax.axis_size(axis)
        bit = 1
        while bit < size:
            steps.append((axis, [(s, s ^ bit) for s in range(size)], bit))
            bit *= 2
    return steps


def side_of(axis, bit):
    return (lax.axis_index(axis) // bit) % 2


class Order:
    def __init__(self):
        self.token = jnp.zeros((8, LANES), wide)

    def __call__(self, x):
        x, self.token = lax.optimization_barrier((x, self.token))
        return x


class RowSum:
    def __init__(self, x, steps, order, middle=lambda x: x):
        self.x, self.steps, self.order, self.middle = x, steps, order, middle
        self.at = 0

    def step(self):
        count = len(self.steps)
        if self.at < count:
            axis, perm, bit = self.steps[self.at]
            half = self.x.shape[0] // 2
            side = side_of(axis, bit)
            sent = lax.dynamic_slice_in_dim(self.x, (1 - side) * half, half, 0).astype(low)
            kept = lax.dynamic_slice_in_dim(self.x, side * half, half, 0)
            got = lax.ppermute(self.order(sent), axis, perm)
            self.x = kept.astype(wide) + got.astype(wide)
            if self.at == count - 1:
                self.x = self.middle(self.x).astype(low)
        elif self.at < 2 * count:
            axis, perm, bit = self.steps[2 * count - 1 - self.at]
            x = self.order(self.x)
            got = lax.ppermute(x, axis, perm)
            self.x = jnp.where(
                side_of(axis, bit) == 0,
                jnp.concatenate([x, got], axis=0),
                jnp.concatenate([got, x], axis=0),
            )
        self.at += 1

    def done(self):
        return self.at >= 2 * len(self.steps)


def own_rows(x, steps):
    for axis, _, bit in steps:
        half = x.shape[0] // 2
        x = lax.dynamic_slice_in_dim(x, side_of(axis, bit) * half, half, 0)
    return x


def sum_small(x, steps):
    for axis, perm, _ in steps:
        x = x + lax.ppermute(x, axis, perm)
    return x


def on_device(
    residual,
    block_order,
    projections,
    offsets,
    mixing,
    baseline,
    expand,
    thresholds,
    contract,
    norm_scale,
    norm_shift,
    cotangent,
):
    seq_count, local_rows, model = residual.shape
    local = mixing.shape[0]
    heads = local // HEAD_DIM
    n = lax.axis_size("seq")
    me = lax.axis_index("seq")
    blocks = block_order.shape[1]
    length = local_rows * n
    span = length // blocks
    per_device = blocks // n
    tokens = seq_count * local_rows
    rounds = seq_count * heads // n
    tables = [jnp.asarray(t) for t in rotary_tables(length)]
    order = Order()
    batch_steps = steps_over("dp", "seq")
    tensor_steps = steps_over("tensor")

    own_blocks = lax.dynamic_slice_in_dim(block_order, me * per_device, per_device, 1).reshape(-1)
    residual_blocks = residual.reshape(seq_count * per_device, span, model)
    sends, attn_in, feed_in = project(
        residual_blocks,
        cotangent.reshape(residual_blocks.shape),
        own_blocks,
        projections,
        offsets,
        mixing,
        norm_scale,
        norm_shift,
        tables,
        (seq_count, per_device, heads),
    )
    received = []
    for r in range(rounds):
        received.append([lax.dynamic_index_in_dim(sends, r * n + me, 0, keepdims=False)])
        for k in range(1, n):
            part = lax.dynamic_index_in_dim(sends, r * n + (me + k) % n, 0, keepdims=False)
            received[r].append(
                lax.ppermute(order(part), "seq", [(s, (s + k) % n) for s in range(n)])
            )

    stored = jnp.arange(blocks, dtype=jnp.int32)
    slot_of = ((me - stored // per_device) % n) * per_device + stored % per_device

    def slots_in(r):
        order = lax.dynamic_index_in_dim(block_order, (r * n + me) // heads, 0, keepdims=False)
        return jnp.sum(
            jnp.where(order[None, :] == stored[:, None], slot_of[None, :], 0), axis=1
        ).astype(jnp.int32)

    attn_in = attn_in.reshape(tokens, model)
    feed_in = order(feed_in).reshape(tokens, model)
    upstream_low = cotangent.reshape(tokens, model)
    activated, grad_hidden, feed_out, feed_part, feed_sums = feed_forward(
        feed_in, upstream_low, expand, thresholds, contract, span
    )

    def dot_tn(a, b):
        return lax.dot_general(a, b, (((0,), (0,)), ((), ())), preferred_element_type=wide)

    grad_contract, grad_expand = lax.psum(
        order((dot_tn(activated, upstream_low).astype(low), dot_tn(feed_in, grad_hidden).astype(low))),
        ("dp", "seq"),
    )

    back = []
    for r in range(rounds):
        pieces = attention(received[r], slots_in(r), tables, per_device)
        full = jnp.zeros((n,) + pieces[0].shape, low)
        for k in range(n):
            piece = pieces[k]
            if k:
                piece = lax.ppermute(
                    order(piece), "seq", [(s, (s - k) % n) for s in range(n)]
                )
            full = lax.dynamic_update_index_in_dim(full, piece, (me + k) % n, 0)
        back.append(full)

    flat_residual = residual.reshape(tokens, model)

    def finish(mine, totals):
        inputs = own_rows(flat_residual[mine], tensor_steps).astype(wide)
        layer_own = inputs + totals[:, :model] + baseline
        combined = totals[:, model:]
        centred = inputs - jnp.mean(inputs, axis=-1, keepdims=True)
        inverse = lax.rsqrt(jnp.mean(centred * centred, axis=-1, keepdims=True) + norm_eps)
        normed = centred * inverse
        grad_own = own_rows(upstream_low[mine], tensor_steps).astype(wide) + inverse * (
            combined
            - jnp.mean(combined, axis=-1, keepdims=True)
            - normed * jnp.mean(combined * normed, axis=-1, keepdims=True)
        )
        return jnp.concatenate([layer_own.astype(low), grad_own.astype(low)], axis=1)

    small_sums, branches, attended, grad_linear = [], [], [], []
    for s in range(seq_count):
        pairs = range(s * heads, (s + 1) * heads)
        if heads % n == 0:
            pieces = [back[r] for r in range(s * heads // n, (s + 1) * heads // n)]
            pairs_back = pieces[0] if len(pieces) == 1 else jnp.concatenate(pieces, axis=0)
        else:
            pairs_back = jnp.stack([back[p // n][p % n] for p in pairs])
        if s:
            pairs_back = order(pairs_back)
        both, attended_s, linear_s, sums_s, offs_s = close(
            pairs_back,
            mixing,
            projections,
            feed_out,
            feed_part,
            residual_blocks,
            norm_scale,
            s * per_device,
        )
        attended.append(attended_s)
        grad_linear.append(linear_s)
        small_sums.append((sums_s, offs_s))
        mine = slice(s * local_rows, (s + 1) * local_rows)
        branches.append(RowSum(both, tensor_steps, order, functools.partial(finish, mine)))
        branches[s].step()
        if s < seq_count - 1:
            branches[s].step()

    attended = jnp.concatenate(attended, axis=0)
    grad_linear = jnp.concatenate(grad_linear, axis=1)
    grad_projections = RowSum(
        jnp.concatenate([dot_tn(attn_in, grad_linear[i]) for i in range(3)], axis=0),
        batch_steps,
        order,
    )
    grad_projections.step()
    sums = sum_small(sum(s for s, _ in small_sums)[:4], tensor_steps)
    grad_offsets = sum(o for _, o in small_sums)[:3]
    small = jnp.concatenate(
        [sums.reshape(-1), grad_offsets.reshape(-1), feed_sums[0], feed_sums[1]]
    )
    shares = 1
    for axis, _, _ in batch_steps:
        shares *= 2
    unit = model * shares
    padded = -(-small.shape[0] // unit) * unit
    small_rows = jnp.pad(small, (0, padded - small.shape[0])).reshape(-1, model)
    grad_mixing = RowSum(
        jnp.concatenate([dot_tn(attended, upstream_low), small_rows], axis=0), batch_steps, order
    )
    grad_mixing.step()
    params = [grad_projections, grad_mixing]
    while not all(b.done() for b in branches + params):
        for chain in branches[::-1] + params:
            chain.step()

    results = jnp.stack([b.x for b in branches])
    grad_projections = grad_projections.x.astype(wide).reshape(3, model, local)
    small = grad_mixing.x[local:].astype(wide).reshape(-1)
    grad_mixing = grad_mixing.x[:local].astype(wide)
    grad_contract, grad_expand = grad_contract.astype(wide), grad_expand.astype(wide)
    sizes = [2 * model, 2 * model, 3 * local, thresholds.shape[0], model]
    cuts = np.cumsum(sizes)
    grad_scale, grad_shift, grad_offsets, grad_thresholds, grad_baseline = jnp.split(
        small[: cuts[-1]], cuts[:-1]
    )
    return (
        results[:, :, :model],
        results[:, :, model:],
        grad_projections,
        grad_offsets.reshape(3, local),
        grad_mixing,
        grad_baseline,
        grad_expand,
        grad_thresholds,
        grad_contract,
        grad_scale.reshape(2, model),
        grad_shift.reshape(2, model),
    )


def solution(mesh):
    in_specs = (
        P("dp", "seq", None),
        P("dp", None),
        P(None, None, "tensor"),
        P(None, "tensor"),
        P("tensor", None),
        P(),
        P(None, "tensor"),
        P("tensor"),
        P("tensor", None),
        P(),
        P(),
        P("dp", "seq", None),
    )
    out_specs = (
        P("dp", "seq", None),
        P("dp", "seq", None),
        P(None, None, "tensor"),
        P(None, "tensor"),
        P("tensor", None),
        P(),
        P(None, "tensor"),
        P("tensor"),
        P("tensor", None),
        P(),
        P(),
    )
    return jax.shard_map(
        on_device, mesh=mesh, in_specs=in_specs, out_specs=out_specs, check_vma=False
    )
```

time: 398 us -> 333 us (0.84); the launches traced: 393 us -> 333 us
  matrix products: 47.6 us -> 14 us
  Pallas kernels: 45.1 us -> 73 us
  starting transfers between devices: 64.1 us -> 41.8 us
  other arithmetic: 45 us -> 23.7 us
  waiting for transfers between devices: 160 us -> 147 us
  between operations: 2.22 us -> 15.2 us
  local copies, waits for them, and re-layouts: 29.1 us -> 17.8 us
    dot_general x14 -> x6, matrix products: 47.6 us -> 14 us  [dot_tn(): lax.dot_general(a, b, (((0,), (0,)), ((), ())), preferred_element_type=wide)]
    pallas_call x0 -> x3, Pallas kernels: none -> 27.3 us  [the longest x1 14.6 us: feed_forward(): pl.pallas_call(feed_kernel, grid=(tokens // span,), in_specs=[rows(model)...]
    ppermute x41 -> x32, starting transfers between devices: 60.6 us -> 40.1 us  [the longest x6 13.6 us: on_device(): lax.ppermute(order(piece), 'seq', [(s, (s - k) % n) for s in range(n)])]
    select_n x13 -> x10, other arithmetic: 12.2 us -> 3.64 us  [step(): jnp.where(side_of(axis, bit) == 0, jnp.concatenate([x, got], axis=0), jnp...]
    ppermute x5 -> x2, waiting for transfers between devices: 10.6 us -> 2.18 us  [sum_small(): x = x + lax.ppermute(x, axis, perm)]
    convert_element_type x11 -> x8, other arithmetic: 18.8 us -> 11.7 us  [the longest x1 4.22 us: on_device(): grad_expand.astype(wide)]
    unnamed x82 -> x57, local copies, waits for them, and re-layouts: 13.6 us -> 6.73 us
    convert_element_type x16 -> x7, local copies, waits for them, and re-layouts: 6.41 us -> 0.37 us  [step(): lax.dynamic_slice_in_dim(self.x, (1 - side) * half, half, 0).astype(low)]
  transfers between devices with their start and end apart: 46 -> 35, of which waited for: 18 -> 16; matrix products, arithmetic and copies ran while one was open for 26% -> 11% of each run, Pallas kernels for 10% -> 19%
where the time goes in v2:
time: 333 us
  waiting for transfers between devices  147 us (44%)
  Pallas kernels  73 us (22%)
  starting transfers between devices  41.8 us (13%)
  other arithmetic  23.7 us (7%)
  local copies, waits for them, and re-layouts  17.8 us (5%)
  between operations  15.2 us (5%)
  matrix products  14 us (4%)
    ppermute x10, waiting for transfers between devices, step(): got = lax.ppermute(self.order(sent), axis, perm)  52.2 us
    ppermute x10, waiting for transfers between devices, step(): got = lax.ppermute(x, axis, perm)  49 us
    ppermute x6, waiting for transfers between devices, on_device(): lax.ppermute(order(piece), 'seq', [(s, (s - k) % n) for s in range(n)])  43.7 us
    pallas_call x2, Pallas kernels, attention(): pl.pallas_call(functools.partial(attention_kernel, n, per_device), in_spe...  36.2 us
    pallas_call x1, Pallas kernels, feed_forward(): pl.pallas_call(feed_kernel, grid=(tokens // span,), in_specs=[rows(model)...  14.6 us
    dot_general x6, matrix products, dot_tn(): lax.dot_general(a, b, (((0,), (0,)), ((), ())), preferred_element_type=wide)  14 us
    ppermute x6, starting transfers between devices, on_device(): lax.ppermute(order(piece), 'seq', [(s, (s - k) % n) for s in range(n)])  13.6 us
    pallas_call x2, Pallas kernels, close(): pl.pallas_call(close_kernel, grid=(per_device,), in_specs=[pl.BlockSpec((...  12.7 us
  transfers between devices with their start and end apart: 35, of which 16 were waited for; matrix products, arithmetic and copies ran while one was open for 11% of the time, Pallas kernels for 19%

profile of v2, /device:TPU:0, one launch (start us, length us, event | category | flops | bytes accessed | tf_op | source)
XLA Modules:
  0.0 332.6 jit_solution(5784729786089773718)
XLA Ops:
  7.3 0.8 constant_dynamic-slice_fusion.3
  8.6 9.6 %shard_map.221 = (bf16[8,2,2,256,128]{4,3,2,1,0:T(8,128)(2,1)}, bf16[4,256,1024]{2,1,0:T(8,128)(2,1)}, bf16[4,256,1024]{2,1,0:T(8,128)(2,1)}) custom-call(s32[4]{0:T(128)} %reshape.277.places, bf16[4,256,1024]{2,1,0:T(8,128)(2,1)} %bitcast.143, bf16[4,256,1024]{2,1,0:T(8,128)(2,1)} %bitcast.146, bf16[3,1024,256]{2,1,0:T(8,128)(2,1)} %proj.5, f32[3,256]{1,0:T(4,128)} %offs.1, ...), custom_call_target="tpu_custom_call" | custom-call | flops 2147483648 | bytes 12582912 | tf_op jit(solution)/shard_map/pallas_call | solution.py:119
  18.2 2.6 dynamic-slice_bitcast_fusion.3
  20.9 4.0 %collective-permute-start.1 = (bf16[2,2,256,128]{3,2,1,0:T(8,128)(2,1)}, bf16[2,2,256,128]{3,2,1,0:T(8,128)(2,1)S(1)}, u32[]{:S(2)}, u32[]{:S(2)}) collective-permute-start(bf16[2,2,256,128]{3,2,1,0:T(8,128)(2,1)} %get-tuple-element.82), channel_id=1, source_target_pairs={{0,8},{4,12},{8,0},{12,4},{1,9},{5,13},{9,1},{13,5},{2,10},{6,14},... | collective-permute-start | bytes 786440 | tf_op jit(solution)/shard_map/ppermute | solution.py:549
  24.9 1.6 collective-permute-start
  26.5 2.3 collective-permute-start.2
  29.3 14.6 %shard_map.223 = (bf16[1024,1024]{1,0:T(8,128)(2,1)}, bf16[1024,1024]{1,0:T(8,128)(2,1)}, f32[1024,1024]{1,0:T(8,128)}, f32[1024,1024]{1,0:T(8,128)}, f32[8,1024]{1,0:T(8,128)}) custom-call(bf16[1024,1024]{1,0:T(8,128)(2,1)} %bitcast.162, bf16[1024,1024]{1,0:T(8,128)(2,1)} %bitcast.147, bf16[1024,1024]{1,0:T(8,128)(2,1)} %expand.1, f32[1,1024]{1,0:T(1,128)} %bitcast.164, ...), custom_call_target="tpu_custom_call" | custom-call | flops 8589934592 | bytes 20971520 | tf_op jit(solution)/shard_map/pallas_call | solution.py:181
  43.9 5.5 %convolution_convert_fusion = bf16[1024,1024]{1,0:T(8,128)(2,1)} fusion(bf16[1024,1024]{1,0:T(8,128)(2,1)S(1)} %bitcast.163, bf16[1024,1024]{1,0:T(8,128)(2,1)} %get-tuple-element.94), kind=kOutput, calls=%fused_computation.9 | convolution fusion | flops 2148532224 | bytes 6291456 | tf_op jit(solution)/shard_map/dot_general | solution.py:569
  49.4 3.8 %convolution_convert_fusion.1 = bf16[1024,1024]{1,0:T(8,128)(2,1)} fusion(bf16[1024,1024]{1,0:T(8,128)(2,1)S(1)} %copy-done.26, bf16[1024,1024]{1,0:T(8,128)(2,1)S(1)} %bitcast.148), kind=kOutput, calls=%fused_computation.10 | convolution fusion | flops 2148532224 | bytes 6291456 | tf_op jit(solution)/shard_map/dot_general | solution.py:569
  53.3 1.5 copy-done.2
  54.8 1.5 fusion.49
  56.3 0.9 copy-done.4
  57.1 1.6 fusion.48
  58.7 1.3 convert_reduce_fusion
  60.0 1.3 fusion.28
  61.3 1.2 fusion.27
  62.8 0.8 fusion.52
  63.7 3.5 %collective-permute-start.8 = (bf16[2,2,256,128]{3,2,1,0:T(8,128)(2,1)}, bf16[2,2,256,128]{3,2,1,0:T(8,128)(2,1)S(1)}, u32[]{:S(2)}, u32[]{:S(2)}) collective-permute-start(bf16[2,2,256,128]{3,2,1,0:T(8,128)(2,1)} %get-tuple-element.109), channel_id=1, source_target_pairs={{0,12},{4,0},{8,4},{12,8},{1,13},{5,1},{9,5},{13,9},{2,14},{6,2},{... | collective-permute-start | bytes 786440 | tf_op jit(solution)/shard_map/ppermute | solution.py:549
  67.2 18.5 %shard_map.222 = (bf16[2,2,256,128]{3,2,1,0:T(8,128)(2,1)S(1)}, bf16[2,2,256,128]{3,2,1,0:T(8,128)(2,1)S(1)}, bf16[2,2,256,128]{3,2,1,0:T(8,128)(2,1)S(1)}, bf16[2,2,256,128]{3,2,1,0:T(8,128)(2,1)S(1)}) custom-call(s32[8]{0:T(128)S(1)} %get-tuple-element.152.slots, bf16[2,2,256,128]{3,2,1,0:T(8,128)(2,1)S(1)} %get-tuple-element.170.refs_0_, ...), custom_call_target="tpu_custom_call" | custom-call | flops 16106127360 | bytes 8388608 | tf_op jit(solution)/shard_map/pallas_call | solution.py:337
  86.3 1.7 collective-permute-start.4
  88.0 1.9 collective-permute-start.5
  90.0 17.6 %shard_map.225 = (bf16[2,2,256,128]{3,2,1,0:T(8,128)(2,1)S(1)}, bf16[2,2,256,128]{3,2,1,0:T(8,128)(2,1)S(1)}, bf16[2,2,256,128]{3,2,1,0:T(8,128)(2,1)S(1)}, bf16[2,2,256,128]{3,2,1,0:T(8,128)(2,1)S(1)}) custom-call(s32[8]{0:T(128)S(1)} %get-tuple-element.151.slots, bf16[2,2,256,128]{3,2,1,0:T(8,128)(2,1)S(1)} %get-tuple-element.164.refs_0_, ...), custom_call_target="tpu_custom_call" | custom-call | flops 16106127360 | bytes 8388608 | tf_op jit(solution)/shard_map/pallas_call | solution.py:337
  107.6 1.9 collective-permute-start.13
  110.0 7.4 %collective-permute-start.15 = (bf16[2,2,256,128]{3,2,1,0:T(8,128)(2,1)S(1)}, bf16[2,2,256,128]{3,2,1,0:T(8,128)(2,1)S(1)}, u32[]{:S(2)}, u32[]{:S(2)}) collective-permute-start(bf16[2,2,256,128]{3,2,1,0:T(8,128)(2,1)S(1)} %get-tuple-element.123), channel_id=1, source_target_pairs={{0,4},{4,8},{8,12},{12,0},{1,5},{5,9},{9,13},{13,1},{2,6},{6,10},{... | collective-permute-start | bytes 786440 | tf_op jit(solution)/shard_map/ppermute | solution.py:583
  117.5 15.5 %collective-permute-done.13 = bf16[2,2,256,128]{3,2,1,0:T(8,128)(2,1)S(1)} collective-permute-done((bf16[2,2,256,128]{3,2,1,0:T(8,128)(2,1)S(1)}, bf16[2,2,256,128]{3,2,1,0:T(8,128)(2,1)S(1)}, u32[]{:S(2)}, u32[]{:S(2)}) %collective-permute-start.13) | collective-permute-done | bytes 262176 | tf_op jit(solution)/shard_map/ppermute | solution.py:583
  133.0 14.1 %collective-permute-done.4 = bf16[2,2,256,128]{3,2,1,0:T(8,128)(2,1)S(1)} collective-permute-done((bf16[2,2,256,128]{3,2,1,0:T(8,128)(2,1)S(1)}, bf16[2,2,256,128]{3,2,1,0:T(8,128)(2,1)S(1)}, u32[]{:S(2)}, u32[]{:S(2)}) %collective-permute-start.4) | collective-permute-done | bytes 262176 | tf_op jit(solution)/shard_map/ppermute | solution.py:583
  147.2 14.0 %collective-permute-done.14 = bf16[2,2,256,128]{3,2,1,0:T(8,128)(2,1)S(1)} collective-permute-done((bf16[2,2,256,128]{3,2,1,0:T(8,128)(2,1)S(1)}, bf16[2,2,256,128]{3,2,1,0:T(8,128)(2,1)S(1)}, u32[]{:S(2)}, u32[]{:S(2)}) %collective-permute-start.14) | collective-permute-done | bytes 262176 | tf_op jit(solution)/shard_map/ppermute | solution.py:583
  161.4 0.9 copy-done.7
  162.3 6.5 %shard_map.224 = (bf16[512,2048]{1,0:T(8,128)(2,1)}, bf16[512,256]{1,0:T(8,128)(2,1)}, bf16[3,512,256]{2,1,0:T(8,128)(2,1)}, f32[8,1024]{1,0:T(8,128)}, f32[8,256]{1,0:T(8,128)}) custom-call(bf16[4,2,2,256,128]{4,3,2,1,0:T(8,128)(2,1)} %copy-done.7, bf16[256,1024]{1,0:T(8,128)(2,1)} %mix.5, bf16[3,1024,256]{2,1,0:T(8,128)(2,1)} %proj.5, ...), custom_call_target="tpu_custom_call" | custom-call | flops 1073741824 | bytes 12582912 | tf_op jit(solution)/shard_map/pallas_call | solution.py:397
  168.8 6.2 %shard_map.226 = (bf16[512,2048]{1,0:T(8,128)(2,1)}, bf16[512,256]{1,0:T(8,128)(2,1)}, bf16[3,512,256]{2,1,0:T(8,128)(2,1)}, f32[8,1024]{1,0:T(8,128)}, f32[8,256]{1,0:T(8,128)}) custom-call(bf16[4,2,2,256,128]{4,3,2,1,0:T(8,128)(2,1)} %copy-done.6, bf16[256,1024]{1,0:T(8,128)(2,1)} %mix.5, bf16[3,1024,256]{2,1,0:T(8,128)(2,1)} %proj.5, ...), custom_call_target="tpu_custom_call" | custom-call | flops 1073741824 | bytes 12582912 | tf_op jit(solution)/shard_map/pallas_call | solution.py:397
  175.1 1.0 copy-done.14
  176.9 0.7 fusion.35
  177.7 0.7 fusion.34
  180.1 1.6 collective-permute-start.18
  181.7 2.2 collective-permute-done.18
  184.1 1.7 collective-permute-start.28
  185.8 2.5 fusion.33
  188.3 7.2 %collective-permute-done.28 = bf16[132,1024]{1,0:T(8,128)(2,1)S(1)} collective-permute-done((bf16[132,1024]{1,0:T(8,128)(2,1)S(1)}, bf16[132,1024]{1,0:T(8,128)(2,1)S(1)}, u32[]{:S(2)}, u32[]{:S(2)}) %collective-permute-start.28) | collective-permute-done | bytes 270368 | tf_op jit(solution)/shard_map/ppermute | solution.py:467
  196.0 9.8 %collective-permute-done.29 = bf16[66,1024]{1,0:T(8,128)(2,1)S(1)} collective-permute-done((bf16[66,1024]{1,0:T(8,128)(2,1)S(1)}, bf16[66,1024]{1,0:T(8,128)(2,1)S(1)}, u32[]{:S(2)}, u32[]{:S(2)}) %collective-permute-start.29) | collective-permute-done | bytes 135200 | tf_op jit(solution)/shard_map/ppermute | solution.py:467
  206.1 2.7 collective-permute-start.22
  208.9 3.3 %collective-permute-done.30 = bf16[33,1024]{1,0:T(8,128)(2,1)S(1)} collective-permute-done((bf16[33,1024]{1,0:T(8,128)(2,1)S(1)}, bf16[33,1024]{1,0:T(8,128)(2,1)S(1)}, u32[]{:S(2)}, u32[]{:S(2)}) %collective-permute-start.30) | collective-permute-done | bytes 67616 | tf_op jit(solution)/shard_map/ppermute | solution.py:467
  212.5 8.6 %collective-permute-done.31 = bf16[33,1024]{1,0:T(8,128)(2,1)S(1)} collective-permute-done((bf16[33,1024]{1,0:T(8,128)(2,1)S(1)}, bf16[33,1024]{1,0:T(8,128)(2,1)S(1)}, u32[]{:S(2)}, u32[]{:S(2)}) %collective-permute-start.31) | collective-permute-done | bytes 67616 | tf_op jit(solution)/shard_map/ppermute | solution.py:474
  221.5 17.9 %collective-permute-done.32 = bf16[66,1024]{1,0:T(8,128)(2,1)S(1)} collective-permute-done((bf16[66,1024]{1,0:T(8,128)(2,1)S(1)}, bf16[66,1024]{1,0:T(8,128)(2,1)S(1)}, u32[]{:S(2)}, u32[]{:S(2)}) %collective-permute-start.32) | collective-permute-done | bytes 135200 | tf_op jit(solution)/shard_map/ppermute | solution.py:474
  239.4 3.1 collective-permute-start.33
  242.8 4.2 %collective-permute-done.33 = bf16[132,1024]{1,0:T(8,128)(2,1)S(1)} collective-permute-done((bf16[132,1024]{1,0:T(8,128)(2,1)S(1)}, bf16[132,1024]{1,0:T(8,128)(2,1)S(1)}, u32[]{:S(2)}, u32[]{:S(2)}) %collective-permute-start.33) | collective-permute-done | bytes 270368 | tf_op jit(solution)/shard_map/ppermute | solution.py:474
  247.7 1.5 collective-permute-start.10
  249.6 20.0 %collective-permute-done.23 = bf16[768,256]{1,0:T(8,128)(2,1)S(1)} collective-permute-done((bf16[768,256]{1,0:T(8,128)(2,1)S(1)}, bf16[768,256]{1,0:T(8,128)(2,1)S(1)}, u32[]{:S(2)}, u32[]{:S(2)}) %collective-permute-start.23) | collective-permute-done | bytes 393248 | tf_op jit(solution)/shard_map/ppermute | solution.py:467
  269.8 1.6 collective-permute-start.19
  271.4 11.8 %collective-permute-done.24 = bf16[384,256]{1,0:T(8,128)(2,1)S(1)} collective-permute-done((bf16[384,256]{1,0:T(8,128)(2,1)S(1)}, bf16[384,256]{1,0:T(8,128)(2,1)S(1)}, u32[]{:S(2)}, u32[]{:S(2)}) %collective-permute-start.24) | collective-permute-done | bytes 196640 | tf_op jit(solution)/shard_map/ppermute | solution.py:467
  284.0 0.8 copy-done.8
  285.1 1.7 fusion.32
  286.9 1.5 collective-permute-start.11
  288.4 2.7 collective-permute-done.25
  291.4 1.5 collective-permute-start.20
  294.2 4.9 %collective-permute-done.26 = bf16[768,256]{1,0:T(8,128)(2,1)S(1)} collective-permute-done((bf16[768,256]{1,0:T(8,128)(2,1)S(1)}, bf16[768,256]{1,0:T(8,128)(2,1)S(1)}, u32[]{:S(2)}, u32[]{:S(2)}) %collective-permute-start.26) | collective-permute-done | bytes 393248 | tf_op jit(solution)/shard_map/ppermute | solution.py:474
  299.8 3.4 %collective-permute-done.20 = bf16[128,2048]{1,0:T(8,128)(2,1)S(1)} collective-permute-done((bf16[128,2048]{1,0:T(8,128)(2,1)S(1)}, bf16[128,2048]{1,0:T(8,128)(2,1)S(1)}, u32[]{:S(2)}, u32[]{:S(2)}) %collective-permute-start.20) | collective-permute-done | bytes 524320 | tf_op jit(solution)/shard_map/ppermute | solution.py:474
  304.1 1.1 slice_convert_fusion
  305.2 7.2 %collective-permute-done.27 = bf16[1536,256]{1,0:T(8,128)(2,1)S(1)} collective-permute-done((bf16[1536,256]{1,0:T(8,128)(2,1)S(1)}, bf16[1536,256]{1,0:T(8,128)(2,1)S(1)}, u32[]{:S(2)}, u32[]{:S(2)}) %collective-permute-start.27) | collective-permute-done | bytes 786464 | tf_op jit(solution)/shard_map/ppermute | solution.py:474
  312.9 1.9 convert.5
  314.8 1.0 maximum_select_fusion
  315.8 1.0 maximum_select_fusion.1
  316.8 2.2 pad_maximum_fusion.1
  319.0 4.2 %convert_element_type.169 = f32[1024,1024]{1,0:T(8,128)} convert(bf16[1024,1024]{1,0:T(8,128)(2,1)} %get-tuple-element.153) | non-fusion elementwise | flops 1048576 | bytes 6291456 | tf_op jit(solution)/shard_map/convert_element_type | solution.py:666
  323.2 2.5 convert_element_type.170
  (159 shorter events, 12.7 us)
Async XLA Ops:
  7.2 311.8 %all-reduce.4.cloned.1.call-start = ((), (), s32[]{:S(2)}) async-start(), calls=%async_computation | async-start | bytes 8388608 | tf_op jit(solution)/shard_map/psum | solution.py:571
  20.9 42.8 %collective-permute-start.1 = (bf16[2,2,256,128]{3,2,1,0:T(8,128)(2,1)}, bf16[2,2,256,128]{3,2,1,0:T(8,128)(2,1)S(1)}, u32[]{:S(2)}, u32[]{:S(2)}) collective-permute-start(bf16[2,2,256,128]{3,2,1,0:T(8,128)(2,1)} %get-tuple-element.82), channel_id=1, source_target_pairs={{0,8},{4,12},{8,0},{12,4},{1,9},{5,13},{9,1},{13,5},{2,10},{6,14},... | collective-permute-start | bytes 786440 | tf_op jit(solution)/shard_map/ppermute | solution.py:549
  24.9 42.3 %collective-permute-start = (bf16[2,2,256,128]{3,2,1,0:T(8,128)(2,1)}, bf16[2,2,256,128]{3,2,1,0:T(8,128)(2,1)}, u32[]{:S(2)}, u32[]{:S(2)}) collective-permute-start(bf16[2,2,256,128]{3,2,1,0:T(8,128)(2,1)} %get-tuple-element.80), channel_id=1, source_target_pairs={{0,4},{4,8},{8,12},{12,0},{1,5},{5,9},{9,13},{13,1},{2,6},{6,10},{... | collective-permute-start | bytes 786440 | tf_op jit(solution)/shard_map/ppermute | solution.py:549
  26.5 40.7 %collective-permute-start.2 = (bf16[2,2,256,128]{3,2,1,0:T(8,128)(2,1)}, bf16[2,2,256,128]{3,2,1,0:T(8,128)(2,1)}, u32[]{:S(2)}, u32[]{:S(2)}) collective-permute-start(bf16[2,2,256,128]{3,2,1,0:T(8,128)(2,1)} %get-tuple-element.84), channel_id=1, source_target_pairs={{0,12},{4,0},{8,4},{12,8},{1,13},{5,1},{9,5},{13,9},{2,14},{6,2},{... | collective-permute-start | bytes 786440 | tf_op jit(solution)/shard_map/ppermute | solution.py:549
  28.7 59.3 %collective-permute-start.6 = (bf16[2,2,256,128]{3,2,1,0:T(8,128)(2,1)}, bf16[2,2,256,128]{3,2,1,0:T(8,128)(2,1)S(1)}, u32[]{:S(2)}, u32[]{:S(2)}) collective-permute-start(bf16[2,2,256,128]{3,2,1,0:T(8,128)(2,1)} %get-tuple-element.107), channel_id=1, source_target_pairs={{0,4},{4,8},{8,12},{12,0},{1,5},{5,9},{9,13},{13,1},{2,6},{6,10},{... | collective-permute-start | bytes 786440 | tf_op jit(solution)/shard_map/ppermute | solution.py:549
  28.7 61.3 %collective-permute-start.7 = (bf16[2,2,256,128]{3,2,1,0:T(8,128)(2,1)}, bf16[2,2,256,128]{3,2,1,0:T(8,128)(2,1)S(1)}, u32[]{:S(2)}, u32[]{:S(2)}) collective-permute-start(bf16[2,2,256,128]{3,2,1,0:T(8,128)(2,1)} %get-tuple-element.108), channel_id=1, source_target_pairs={{0,8},{4,12},{8,0},{12,4},{1,9},{5,13},{9,1},{13,5},{2,10},{6,14},... | collective-permute-start | bytes 786440 | tf_op jit(solution)/shard_map/ppermute | solution.py:549
  29.3 14.6 %copy-start.25 = (bf16[4,256,1024]{2,1,0:T(8,128)(2,1)S(1)}, bf16[4,256,1024]{2,1,0:T(8,128)(2,1)}, u32[]{:S(2)}) copy-start(bf16[4,256,1024]{2,1,0:T(8,128)(2,1)} %get-tuple-element.92) | copy-start | bytes 6291460
  43.9 5.5 %copy-start.3 = (bf16[2,512,1024]{2,1,0:T(8,128)(2,1)S(1)}, bf16[2,512,1024]{2,1,0:T(8,128)(2,1)}, u32[]{:S(2)}) copy-start(bf16[2,512,1024]{2,1,0:T(8,128)(2,1)} %param.25) | copy-start | bytes 6291460
  43.9 5.5 %copy-start.26 = (bf16[1024,1024]{1,0:T(8,128)(2,1)S(1)}, bf16[1024,1024]{1,0:T(8,128)(2,1)}, u32[]{:S(2)}) copy-start(bf16[1024,1024]{1,0:T(8,128)(2,1)} %get-tuple-element.93) | copy-start | bytes 6291460
  53.2 1.6 copy-start.2
  54.8 2.3 copy-start.4
  57.1 5.3 %copy-start.20 = (s32[2,8]{1,0:T(2,128)S(1)}, s32[2,8]{1,0:T(2,128)}, u32[]{:S(2)}) copy-start(s32[2,8]{1,0:T(2,128)} %param.15) | copy-start | bytes 196
  57.1 10.0 %copy-start = (f32[2048,128]{1,0:T(8,128)S(1)}, f32[2048,128]{1,0:T(8,128)}, u32[]{:S(2)}) copy-start(f32[2048,128]{1,0:T(8,128)} %constant.413.clone.cosine.refs_4_) | copy-start | bytes 3145732
  57.1 10.0 %copy-start.1 = (f32[2048,128]{1,0:T(8,128)S(1)}, f32[2048,128]{1,0:T(8,128)}, u32[]{:S(2)}) copy-start(f32[2048,128]{1,0:T(8,128)} %constant.414.clone.sine.refs_5_) | copy-start | bytes 3145732
  63.7 26.3 %collective-permute-start.8 = (bf16[2,2,256,128]{3,2,1,0:T(8,128)(2,1)}, bf16[2,2,256,128]{3,2,1,0:T(8,128)(2,1)S(1)}, u32[]{:S(2)}, u32[]{:S(2)}) collective-permute-start(bf16[2,2,256,128]{3,2,1,0:T(8,128)(2,1)} %get-tuple-element.109), channel_id=1, source_target_pairs={{0,12},{4,0},{8,4},{12,8},{1,13},{5,1},{9,5},{13,9},{2,14},{6,2},{... | collective-permute-start | bytes 786440 | tf_op jit(solution)/shard_map/ppermute | solution.py:549
  85.7 24.3 %collective-permute-start.3 = (bf16[2,2,256,128]{3,2,1,0:T(8,128)(2,1)S(1)}, bf16[2,2,256,128]{3,2,1,0:T(8,128)(2,1)S(1)}, u32[]{:S(2)}, u32[]{:S(2)}) collective-permute-start(bf16[2,2,256,128]{3,2,1,0:T(8,128)(2,1)S(1)} %get-tuple-element.97), channel_id=1, source_target_pairs={{0,12},{4,0},{8,4},{12,8},{1,13},{5,1},{9,5},{13,9},{2,14},{6,2},{... | collective-permute-start | bytes 786440 | tf_op jit(solution)/shard_map/ppermute | solution.py:583
  86.3 60.8 %collective-permute-start.4 = (bf16[2,2,256,128]{3,2,1,0:T(8,128)(2,1)S(1)}, bf16[2,2,256,128]{3,2,1,0:T(8,128)(2,1)S(1)}, u32[]{:S(2)}, u32[]{:S(2)}) collective-permute-start(bf16[2,2,256,128]{3,2,1,0:T(8,128)(2,1)S(1)} %get-tuple-element.100), channel_id=1, source_target_pairs={{0,8},{4,12},{8,0},{12,4},{1,9},{5,13},{9,1},{13,5},{2,10},{6,14},... | collective-permute-start | bytes 786440 | tf_op jit(solution)/shard_map/ppermute | solution.py:583
  88.0 73.2 %collective-permute-start.5 = (bf16[2,2,256,128]{3,2,1,0:T(8,128)(2,1)S(1)}, bf16[2,2,256,128]{3,2,1,0:T(8,128)(2,1)S(1)}, u32[]{:S(2)}, u32[]{:S(2)}) collective-permute-start(bf16[2,2,256,128]{3,2,1,0:T(8,128)(2,1)S(1)} %get-tuple-element.103), channel_id=1, source_target_pairs={{0,4},{4,8},{8,12},{12,0},{1,5},{5,9},{9,13},{13,1},{2,6},{6,10},{... | collective-permute-start | bytes 786440 | tf_op jit(solution)/shard_map/ppermute | solution.py:583
  107.6 25.4 %collective-permute-start.13 = (bf16[2,2,256,128]{3,2,1,0:T(8,128)(2,1)S(1)}, bf16[2,2,256,128]{3,2,1,0:T(8,128)(2,1)S(1)}, u32[]{:S(2)}, u32[]{:S(2)}) collective-permute-start(bf16[2,2,256,128]{3,2,1,0:T(8,128)(2,1)S(1)} %get-tuple-element.121), channel_id=1, source_target_pairs={{0,12},{4,0},{8,4},{12,8},{1,13},{5,1},{9,5},{13,9},{2,14},{6,2},{... | collective-permute-start | bytes 786440 | tf_op jit(solution)/shard_map/ppermute | solution.py:583
  109.5 51.7 %collective-permute-start.14 = (bf16[2,2,256,128]{3,2,1,0:T(8,128)(2,1)S(1)}, bf16[2,2,256,128]{3,2,1,0:T(8,128)(2,1)S(1)}, u32[]{:S(2)}, u32[]{:S(2)}) collective-permute-start(bf16[2,2,256,128]{3,2,1,0:T(8,128)(2,1)S(1)} %get-tuple-element.122), channel_id=1, source_target_pairs={{0,8},{4,12},{8,0},{12,4},{1,9},{5,13},{9,1},{13,5},{2,10},{6,14},... | collective-permute-start | bytes 786440 | tf_op jit(solution)/shard_map/ppermute | solution.py:583
  110.0 51.2 %collective-permute-start.15 = (bf16[2,2,256,128]{3,2,1,0:T(8,128)(2,1)S(1)}, bf16[2,2,256,128]{3,2,1,0:T(8,128)(2,1)S(1)}, u32[]{:S(2)}, u32[]{:S(2)}) collective-permute-start(bf16[2,2,256,128]{3,2,1,0:T(8,128)(2,1)S(1)} %get-tuple-element.123), channel_id=1, source_target_pairs={{0,4},{4,8},{8,12},{12,0},{1,5},{5,9},{9,13},{13,1},{2,6},{6,10},{... | collective-permute-start | bytes 786440 | tf_op jit(solution)/shard_map/ppermute | solution.py:583
  161.4 1.0 copy-start.7
  161.4 7.4 %copy-start.6 = (bf16[4,2,2,256,128]{4,3,2,1,0:T(8,128)(2,1)}, bf16[4,2,2,256,128]{4,3,2,1,0:T(8,128)(2,1)S(1)}, u32[]{:S(2)}) copy-start(bf16[4,2,2,256,128]{4,3,2,1,0:T(8,128)(2,1)S(1)} %get-tuple-element.125.back) | copy-start | bytes 3145732
  168.8 6.3 %copy-start.13 = (bf16[3,512,256]{2,1,0:T(8,128)(2,1)S(1)}, bf16[3,512,256]{2,1,0:T(8,128)(2,1)}, u32[]{:S(2)}) copy-start(bf16[3,512,256]{2,1,0:T(8,128)(2,1)} %get-tuple-element.137) | copy-start | bytes 2359300
  175.1 1.1 copy-start.14
  175.1 1.8 copy-start.24
  176.2 1.4 copy-start.15
  177.7 0.8 copy-start.18
  177.7 0.8 copy-start.19
  177.7 1.6 copy-start.5
  177.7 1.6 copy-start.16
  177.7 1.7 copy-start.17
  178.5 3.3 copy-start.22
  178.5 3.3 copy-start.23
  178.5 1.6 collective-permute-start.17
  180.1 3.8 %collective-permute-start.18 = (f32[4,1024]{1,0:T(4,128)S(1)}, f32[4,1024]{1,0:T(4,128)S(1)}, u32[]{:S(2)}, u32[]{:S(2)}) collective-permute-start(f32[4,1024]{1,0:T(4,128)S(1)} %add.386), channel_id=1, source_target_pairs={{0,2},{1,3},{2,0},{3,1},{4,6},{5,7},{6,4},{7,5},{8,10},{9,11},{10,... | collective-permute-start | bytes 49160 | tf_op jit(solution)/shard_map/ppermute | solution.py:495
  184.1 11.4 %collective-permute-start.28 = (bf16[132,1024]{1,0:T(8,128)(2,1)S(1)}, bf16[132,1024]{1,0:T(8,128)(2,1)S(1)}, u32[]{:S(2)}, u32[]{:S(2)}) collective-permute-start(bf16[132,1024]{1,0:T(8,128)(2,1)S(1)} %fusion.14), channel_id=1, source_target_pairs={{0,16},{16,0},{1,17},{17,1},{2,18},{18,2},{3,19},{19,3},{4,20},{20... | collective-permute-start | bytes 811016 | tf_op jit(solution)/shard_map/ppermute | solution.py:467
  195.7 10.1 %collective-permute-start.29 = (bf16[66,1024]{1,0:T(8,128)(2,1)S(1)}, bf16[66,1024]{1,0:T(8,128)(2,1)S(1)}, u32[]{:S(2)}, u32[]{:S(2)}) collective-permute-start(bf16[66,1024]{1,0:T(8,128)(2,1)S(1)} %dynamic-slice_convert_fusion.5), channel_id=1, source_target_pairs={{0,4},{4,0},{8,12},{12,8},{1,5},{5,1},{9,13},{13,9},{2,6},{6,2},{1... | collective-permute-start | bytes 405512 | tf_op jit(solution)/shard_map/ppermute | solution.py:467
  196.0 16.3 %copy-start.12 = (bf16[512,2048]{1,0:T(8,128)(2,1)S(1)}, bf16[512,2048]{1,0:T(8,128)(2,1)}, u32[]{:S(2)}) copy-start(bf16[512,2048]{1,0:T(8,128)(2,1)} %get-tuple-element.106) | copy-start | bytes 6291460
  205.9 15.3 %copy-start.11 = (bf16[512,2048]{1,0:T(8,128)(2,1)S(1)}, bf16[512,2048]{1,0:T(8,128)(2,1)}, u32[]{:S(2)}) copy-start(bf16[512,2048]{1,0:T(8,128)(2,1)} %get-tuple-element.126) | copy-start | bytes 6291460
  205.9 6.3 %collective-permute-start.30 = (bf16[33,1024]{1,0:T(8,128)(2,1)S(1)}, bf16[33,1024]{1,0:T(8,128)(2,1)S(1)}, u32[]{:S(2)}, u32[]{:S(2)}) collective-permute-start(bf16[33,1024]{1,0:T(8,128)(2,1)S(1)} %dynamic-slice_convert_fusion.6), channel_id=1, source_target_pairs={{0,8},{4,12},{8,0},{12,4},{1,9},{5,13},{9,1},{13,5},{2,10},{6,14},... | collective-permute-start | bytes 202760 | tf_op jit(solution)/shard_map/ppermute | solution.py:467
  206.1 36.4 %collective-permute-start.22 = (bf16[1536,256]{1,0:T(8,128)(2,1)S(1)}, bf16[1536,256]{1,0:T(8,128)(2,1)S(1)}, u32[]{:S(2)}, u32[]{:S(2)}) collective-permute-start(bf16[1536,256]{1,0:T(8,128)(2,1)S(1)} %dynamic-slice_convert_fusion), channel_id=1, source_target_pairs={{0,16},{16,0},{1,17},{17,1},{2,18},{18,2},{3,19},{19,3},{4,20},{20... | collective-permute-start | bytes 2359304 | tf_op jit(solution)/shard_map/ppermute | solution.py:467
  212.2 8.9 %collective-permute-start.31 = (bf16[33,1024]{1,0:T(8,128)(2,1)S(1)}, bf16[33,1024]{1,0:T(8,128)(2,1)S(1)}, u32[]{:S(2)}, u32[]{:S(2)}) collective-permute-start(bf16[33,1024]{1,0:T(8,128)(2,1)S(1)} %add_convert_fusion.1), channel_id=1, source_target_pairs={{0,8},{4,12},{8,0},{12,4},{1,9},{5,13},{9,1},{13,5},{2,10},{6,14},... | collective-permute-start | bytes 202760 | tf_op jit(solution)/shard_map/ppermute | solution.py:474
  212.4 34.8 %collective-permute-start.9 = (bf16[256,2048]{1,0:T(8,128)(2,1)S(1)}, bf16[256,2048]{1,0:T(8,128)(2,1)S(1)}, u32[]{:S(2)}, u32[]{:S(2)}) collective-permute-start(bf16[256,2048]{1,0:T(8,128)(2,1)S(1)} %constant_dynamic-slice_fusion.2), channel_id=1, source_target_pairs={{0,1},{1,0},{2,3},{3,2},{4,5},{5,4},{6,7},{7,6},{8,9},{9,8},{10,11... | collective-permute-start | bytes 3145736 | tf_op jit(solution)/shard_map/ppermute | solution.py:467
  221.2 18.2 %collective-permute-start.32 = (bf16[66,1024]{1,0:T(8,128)(2,1)S(1)}, bf16[66,1024]{1,0:T(8,128)(2,1)S(1)}, u32[]{:S(2)}, u32[]{:S(2)}) collective-permute-start(bf16[66,1024]{1,0:T(8,128)(2,1)S(1)} %maximum_select_fusion.9), channel_id=1, source_target_pairs={{0,4},{4,0},{8,12},{12,8},{1,5},{5,1},{9,13},{13,9},{2,6},{6,2},{1... | collective-permute-start | bytes 405512 | tf_op jit(solution)/shard_map/ppermute | solution.py:474
  221.4 27.8 %collective-permute-start.16 = (bf16[256,2048]{1,0:T(8,128)(2,1)S(1)}, bf16[256,2048]{1,0:T(8,128)(2,1)S(1)}, u32[]{:S(2)}, u32[]{:S(2)}) collective-permute-start(bf16[256,2048]{1,0:T(8,128)(2,1)S(1)} %constant_dynamic-slice_fusion), channel_id=1, source_target_pairs={{0,1},{1,0},{2,3},{3,2},{4,5},{5,4},{6,7},{7,6},{8,9},{9,8},{10,11... | collective-permute-start | bytes 3145736 | tf_op jit(solution)/shard_map/ppermute | solution.py:467
  239.4 7.6 %collective-permute-start.33 = (bf16[132,1024]{1,0:T(8,128)(2,1)S(1)}, bf16[132,1024]{1,0:T(8,128)(2,1)S(1)}, u32[]{:S(2)}, u32[]{:S(2)}) collective-permute-start(bf16[132,1024]{1,0:T(8,128)(2,1)S(1)} %maximum_select_fusion.8), channel_id=1, source_target_pairs={{0,16},{16,0},{1,17},{17,1},{2,18},{18,2},{3,19},{19,3},{4,20},{20... | collective-permute-start | bytes 811016 | tf_op jit(solution)/shard_map/ppermute | solution.py:474
  242.7 26.8 %collective-permute-start.23 = (bf16[768,256]{1,0:T(8,128)(2,1)S(1)}, bf16[768,256]{1,0:T(8,128)(2,1)S(1)}, u32[]{:S(2)}, u32[]{:S(2)}) collective-permute-start(bf16[768,256]{1,0:T(8,128)(2,1)S(1)} %dynamic-slice_convert_fusion.3), channel_id=1, source_target_pairs={{0,4},{4,0},{8,12},{12,8},{1,5},{5,1},{9,13},{13,9},{2,6},{6,2},{1... | collective-permute-start | bytes 1179656 | tf_op jit(solution)/shard_map/ppermute | solution.py:467
  247.7 35.7 %collective-permute-start.10 = (bf16[128,2048]{1,0:T(8,128)(2,1)S(1)}, bf16[128,2048]{1,0:T(8,128)(2,1)S(1)}, u32[]{:S(2)}, u32[]{:S(2)}) collective-permute-start(bf16[128,2048]{1,0:T(8,128)(2,1)S(1)} %dynamic-slice_convert_fusion.2), channel_id=1, source_target_pairs={{0,2},{1,3},{2,0},{3,1},{4,6},{5,7},{6,4},{7,5},{8,10},{9,11},{10,... | collective-permute-start | bytes 1572872 | tf_op jit(solution)/shard_map/ppermute | solution.py:467
  269.7 13.9 %copy-start.9 = (bf16[1,512,1024]{2,1,0:T(8,128)(2,1)S(1)}, bf16[1,512,1024]{2,1,0:T(8,128)(2,1)}, u32[]{:S(2)}) copy-start(bf16[1,512,1024]{2,1,0:T(8,128)(2,1)} %get-tuple-element.162) | copy-start | bytes 3145732
  269.7 13.6 %collective-permute-start.24 = (bf16[384,256]{1,0:T(8,128)(2,1)S(1)}, bf16[384,256]{1,0:T(8,128)(2,1)S(1)}, u32[]{:S(2)}, u32[]{:S(2)}) collective-permute-start(bf16[384,256]{1,0:T(8,128)(2,1)S(1)} %dynamic-slice_convert_fusion.4), channel_id=1, source_target_pairs={{0,8},{4,12},{8,0},{12,4},{1,9},{5,13},{9,1},{13,5},{2,10},{6,14},... | collective-permute-start | bytes 589832 | tf_op jit(solution)/shard_map/ppermute | solution.py:467
  269.8 14.0 %collective-permute-start.19 = (bf16[128,2048]{1,0:T(8,128)(2,1)S(1)}, bf16[128,2048]{1,0:T(8,128)(2,1)S(1)}, u32[]{:S(2)}, u32[]{:S(2)}) collective-permute-start(bf16[128,2048]{1,0:T(8,128)(2,1)S(1)} %dynamic-slice_convert_fusion.1), channel_id=1, source_target_pairs={{0,2},{1,3},{2,0},{3,1},{4,6},{5,7},{6,4},{7,5},{8,10},{9,11},{10,... | collective-permute-start | bytes 1572872 | tf_op jit(solution)/shard_map/ppermute | solution.py:467
  283.3 7.8 %collective-permute-start.25 = (bf16[384,256]{1,0:T(8,128)(2,1)S(1)}, bf16[384,256]{1,0:T(8,128)(2,1)S(1)}, u32[]{:S(2)}, u32[]{:S(2)}) collective-permute-start(bf16[384,256]{1,0:T(8,128)(2,1)S(1)} %add_convert_fusion), channel_id=1, source_target_pairs={{0,8},{4,12},{8,0},{12,4},{1,9},{5,13},{9,1},{13,5},{2,10},{6,14},... | collective-permute-start | bytes 589832 | tf_op jit(solution)/shard_map/ppermute | solution.py:474
  283.6 1.2 copy-start.8
  283.6 1.5 copy-start.21
  286.9 12.6 %collective-permute-start.11 = (bf16[128,2048]{1,0:T(8,128)(2,1)S(1)}, bf16[128,2048]{1,0:T(8,128)(2,1)S(1)}, u32[]{:S(2)}, u32[]{:S(2)}) collective-permute-start(bf16[128,2048]{1,0:T(8,128)(2,1)S(1)} %pad_maximum_fusion.2), channel_id=1, source_target_pairs={{0,2},{1,3},{2,0},{3,1},{4,6},{5,7},{6,4},{7,5},{8,10},{9,11},{10,... | collective-permute-start | bytes 1572872 | tf_op jit(solution)/shard_map/ppermute | solution.py:474
  291.3 7.8 %collective-permute-start.26 = (bf16[768,256]{1,0:T(8,128)(2,1)S(1)}, bf16[768,256]{1,0:T(8,128)(2,1)S(1)}, u32[]{:S(2)}, u32[]{:S(2)}) collective-permute-start(bf16[768,256]{1,0:T(8,128)(2,1)S(1)} %maximum_select_fusion.7), channel_id=1, source_target_pairs={{0,4},{4,0},{8,12},{12,8},{1,5},{5,1},{9,13},{13,9},{2,6},{6,2},{1... | collective-permute-start | bytes 1179656 | tf_op jit(solution)/shard_map/ppermute | solution.py:474
  291.4 11.8 %collective-permute-start.20 = (bf16[128,2048]{1,0:T(8,128)(2,1)S(1)}, bf16[128,2048]{1,0:T(8,128)(2,1)S(1)}, u32[]{:S(2)}, u32[]{:S(2)}) collective-permute-start(bf16[128,2048]{1,0:T(8,128)(2,1)S(1)} %pad_maximum_fusion.3), channel_id=1, source_target_pairs={{0,2},{1,3},{2,0},{3,1},{4,6},{5,7},{6,4},{7,5},{8,10},{9,11},{10,... | collective-permute-start | bytes 1572872 | tf_op jit(solution)/shard_map/ppermute | solution.py:474
  299.4 13.1 %collective-permute-start.27 = (bf16[1536,256]{1,0:T(8,128)(2,1)S(1)}, bf16[1536,256]{1,0:T(8,128)(2,1)S(1)}, u32[]{:S(2)}, u32[]{:S(2)}) collective-permute-start(bf16[1536,256]{1,0:T(8,128)(2,1)S(1)} %maximum_select_fusion.5), channel_id=1, source_target_pairs={{0,16},{16,0},{1,17},{17,1},{2,18},{18,2},{3,19},{19,3},{4,20},{20... | collective-permute-start | bytes 2359304 | tf_op jit(solution)/shard_map/ppermute | solution.py:474
  299.7 15.1 %collective-permute-start.12 = (bf16[256,2048]{1,0:T(8,128)(2,1)S(1)}, bf16[256,2048]{1,0:T(8,128)(2,1)S(1)}, u32[]{:S(2)}, u32[]{:S(2)}) collective-permute-start(bf16[256,2048]{1,0:T(8,128)(2,1)S(1)} %maximum_select_fusion.3), channel_id=1, source_target_pairs={{0,1},{1,0},{2,3},{3,2},{4,5},{5,4},{6,7},{7,6},{8,9},{9,8},{10,11... | collective-permute-start | bytes 3145736 | tf_op jit(solution)/shard_map/ppermute | solution.py:474
  303.4 12.3 %collective-permute-start.21 = (bf16[256,2048]{1,0:T(8,128)(2,1)S(1)}, bf16[256,2048]{1,0:T(8,128)(2,1)S(1)}, u32[]{:S(2)}, u32[]{:S(2)}) collective-permute-start(bf16[256,2048]{1,0:T(8,128)(2,1)S(1)} %maximum_select_fusion.4), channel_id=1, source_target_pairs={{0,1},{1,0},{2,3},{3,2},{4,5},{5,4},{6,7},{7,6},{8,9},{9,8},{10,11... | collective-permute-start | bytes 3145736 | tf_op jit(solution)/shard_map/ppermute | solution.py:474
  319.0 4.2 %copy-start.10 = (bf16[1024,1024]{1,0:T(8,128)(2,1)S(1)}, bf16[1024,1024]{1,0:T(8,128)(2,1)}, u32[]{:S(2)}) copy-start(bf16[1024,1024]{1,0:T(8,128)(2,1)} %get-tuple-element.154) | copy-start | bytes 6291460
Sparse Core Ops, SparseCore 0:
  53.3 222.5 all-reduce.3

commit v3 on v2

--- a/solution.py
+++ b/solution.py
@@ -442,36 +442,40 @@
     return (lax.axis_index(axis) // bit) % 2
 
 
-class Order:
-    def __init__(self):
-        self.token = jnp.zeros((8, LANES), wide)
-
-    def __call__(self, x):
-        x, self.token = lax.optimization_barrier((x, self.token))
-        return x
+def after(x, earlier):
+    first = earlier[(0,) * earlier.ndim].astype(wide)
+    return x + jnp.minimum(jnp.abs(first), 0.0).astype(x.dtype)
 
 
 class RowSum:
-    def __init__(self, x, steps, order, middle=lambda x: x):
-        self.x, self.steps, self.order, self.middle = x, steps, order, middle
+    def __init__(self, x, steps, middle=lambda x: x):
+        self.x, self.steps, self.middle = x, steps, middle
+        self.sent = None
         self.at = 0
 
-    def step(self):
+    def step(self, earlier=None):
         count = len(self.steps)
+        if self.done():
+            return
         if self.at < count:
             axis, perm, bit = self.steps[self.at]
             half = self.x.shape[0] // 2
             side = side_of(axis, bit)
             sent = lax.dynamic_slice_in_dim(self.x, (1 - side) * half, half, 0).astype(low)
             kept = lax.dynamic_slice_in_dim(self.x, side * half, half, 0)
-            got = lax.ppermute(self.order(sent), axis, perm)
+            if earlier is not None:
+                sent = after(sent, earlier)
+            self.sent = sent
+            got = lax.ppermute(sent, axis, perm)
             self.x = kept.astype(wide) + got.astype(wide)
             if self.at == count - 1:
                 self.x = self.middle(self.x).astype(low)
-        elif self.at < 2 * count:
+        else:
             axis, perm, bit = self.steps[2 * count - 1 - self.at]
-            x = self.order(self.x)
+            x = self.x if earlier is None else after(self.x, earlier)
+            self.sent = x
             got = lax.ppermute(x, axis, perm)
+            self.last = (side_of(axis, bit), x, got)
             self.x = jnp.where(
                 side_of(axis, bit) == 0,
                 jnp.concatenate([x, got], axis=0),
@@ -522,7 +526,6 @@
     tokens = seq_count * local_rows
     rounds = seq_count * heads // n
     tables = [jnp.asarray(t) for t in rotary_tables(length)]
-    order = Order()
     batch_steps = steps_over("dp", "seq")
     tensor_steps = steps_over("tensor")
 
@@ -542,12 +545,11 @@
     )
     received = []
     for r in range(rounds):
+        first = r * n
         received.append([lax.dynamic_index_in_dim(sends, r * n + me, 0, keepdims=False)])
         for k in range(1, n):
-            part = lax.dynamic_index_in_dim(sends, r * n + (me + k) % n, 0, keepdims=False)
-            received[r].append(
-                lax.ppermute(order(part), "seq", [(s, (s + k) % n) for s in range(n)])
-            )
+            part = lax.dynamic_index_in_dim(sends, first + (me + k) % n, 0, keepdims=False)
+            received[r].append(lax.ppermute(part, "seq", [(s, (s + k) % n) for s in range(n)]))
 
     stored = jnp.arange(blocks, dtype=jnp.int32)
     slot_of = ((me - stored // per_device) % n) * per_device + stored % per_device
@@ -559,7 +561,7 @@
         ).astype(jnp.int32)
 
     attn_in = attn_in.reshape(tokens, model)
-    feed_in = order(feed_in).reshape(tokens, model)
+    feed_in = feed_in.reshape(tokens, model)
     upstream_low = cotangent.reshape(tokens, model)
     activated, grad_hidden, feed_out, feed_part, feed_sums = feed_forward(
         feed_in, upstream_low, expand, thresholds, contract, span
@@ -568,10 +570,14 @@
     def dot_tn(a, b):
         return lax.dot_general(a, b, (((0,), (0,)), ((), ())), preferred_element_type=wide)
 
-    grad_contract, grad_expand = lax.psum(
-        order((dot_tn(activated, upstream_low).astype(low), dot_tn(feed_in, grad_hidden).astype(low))),
-        ("dp", "seq"),
-    )
+    grad_contract = lax.psum(dot_tn(activated, upstream_low).astype(low), ("dp", "seq"))
+    expand_sum = RowSum(
+        dot_tn(feed_in, grad_hidden),
+        steps_over("dp"),
+        lambda x: lax.psum(x.astype(low), "seq"),
+    )
+    for _ in expand_sum.steps:
+        expand_sum.step()
 
     back = []
     for r in range(rounds):
@@ -580,9 +586,7 @@
         for k in range(n):
             piece = pieces[k]
             if k:
-                piece = lax.ppermute(
-                    order(piece), "seq", [(s, (s - k) % n) for s in range(n)]
-                )
+                piece = lax.ppermute(piece, "seq", [(s, (s - k) % n) for s in range(n)])
             full = lax.dynamic_update_index_in_dim(full, piece, (me + k) % n, 0)
         back.append(full)
 
@@ -610,8 +614,6 @@
             pairs_back = pieces[0] if len(pieces) == 1 else jnp.concatenate(pieces, axis=0)
         else:
             pairs_back = jnp.stack([back[p // n][p % n] for p in pairs])
-        if s:
-            pairs_back = order(pairs_back)
         both, attended_s, linear_s, sums_s, offs_s = close(
             pairs_back,
             mixing,
@@ -619,59 +621,75 @@
             feed_out,
             feed_part,
             residual_blocks,
-            norm_scale,
+            after(norm_scale, branches[-1].sent) if branches else norm_scale,
             s * per_device,
         )
         attended.append(attended_s)
         grad_linear.append(linear_s)
         small_sums.append((sums_s, offs_s))
         mine = slice(s * local_rows, (s + 1) * local_rows)
-        branches.append(RowSum(both, tensor_steps, order, functools.partial(finish, mine)))
+        branches.append(RowSum(both, tensor_steps, functools.partial(finish, mine)))
         branches[s].step()
         if s < seq_count - 1:
             branches[s].step()
 
     attended = jnp.concatenate(attended, axis=0)
     grad_linear = jnp.concatenate(grad_linear, axis=1)
-    grad_projections = RowSum(
-        jnp.concatenate([dot_tn(attn_in, grad_linear[i]) for i in range(3)], axis=0),
-        batch_steps,
-        order,
-    )
-    grad_projections.step()
     sums = sum_small(sum(s for s, _ in small_sums)[:4], tensor_steps)
     grad_offsets = sum(o for _, o in small_sums)[:3]
     small = jnp.concatenate(
         [sums.reshape(-1), grad_offsets.reshape(-1), feed_sums[0], feed_sums[1]]
     )
     shares = 1
-    for axis, _, _ in batch_steps:
+    for _ in batch_steps:
         shares *= 2
     unit = model * shares
     padded = -(-small.shape[0] // unit) * unit
     small_rows = jnp.pad(small, (0, padded - small.shape[0])).reshape(-1, model)
-    grad_mixing = RowSum(
-        jnp.concatenate([dot_tn(attended, upstream_low), small_rows], axis=0), batch_steps, order
-    )
-    grad_mixing.step()
-    params = [grad_projections, grad_mixing]
-    while not all(b.done() for b in branches + params):
-        for chain in branches[::-1] + params:
+    params = [
+        RowSum(
+            jnp.concatenate([dot_tn(attn_in, grad_linear[i]) for i in range(3)], axis=0),
+            batch_steps,
+        ),
+        RowSum(
+            jnp.concatenate([dot_tn(attended, upstream_low), small_rows], axis=0), batch_steps
+        ),
+    ]
+    params[0].step()
+    params[1].step(params[0].sent)
+    grad_contract = grad_contract.astype(wide)
+    turn = 0
+    while not all(b.done() for b in branches + params + [expand_sum]):
+        for chain in branches[::-1]:
             chain.step()
-
-    results = jnp.stack([b.x for b in branches])
-    grad_projections = grad_projections.x.astype(wide).reshape(3, model, local)
-    small = grad_mixing.x[local:].astype(wide).reshape(-1)
-    grad_mixing = grad_mixing.x[:local].astype(wide)
-    grad_contract, grad_expand = grad_contract.astype(wide), grad_expand.astype(wide)
+        last = params[0].at == 2 * len(batch_steps) - 1
+        params[0].step(grad_contract if last else expand_sum.sent if turn > 1 else None)
+        if not params[1].done():
+            params[1].step(params[0].sent)
+        turn += 1
+        if turn > 1:
+            expand_sum.step(params[0].sent)
+    grad_expand = expand_sum.x.astype(wide)
+
+    layer_output = jnp.zeros((seq_count, local_rows, model), low)
+    grad_residual = layer_output
+    for s, chain in enumerate(branches):
+        side, *pieces = chain.last
+        for position, piece in zip((side, 1 - side), pieces):
+            at = (s, position * piece.shape[0], 0)
+            layer_output = lax.dynamic_update_slice(layer_output, piece[None, :, :model], at)
+            grad_residual = lax.dynamic_update_slice(grad_residual, piece[None, :, model:], at)
+    grad_projections = params[0].x.astype(wide).reshape(3, model, local)
+    small = params[1].x[local:].astype(wide).reshape(-1)
+    grad_mixing = params[1].x[:local].astype(wide)
     sizes = [2 * model, 2 * model, 3 * local, thresholds.shape[0], model]
     cuts = np.cumsum(sizes)
     grad_scale, grad_shift, grad_offsets, grad_thresholds, grad_baseline = jnp.split(
         small[: cuts[-1]], cuts[:-1]
     )
     return (
-        results[:, :, :model],
-        results[:, :, model:],
+        layer_output,
+        grad_residual,
         grad_projections,
         grad_offsets.reshape(3, local),
         grad_mixing,

time: 333 us -> 330 us (level)
  waiting for transfers between devices: 147 us -> 93 us
  local copies, waits for them, and re-layouts: 17.8 us -> 46.9 us
  other arithmetic: 23.7 us -> 35.6 us
  between operations: 15.2 us -> 21.1 us
    ppermute x22 -> x23, waiting for transfers between devices: 95.9 us -> 41.8 us  [the longest x11 21.8 us: step(): got = lax.ppermute(sent, axis, perm)]
    ppermute x10 -> x11, waiting for transfers between devices: 49 us -> 20.9 us  [step(): got = lax.ppermute(x, axis, perm)]
    psum x1 -> x2, waiting for transfers between devices: 0.01 us -> 26.6 us  [the longest x1 25.2 us: on_device(): lax.psum(x.astype(low), 'seq')]
    slice x0 -> x9, local copies, waits for them, and re-layouts: none -> 6.54 us  [after(): first = earlier[(0,) * earlier.ndim].astype(wide)]
    dynamic_update_slice x0 -> x5, local copies, waits for them, and re-layouts: none -> 5.92 us  [the longest x4 5.08 us: on_device(): lax.dynamic_update_slice(grad_residual, piece[None, :, model:], at)]
    add x0 -> x11, other arithmetic: none -> 5.57 us  [after(): return x + jnp.minimum(jnp.abs(first), 0.0).astype(x.dtype)]
    add x8, other arithmetic: 1.43 us -> 6.64 us  [step(): self.x = kept.astype(wide) + got.astype(wide)]
    convert_element_type x7 -> x6, local copies, waits for them, and re-layouts: 0.37 us -> 5.55 us  [step(): lax.dynamic_slice_in_dim(self.x, (1 - side) * half, half, 0).astype(low)]
  transfers between devices with their start and end apart: 35 -> 38, of which waited for: 16 -> 15; matrix products, arithmetic and copies ran while one was open for 11% -> 24% of each run, Pallas kernels for 19% -> 19%
where the time goes in v3:
time: 330 us; the launch traced here: 328 us
  waiting for transfers between devices  93 us (28%)
  Pallas kernels  72.7 us (22%)
  local copies, waits for them, and re-layouts  46.9 us (14%)
  starting transfers between devices  43.4 us (13%)
  other arithmetic  35.6 us (11%)
  between operations  21.1 us (6%)
  matrix products  15.3 us (5%)
    pallas_call x2, Pallas kernels, attention(): pl.pallas_call(functools.partial(attention_kernel, n, per_device), in_spe...  36.2 us
    psum x1, waiting for transfers between devices, on_device(): lax.psum(x.astype(low), 'seq')  25.2 us
    ppermute x11, waiting for transfers between devices, step(): got = lax.ppermute(sent, axis, perm)  21.8 us
    ppermute x11, waiting for transfers between devices, step(): got = lax.ppermute(x, axis, perm)  20.9 us
    ppermute x6, waiting for transfers between devices, on_device(): piece = lax.ppermute(piece, 'seq', [(s, (s - k) % n) for s in range(n)])  20 us
    dot_general x6, matrix products, dot_tn(): lax.dot_general(a, b, (((0,), (0,)), ((), ())), preferred_element_type=wide)  15.3 us
    pallas_call x1, Pallas kernels, feed_forward(): pl.pallas_call(feed_kernel, grid=(tokens // span,), in_specs=[rows(model)...  14.5 us
    ppermute x11, starting transfers between devices, step(): got = lax.ppermute(sent, axis, perm)  14.4 us
  transfers between devices with their start and end apart: 38, of which 15 were waited for; matrix products, arithmetic and copies ran while one was open for 24% of the time, Pallas kernels for 19%

profile of v3, /device:TPU:0, one launch (start us, length us, event | category | flops | bytes accessed | tf_op | source)
XLA Modules:
  0.0 328.1 jit_solution(12457611033627333552)
XLA Ops:
  8.6 9.6 %shard_map.221 = (bf16[8,2,2,256,128]{4,3,2,1,0:T(8,128)(2,1)}, bf16[4,256,1024]{2,1,0:T(8,128)(2,1)}, bf16[4,256,1024]{2,1,0:T(8,128)(2,1)}) custom-call(s32[4]{0:T(128)} %reshape.210.places, bf16[4,256,1024]{2,1,0:T(8,128)(2,1)} %bitcast.180, bf16[4,256,1024]{2,1,0:T(8,128)(2,1)} %bitcast.183, bf16[3,1024,256]{2,1,0:T(8,128)(2,1)} %proj.5, f32[3,256]{1,0:T(4,128)} %offs.1, ...), custom_call_target="tpu_custom_call" | custom-call | flops 2147483648 | bytes 12582912 | tf_op jit(solution)/shard_map/pallas_call | solution.py:119
  18.2 2.7 dynamic-slice_bitcast_fusion
  20.9 3.0 collective-permute-start
  23.9 2.6 collective-permute-start.1
  26.5 1.3 collective-permute-start.2
  28.9 14.5 %shard_map.223 = (bf16[1024,1024]{1,0:T(8,128)(2,1)}, bf16[1024,1024]{1,0:T(8,128)(2,1)}, f32[1024,1024]{1,0:T(8,128)}, f32[1024,1024]{1,0:T(8,128)}, f32[8,1024]{1,0:T(8,128)}) custom-call(bf16[1024,1024]{1,0:T(8,128)(2,1)} %bitcast.195, bf16[1024,1024]{1,0:T(8,128)(2,1)} %bitcast.184, bf16[1024,1024]{1,0:T(8,128)(2,1)} %expand.1, f32[1,1024]{1,0:T(1,128)} %bitcast.197, ...), custom_call_target="tpu_custom_call" | custom-call | flops 8589934592 | bytes 20971520 | tf_op jit(solution)/shard_map/pallas_call | solution.py:181
  43.4 5.3 %convolution_convert_fusion = bf16[1024,1024]{1,0:T(8,128)(2,1)} fusion(bf16[1024,1024]{1,0:T(8,128)(2,1)} %get-tuple-element.55, bf16[1024,1024]{1,0:T(8,128)(2,1)S(1)} %bitcast.185), kind=kOutput, calls=%fused_computation.7 | convolution fusion | flops 2148532224 | bytes 6291456 | tf_op jit(solution)/shard_map/dot_general | solution.py:571
  48.9 1.4 copy-done.2
  50.3 1.6 fusion.66
  52.7 1.5 fusion.65
  55.0 6.1 %fusion.70 = f32[1024,1024]{1,0:T(8,128)} fusion(bf16[1024,1024]{1,0:T(8,128)(2,1)S(1)} %bitcast.196, bf16[1024,1024]{1,0:T(8,128)(2,1)} %get-tuple-element.54), kind=kOutput, calls=%fused_computation.178 | convolution fusion | flops 2147483648 | bytes 8388608 | tf_op jit(solution)/shard_map/dot_general | solution.py:571
  61.1 1.4 convert_reduce_fusion
  65.0 2.7 dynamic-slice_convert_fusion
  68.8 3.4 %collective-permute-start.12 = (bf16[2,2,256,128]{3,2,1,0:T(8,128)(2,1)}, bf16[2,2,256,128]{3,2,1,0:T(8,128)(2,1)S(1)}, u32[]{:S(2)}, u32[]{:S(2)}) collective-permute-start(bf16[2,2,256,128]{3,2,1,0:T(8,128)(2,1)} %get-tuple-element.75), channel_id=1, source_target_pairs={{0,12},{4,0},{8,4},{12,8},{1,13},{5,1},{9,5},{13,9},{2,14},{6,2},{... | collective-permute-start | bytes 786440 | tf_op jit(solution)/shard_map/ppermute | solution.py:552
  72.2 1.6 collective-permute-start.23
  73.8 18.5 %shard_map.222 = (bf16[2,2,256,128]{3,2,1,0:T(8,128)(2,1)S(1)}, bf16[2,2,256,128]{3,2,1,0:T(8,128)(2,1)S(1)}, bf16[2,2,256,128]{3,2,1,0:T(8,128)(2,1)S(1)}, bf16[2,2,256,128]{3,2,1,0:T(8,128)(2,1)S(1)}) custom-call(s32[8]{0:T(128)S(1)} %get-tuple-element.68.slots, bf16[2,2,256,128]{3,2,1,0:T(8,128)(2,1)S(1)} %get-tuple-element.82.refs_0_, ...), custom_call_target="tpu_custom_call" | custom-call | flops 16106127360 | bytes 8388608 | tf_op jit(solution)/shard_map/pallas_call | solution.py:337
  94.2 1.9 collective-permute-start.5
  96.1 17.6 %shard_map.225 = (bf16[2,2,256,128]{3,2,1,0:T(8,128)(2,1)S(1)}, bf16[2,2,256,128]{3,2,1,0:T(8,128)(2,1)S(1)}, bf16[2,2,256,128]{3,2,1,0:T(8,128)(2,1)S(1)}, bf16[2,2,256,128]{3,2,1,0:T(8,128)(2,1)S(1)}) custom-call(s32[8]{0:T(128)S(1)} %get-tuple-element.67.slots, bf16[2,2,256,128]{3,2,1,0:T(8,128)(2,1)S(1)} %get-tuple-element.78.refs_0_, ...), custom_call_target="tpu_custom_call" | custom-call | flops 16106127360 | bytes 8388608 | tf_op jit(solution)/shard_map/pallas_call | solution.py:337
  113.7 1.9 collective-permute-start.13
  116.4 7.6 %collective-permute-done.4 = bf16[2,2,256,128]{3,2,1,0:T(8,128)(2,1)S(1)} collective-permute-done((bf16[2,2,256,128]{3,2,1,0:T(8,128)(2,1)S(1)}, bf16[2,2,256,128]{3,2,1,0:T(8,128)(2,1)S(1)}, u32[]{:S(2)}, u32[]{:S(2)}) %collective-permute-start.4) | collective-permute-done | bytes 262176 | tf_op jit(solution)/shard_map/ppermute | solution.py:589
  125.1 6.1 %shard_map.224 = (bf16[512,2048]{1,0:T(8,128)(2,1)}, bf16[512,256]{1,0:T(8,128)(2,1)}, bf16[3,512,256]{2,1,0:T(8,128)(2,1)}, f32[8,1024]{1,0:T(8,128)}, f32[8,256]{1,0:T(8,128)}) custom-call(bf16[4,2,2,256,128]{4,3,2,1,0:T(8,128)(2,1)} %copy-done.12, bf16[256,1024]{1,0:T(8,128)(2,1)} %mix.5, bf16[3,1024,256]{2,1,0:T(8,128)(2,1)} %proj.5, ...), custom_call_target="tpu_custom_call" | custom-call | flops 1073741824 | bytes 12582912 | tf_op jit(solution)/shard_map/pallas_call | solution.py:397
  131.2 1.4 constant_dynamic-slice_fusion.2
  133.1 12.4 %collective-permute-done.14 = bf16[2,2,256,128]{3,2,1,0:T(8,128)(2,1)S(1)} collective-permute-done((bf16[2,2,256,128]{3,2,1,0:T(8,128)(2,1)S(1)}, bf16[2,2,256,128]{3,2,1,0:T(8,128)(2,1)S(1)}, u32[]{:S(2)}, u32[]{:S(2)}) %collective-permute-start.14) | collective-permute-done | bytes 262176 | tf_op jit(solution)/shard_map/ppermute | solution.py:589
  146.5 1.3 copy-done.9
  151.1 6.3 %shard_map.226 = (bf16[512,2048]{1,0:T(8,128)(2,1)}, bf16[512,256]{1,0:T(8,128)(2,1)}, bf16[3,512,256]{2,1,0:T(8,128)(2,1)}, f32[8,1024]{1,0:T(8,128)}, f32[8,256]{1,0:T(8,128)}) custom-call(bf16[4,2,2,256,128]{4,3,2,1,0:T(8,128)(2,1)} %copy-done.11, bf16[256,1024]{1,0:T(8,128)(2,1)} %mix.5, bf16[3,1024,256]{2,1,0:T(8,128)(2,1)} %proj.5, ...), custom_call_target="tpu_custom_call" | custom-call | flops 1073741824 | bytes 12582912 | tf_op jit(solution)/shard_map/pallas_call | solution.py:397
  160.1 1.6 collective-permute-start.7
  162.8 1.5 copy-done.5
  164.3 1.7 fusion.45
  169.6 3.6 %collective-permute-done.28 = f32[4,1024]{1,0:T(4,128)S(1)} collective-permute-done((f32[4,1024]{1,0:T(4,128)S(1)}, f32[4,1024]{1,0:T(4,128)S(1)}, u32[]{:S(2)}, u32[]{:S(2)}) %collective-permute-start.28) | collective-permute-done | bytes 16416 | tf_op jit(solution)/shard_map/ppermute | solution.py:499
  173.2 1.9 fusion.50
  175.1 2.6 collective-permute-start.29
  177.7 3.2 add_convert_fusion
  181.1 2.4 constant_dynamic-slice_fusion
  183.5 1.7 collective-permute-done.29
  186.1 1.4 all-reduce.6.cloned.1.call-done
  189.4 4.2 %convert_element_type.257 = f32[1024,1024]{1,0:T(8,128)} convert(bf16[1024,1024]{1,0:T(8,128)(2,1)} %all-reduce.6.cloned.1.call-done) | non-fusion elementwise | flops 1048576 | bytes 6291456 | tf_op jit(solution)/shard_map/convert_element_type | solution.py:660
  197.0 3.5 %collective-permute-done.20 = bf16[1536,256]{1,0:T(8,128)(2,1)} collective-permute-done((bf16[1536,256]{1,0:T(8,128)(2,1)}, bf16[1536,256]{1,0:T(8,128)(2,1)}, u32[]{:S(2)}, u32[]{:S(2)}) %collective-permute-start.20) | collective-permute-done | bytes 786464 | tf_op jit(solution)/shard_map/ppermute | solution.py:469
  203.2 2.0 collective-permute-start.21
  205.2 11.7 %collective-permute-done.30 = bf16[66,1024]{1,0:T(8,128)(2,1)S(1)} collective-permute-done((bf16[66,1024]{1,0:T(8,128)(2,1)S(1)}, bf16[66,1024]{1,0:T(8,128)(2,1)S(1)}, u32[]{:S(2)}, u32[]{:S(2)}) %collective-permute-start.30) | collective-permute-done | bytes 135200 | tf_op jit(solution)/shard_map/ppermute | solution.py:469
  216.9 1.6 convert_add_fusion
  219.4 1.5 collective-permute-start.17
  220.8 4.7 %collective-permute-done.21 = bf16[768,256]{1,0:T(8,128)(2,1)S(1)} collective-permute-done((bf16[768,256]{1,0:T(8,128)(2,1)S(1)}, bf16[768,256]{1,0:T(8,128)(2,1)S(1)}, u32[]{:S(2)}, u32[]{:S(2)}) %collective-permute-start.21) | collective-permute-done | bytes 393248 | tf_op jit(solution)/shard_map/ppermute | solution.py:469
  226.2 2.4 collective-permute-start.22
  229.3 25.2 %all-reduce.4.cloned.1.call-done = bf16[512,1024]{1,0:T(8,128)(2,1)} async-done(((bf16[512,1024]{1,0:T(8,128)(2,1)}), bf16[512,1024]{1,0:T(8,128)(2,1)}) %all-reduce.4.cloned.1.call-update) | async-done | bytes 1048592 | tf_op jit(solution)/shard_map/psum | solution.py:577
  254.5 1.3 broadcast_add_fusion
  255.8 1.4 collective-permute-start.35
  257.7 2.6 collective-permute-start.31
  263.9 2.4 collective-permute-start.32
  266.3 8.7 %collective-permute-done.24 = bf16[384,256]{1,0:T(8,128)(2,1)S(1)} collective-permute-done((bf16[384,256]{1,0:T(8,128)(2,1)S(1)}, bf16[384,256]{1,0:T(8,128)(2,1)S(1)}, u32[]{:S(2)}, u32[]{:S(2)}) %collective-permute-start.24) | collective-permute-done | bytes 196640 | tf_op jit(solution)/shard_map/ppermute | solution.py:477
  276.9 1.6 collective-permute-start.33
  280.1 1.8 fusion.33
  281.9 1.5 collective-permute-start.8
  284.1 1.8 collective-permute-done.25
  286.7 1.3 collective-permute-start.26
  289.6 7.3 %collective-permute-done.8 = bf16[128,2048]{1,0:T(8,128)(2,1)S(1)} collective-permute-done((bf16[128,2048]{1,0:T(8,128)(2,1)S(1)}, bf16[128,2048]{1,0:T(8,128)(2,1)S(1)}, u32[]{:S(2)}, u32[]{:S(2)}) %collective-permute-start.8) | collective-permute-done | bytes 524320 | tf_op jit(solution)/shard_map/ppermute | solution.py:477
  297.2 1.6 broadcast_in_dim.84.clone.1
  299.9 1.3 copy-done.16
  301.2 2.9 collective-permute-done.18
  304.5 2.9 fusion
  310.7 1.8 maximum_select_fusion.1
  312.5 1.9 convert.5
  314.9 2.1 fusion.39
  317.9 2.1 fusion.37
  320.0 1.3 copy-done.18
  (194 shorter events, 45.2 us)
Async XLA Ops:
  7.2 180.3 %all-reduce.6.cloned.1.call-start = ((), (), s32[]{:S(2)}) async-start(), calls=%async_computation.1 | async-start | bytes 4194304 | tf_op jit(solution)/shard_map/psum | solution.py:573
  20.9 48.0 %collective-permute-start = (bf16[2,2,256,128]{3,2,1,0:T(8,128)(2,1)}, bf16[2,2,256,128]{3,2,1,0:T(8,128)(2,1)S(1)}, u32[]{:S(2)}, u32[]{:S(2)}) collective-permute-start(bf16[2,2,256,128]{3,2,1,0:T(8,128)(2,1)} %get-tuple-element.81), channel_id=1, source_target_pairs={{0,4},{4,8},{8,12},{12,0},{1,5},{5,9},{9,13},{13,1},{2,6},{6,10},{... | collective-permute-start | bytes 786440 | tf_op jit(solution)/shard_map/ppermute | solution.py:552
  23.9 48.3 %collective-permute-start.1 = (bf16[2,2,256,128]{3,2,1,0:T(8,128)(2,1)}, bf16[2,2,256,128]{3,2,1,0:T(8,128)(2,1)}, u32[]{:S(2)}, u32[]{:S(2)}) collective-permute-start(bf16[2,2,256,128]{3,2,1,0:T(8,128)(2,1)} %get-tuple-element.80), channel_id=1, source_target_pairs={{0,8},{4,12},{8,0},{12,4},{1,9},{5,13},{9,1},{13,5},{2,10},{6,14},... | collective-permute-start | bytes 786440 | tf_op jit(solution)/shard_map/ppermute | solution.py:552
  26.5 47.3 %collective-permute-start.2 = (bf16[2,2,256,128]{3,2,1,0:T(8,128)(2,1)}, bf16[2,2,256,128]{3,2,1,0:T(8,128)(2,1)}, u32[]{:S(2)}, u32[]{:S(2)}) collective-permute-start(bf16[2,2,256,128]{3,2,1,0:T(8,128)(2,1)} %get-tuple-element.79), channel_id=1, source_target_pairs={{0,12},{4,0},{8,4},{12,8},{1,13},{5,1},{9,5},{13,9},{2,14},{6,2},{... | collective-permute-start | bytes 786440 | tf_op jit(solution)/shard_map/ppermute | solution.py:552
  27.8 65.5 %collective-permute-start.10 = (bf16[2,2,256,128]{3,2,1,0:T(8,128)(2,1)}, bf16[2,2,256,128]{3,2,1,0:T(8,128)(2,1)S(1)}, u32[]{:S(2)}, u32[]{:S(2)}) collective-permute-start(bf16[2,2,256,128]{3,2,1,0:T(8,128)(2,1)} %get-tuple-element.77), channel_id=1, source_target_pairs={{0,4},{4,8},{8,12},{12,0},{1,5},{5,9},{9,13},{13,1},{2,6},{6,10},{... | collective-permute-start | bytes 786440 | tf_op jit(solution)/shard_map/ppermute | solution.py:552
  28.5 65.6 %collective-permute-start.11 = (bf16[2,2,256,128]{3,2,1,0:T(8,128)(2,1)}, bf16[2,2,256,128]{3,2,1,0:T(8,128)(2,1)S(1)}, u32[]{:S(2)}, u32[]{:S(2)}) collective-permute-start(bf16[2,2,256,128]{3,2,1,0:T(8,128)(2,1)} %get-tuple-element.76), channel_id=1, source_target_pairs={{0,8},{4,12},{8,0},{12,4},{1,9},{5,13},{9,1},{13,5},{2,10},{6,14},... | collective-permute-start | bytes 786440 | tf_op jit(solution)/shard_map/ppermute | solution.py:552
  28.8 14.5 %copy-start.3 = (bf16[2,512,1024]{2,1,0:T(8,128)(2,1)S(1)}, bf16[2,512,1024]{2,1,0:T(8,128)(2,1)}, u32[]{:S(2)}) copy-start(bf16[2,512,1024]{2,1,0:T(8,128)(2,1)} %param.25) | copy-start | bytes 6291460
  48.7 1.6 copy-start.2
  48.8 205.7 %all-reduce.4.cloned.1.call-start = ((), (), s32[]{:S(2)}) async-start(), calls=%async_computation | async-start | bytes 2097152 | tf_op jit(solution)/shard_map/psum | solution.py:577
  50.3 2.3 copy-start.4
  52.7 2.3 copy-start.31
  55.0 9.9 %copy-start.26 = (s32[2,8]{1,0:T(2,128)S(1)}, s32[2,8]{1,0:T(2,128)}, u32[]{:S(2)}) copy-start(s32[2,8]{1,0:T(2,128)} %param.15) | copy-start | bytes 196
  61.1 12.7 %copy-start = (f32[2048,128]{1,0:T(8,128)S(1)}, f32[2048,128]{1,0:T(8,128)}, u32[]{:S(2)}) copy-start(f32[2048,128]{1,0:T(8,128)} %constant.433.clone.cosine.refs_4_) | copy-start | bytes 3145732
  61.1 12.7 %copy-start.1 = (f32[2048,128]{1,0:T(8,128)S(1)}, f32[2048,128]{1,0:T(8,128)}, u32[]{:S(2)}) copy-start(f32[2048,128]{1,0:T(8,128)} %constant.434.clone.sine.refs_5_) | copy-start | bytes 3145732
  68.8 27.3 %collective-permute-start.12 = (bf16[2,2,256,128]{3,2,1,0:T(8,128)(2,1)}, bf16[2,2,256,128]{3,2,1,0:T(8,128)(2,1)S(1)}, u32[]{:S(2)}, u32[]{:S(2)}) collective-permute-start(bf16[2,2,256,128]{3,2,1,0:T(8,128)(2,1)} %get-tuple-element.75), channel_id=1, source_target_pairs={{0,12},{4,0},{8,4},{12,8},{1,13},{5,1},{9,5},{13,9},{2,14},{6,2},{... | collective-permute-start | bytes 786440 | tf_op jit(solution)/shard_map/ppermute | solution.py:552
  72.2 105.5 %collective-permute-start.23 = (bf16[512,1024]{1,0:T(8,128)(2,1)}, bf16[512,1024]{1,0:T(8,128)(2,1)}, u32[]{:S(2)}, u32[]{:S(2)}) collective-permute-start(bf16[512,1024]{1,0:T(8,128)(2,1)} %dynamic-slice_convert_fusion), channel_id=1, source_target_pairs={{0,16},{16,0},{1,17},{17,1},{2,18},{18,2},{3,19},{19,3},{4,20},{20... | collective-permute-start | bytes 3145736 | tf_op jit(solution)/shard_map/ppermute | solution.py:469
  92.3 23.6 %collective-permute-start.3 = (bf16[2,2,256,128]{3,2,1,0:T(8,128)(2,1)S(1)}, bf16[2,2,256,128]{3,2,1,0:T(8,128)(2,1)S(1)}, u32[]{:S(2)}, u32[]{:S(2)}) collective-permute-start(bf16[2,2,256,128]{3,2,1,0:T(8,128)(2,1)S(1)} %get-tuple-element.39), channel_id=1, source_target_pairs={{0,12},{4,0},{8,4},{12,8},{1,13},{5,1},{9,5},{13,9},{2,14},{6,2},{... | collective-permute-start | bytes 786440 | tf_op jit(solution)/shard_map/ppermute | solution.py:589
  93.4 30.7 %collective-permute-start.4 = (bf16[2,2,256,128]{3,2,1,0:T(8,128)(2,1)S(1)}, bf16[2,2,256,128]{3,2,1,0:T(8,128)(2,1)S(1)}, u32[]{:S(2)}, u32[]{:S(2)}) collective-permute-start(bf16[2,2,256,128]{3,2,1,0:T(8,128)(2,1)S(1)} %get-tuple-element.40), channel_id=1, source_target_pairs={{0,8},{4,12},{8,0},{12,4},{1,9},{5,13},{9,1},{13,5},{2,10},{6,14},... | collective-permute-start | bytes 786440 | tf_op jit(solution)/shard_map/ppermute | solution.py:589
  94.2 29.9 %collective-permute-start.5 = (bf16[2,2,256,128]{3,2,1,0:T(8,128)(2,1)S(1)}, bf16[2,2,256,128]{3,2,1,0:T(8,128)(2,1)S(1)}, u32[]{:S(2)}, u32[]{:S(2)}) collective-permute-start(bf16[2,2,256,128]{3,2,1,0:T(8,128)(2,1)S(1)} %get-tuple-element.41), channel_id=1, source_target_pairs={{0,4},{4,8},{8,12},{12,0},{1,5},{5,9},{9,13},{13,1},{2,6},{6,10},{... | collective-permute-start | bytes 786440 | tf_op jit(solution)/shard_map/ppermute | solution.py:589
  113.7 19.2 %collective-permute-start.13 = (bf16[2,2,256,128]{3,2,1,0:T(8,128)(2,1)S(1)}, bf16[2,2,256,128]{3,2,1,0:T(8,128)(2,1)S(1)}, u32[]{:S(2)}, u32[]{:S(2)}) collective-permute-start(bf16[2,2,256,128]{3,2,1,0:T(8,128)(2,1)S(1)} %get-tuple-element.47), channel_id=1, source_target_pairs={{0,12},{4,0},{8,4},{12,8},{1,13},{5,1},{9,5},{13,9},{2,14},{6,2},{... | collective-permute-start | bytes 786440 | tf_op jit(solution)/shard_map/ppermute | solution.py:589
  115.9 29.5 %collective-permute-start.14 = (bf16[2,2,256,128]{3,2,1,0:T(8,128)(2,1)S(1)}, bf16[2,2,256,128]{3,2,1,0:T(8,128)(2,1)S(1)}, u32[]{:S(2)}, u32[]{:S(2)}) collective-permute-start(bf16[2,2,256,128]{3,2,1,0:T(8,128)(2,1)S(1)} %get-tuple-element.48), channel_id=1, source_target_pairs={{0,8},{4,12},{8,0},{12,4},{1,9},{5,13},{9,1},{13,5},{2,10},{6,14},... | collective-permute-start | bytes 786440 | tf_op jit(solution)/shard_map/ppermute | solution.py:589
  124.0 21.4 %collective-permute-start.15 = (bf16[2,2,256,128]{3,2,1,0:T(8,128)(2,1)S(1)}, bf16[2,2,256,128]{3,2,1,0:T(8,128)(2,1)S(1)}, u32[]{:S(2)}, u32[]{:S(2)}) collective-permute-start(bf16[2,2,256,128]{3,2,1,0:T(8,128)(2,1)S(1)} %get-tuple-element.49), channel_id=1, source_target_pairs={{0,4},{4,8},{8,12},{12,0},{1,5},{5,9},{9,13},{13,1},{2,6},{6,10},{... | collective-permute-start | bytes 786440 | tf_op jit(solution)/shard_map/ppermute | solution.py:589
  131.2 1.8 copy-start.20
  132.6 13.0 %collective-permute-start.6 = (bf16[256,2048]{1,0:T(8,128)(2,1)S(1)}, bf16[256,2048]{1,0:T(8,128)(2,1)S(1)}, u32[]{:S(2)}, u32[]{:S(2)}) collective-permute-start(bf16[256,2048]{1,0:T(8,128)(2,1)S(1)} %constant_dynamic-slice_fusion.2), channel_id=1, source_target_pairs={{0,1},{1,0},{2,3},{3,2},{4,5},{5,4},{6,7},{7,6},{8,9},{9,8},{10,11... | collective-permute-start | bytes 3145736 | tf_op jit(solution)/shard_map/ppermute | solution.py:469
  132.9 12.7 %copy-start.15 = (bf16[512,2048]{1,0:T(8,128)(2,1)S(1)}, bf16[512,2048]{1,0:T(8,128)(2,1)}, u32[]{:S(2)}) copy-start(bf16[512,2048]{1,0:T(8,128)(2,1)} %get-tuple-element.45) | copy-start | bytes 6291460
  145.5 5.0 %copy-start.23 = (f32[2,1024]{1,0:T(2,128)S(1)}, f32[2,1024]{1,0:T(2,128)}, u32[]{:S(2)}) copy-start(f32[2,1024]{1,0:T(2,128)} %scale.3) | copy-start | bytes 24580
  151.1 7.5 %copy-start.30 = (bf16[4,256,1024]{2,1,0:T(8,128)(2,1)S(1)}, bf16[4,256,1024]{2,1,0:T(8,128)(2,1)}, u32[]{:S(2)}) copy-start(bf16[4,256,1024]{2,1,0:T(8,128)(2,1)} %get-tuple-element.51) | copy-start | bytes 6291460
  159.4 2.3 copy-start.24
  159.4 2.3 copy-start.25
  160.1 33.5 %collective-permute-start.7 = (bf16[128,2048]{1,0:T(8,128)(2,1)}, bf16[128,2048]{1,0:T(8,128)(2,1)}, u32[]{:S(2)}, u32[]{:S(2)}) collective-permute-start(bf16[128,2048]{1,0:T(8,128)(2,1)} %dynamic-slice_convert_fusion.3), channel_id=1, source_target_pairs={{0,2},{1,3},{2,0},{3,1},{4,6},{5,7},{6,4},{7,5},{8,10},{9,11},{10,... | collective-permute-start | bytes 1572872 | tf_op jit(solution)/shard_map/ppermute | solution.py:469
  161.7 5.3 %collective-permute-start.27 = (f32[4,1024]{1,0:T(4,128)S(1)}, f32[4,1024]{1,0:T(4,128)S(1)}, u32[]{:S(2)}, u32[]{:S(2)}) collective-permute-start(f32[4,1024]{1,0:T(4,128)S(1)} %slice_add_fusion), channel_id=1, source_target_pairs={{0,1},{1,0},{2,3},{3,2},{4,5},{5,4},{6,7},{7,6},{8,9},{9,8},{10,11... | collective-permute-start | bytes 49160 | tf_op jit(solution)/shard_map/ppermute | solution.py:499
  162.5 1.7 copy-start.5
  162.5 1.7 copy-start.21
  162.6 1.8 copy-start.22
  164.3 3.4 %copy-start.28 = (f32[8,256]{1,0:T(8,128)S(1)}, f32[8,256]{1,0:T(8,128)}, u32[]{:S(2)}) copy-start(f32[8,256]{1,0:T(8,128)} %get-tuple-element.60) | copy-start | bytes 24580
  164.3 3.4 %copy-start.29 = (f32[8,256]{1,0:T(8,128)S(1)}, f32[8,256]{1,0:T(8,128)}, u32[]{:S(2)}) copy-start(f32[8,256]{1,0:T(8,128)} %get-tuple-element.61) | copy-start | bytes 24580
  167.0 6.1 %collective-permute-start.28 = (f32[4,1024]{1,0:T(4,128)S(1)}, f32[4,1024]{1,0:T(4,128)S(1)}, u32[]{:S(2)}, u32[]{:S(2)}) collective-permute-start(f32[4,1024]{1,0:T(4,128)S(1)} %add.501), channel_id=1, source_target_pairs={{0,2},{1,3},{2,0},{3,1},{4,6},{5,7},{6,4},{7,5},{8,10},{9,11},{10,... | collective-permute-start | bytes 49160 | tf_op jit(solution)/shard_map/ppermute | solution.py:499
  175.1 10.0 %collective-permute-start.29 = (bf16[132,1024]{1,0:T(8,128)(2,1)}, bf16[132,1024]{1,0:T(8,128)(2,1)S(1)}, u32[]{:S(2)}, u32[]{:S(2)}) collective-permute-start(bf16[132,1024]{1,0:T(8,128)(2,1)} %fusion.50), channel_id=1, source_target_pairs={{0,16},{16,0},{1,17},{17,1},{2,18},{18,2},{3,19},{19,3},{4,20},{20... | collective-permute-start | bytes 811016 | tf_op jit(solution)/shard_map/ppermute | solution.py:469
  181.0 4.2 %copy-start.6 = (f32[256,1024]{1,0:T(8,128)S(1)}, f32[256,1024]{1,0:T(8,128)}, u32[]{:S(2)}) copy-start(f32[256,1024]{1,0:T(8,128)} %fusion.45) | copy-start | bytes 3145732
  181.0 19.5 %collective-permute-start.20 = (bf16[1536,256]{1,0:T(8,128)(2,1)}, bf16[1536,256]{1,0:T(8,128)(2,1)}, u32[]{:S(2)}, u32[]{:S(2)}) collective-permute-start(bf16[1536,256]{1,0:T(8,128)(2,1)} %dynamic-slice_convert_fusion.1), channel_id=1, source_target_pairs={{0,16},{16,0},{1,17},{17,1},{2,18},{18,2},{3,19},{19,3},{4,20},{20... | collective-permute-start | bytes 2359304 | tf_op jit(solution)/shard_map/ppermute | solution.py:469
  183.5 33.5 %collective-permute-start.16 = (bf16[256,2048]{1,0:T(8,128)(2,1)}, bf16[256,2048]{1,0:T(8,128)(2,1)}, u32[]{:S(2)}, u32[]{:S(2)}) collective-permute-start(bf16[256,2048]{1,0:T(8,128)(2,1)} %constant_dynamic-slice_fusion), channel_id=1, source_target_pairs={{0,1},{1,0},{2,3},{3,2},{4,5},{5,4},{6,7},{7,6},{8,9},{9,8},{10,11... | collective-permute-start | bytes 3145736 | tf_op jit(solution)/shard_map/ppermute | solution.py:469
  189.4 4.2 %copy-start.10 = (f32[256,2048]{1,0:T(8,128)S(1)}, f32[256,2048]{1,0:T(8,128)}, u32[]{:S(2)}) copy-start(f32[256,2048]{1,0:T(8,128)} %copy-done.9) | copy-start | bytes 6291460
  197.0 6.1 %copy-start.19 = (f32[132,1024]{1,0:T(8,128)S(1)}, f32[132,1024]{1,0:T(8,128)}, u32[]{:S(2)}) copy-start(f32[132,1024]{1,0:T(8,128)} %fusion.17) | copy-start | bytes 1622020
  197.0 19.9 %copy-start.14 = (bf16[512,2048]{1,0:T(8,128)(2,1)S(1)}, bf16[512,2048]{1,0:T(8,128)(2,1)}, u32[]{:S(2)}) copy-start(bf16[512,2048]{1,0:T(8,128)(2,1)} %get-tuple-element.50) | copy-start | bytes 6291460
  203.1 13.8 %collective-permute-start.30 = (bf16[66,1024]{1,0:T(8,128)(2,1)S(1)}, bf16[66,1024]{1,0:T(8,128)(2,1)S(1)}, u32[]{:S(2)}, u32[]{:S(2)}) collective-permute-start(bf16[66,1024]{1,0:T(8,128)(2,1)S(1)} %fusion.53), channel_id=1, source_target_pairs={{0,4},{4,0},{8,12},{12,8},{1,5},{5,1},{9,13},{13,9},{2,6},{6,2},{1... | collective-permute-start | bytes 405512 | tf_op jit(solution)/shard_map/ppermute | solution.py:469
  203.2 22.4 %collective-permute-start.21 = (bf16[768,256]{1,0:T(8,128)(2,1)S(1)}, bf16[768,256]{1,0:T(8,128)(2,1)S(1)}, u32[]{:S(2)}, u32[]{:S(2)}) collective-permute-start(bf16[768,256]{1,0:T(8,128)(2,1)S(1)} %dynamic-slice_convert_fusion.4), channel_id=1, source_target_pairs={{0,4},{4,0},{8,12},{12,8},{1,5},{5,1},{9,13},{13,9},{2,6},{6,2},{1... | collective-permute-start | bytes 1179656 | tf_op jit(solution)/shard_map/ppermute | solution.py:469
  219.4 59.2 %collective-permute-start.17 = (bf16[128,2048]{1,0:T(8,128)(2,1)}, bf16[128,2048]{1,0:T(8,128)(2,1)}, u32[]{:S(2)}, u32[]{:S(2)}) collective-permute-start(bf16[128,2048]{1,0:T(8,128)(2,1)} %dynamic-slice_convert_fusion.2), channel_id=1, source_target_pairs={{0,2},{1,3},{2,0},{3,1},{4,6},{5,7},{6,4},{7,5},{8,10},{9,11},{10,... | collective-permute-start | bytes 1572872 | tf_op jit(solution)/shard_map/ppermute | solution.py:469
  226.2 34.8 %collective-permute-start.22 = (bf16[384,256]{1,0:T(8,128)(2,1)S(1)}, bf16[384,256]{1,0:T(8,128)(2,1)}, u32[]{:S(2)}, u32[]{:S(2)}) collective-permute-start(bf16[384,256]{1,0:T(8,128)(2,1)S(1)} %dynamic-slice_convert_fusion.5), channel_id=1, source_target_pairs={{0,8},{4,12},{8,0},{12,4},{1,9},{5,13},{9,1},{13,5},{2,10},{6,14},... | collective-permute-start | bytes 589832 | tf_op jit(solution)/shard_map/ppermute | solution.py:469
  255.8 48.7 %collective-permute-start.35 = (bf16[512,1024]{1,0:T(8,128)(2,1)S(1)}, bf16[512,1024]{1,0:T(8,128)(2,1)S(1)}, u32[]{:S(2)}, u32[]{:S(2)}) collective-permute-start(bf16[512,1024]{1,0:T(8,128)(2,1)S(1)} %broadcast_add_fusion), channel_id=1, source_target_pairs={{0,16},{16,0},{1,17},{17,1},{2,18},{18,2},{3,19},{19,3},{4,20},{20... | collective-permute-start | bytes 3145736 | tf_op jit(solution)/shard_map/ppermute | solution.py:477
  257.7 6.1 %collective-permute-start.31 = (bf16[33,1024]{1,0:T(8,128)(2,1)S(1)}, bf16[33,1024]{1,0:T(8,128)(2,1)S(1)}, u32[]{:S(2)}, u32[]{:S(2)}) collective-permute-start(bf16[33,1024]{1,0:T(8,128)(2,1)S(1)} %fusion.55), channel_id=1, source_target_pairs={{0,8},{4,12},{8,0},{12,4},{1,9},{5,13},{9,1},{13,5},{2,10},{6,14},... | collective-permute-start | bytes 202760 | tf_op jit(solution)/shard_map/ppermute | solution.py:469
  262.0 17.7 %copy-start.13 = (bf16[1,512,1024]{2,1,0:T(8,128)(2,1)S(1)}, bf16[1,512,1024]{2,1,0:T(8,128)(2,1)}, u32[]{:S(2)}) copy-start(bf16[1,512,1024]{2,1,0:T(8,128)(2,1)} %get-tuple-element.73) | copy-start | bytes 3145732
  262.5 12.5 %collective-permute-start.24 = (bf16[384,256]{1,0:T(8,128)(2,1)S(1)}, bf16[384,256]{1,0:T(8,128)(2,1)S(1)}, u32[]{:S(2)}, u32[]{:S(2)}) collective-permute-start(bf16[384,256]{1,0:T(8,128)(2,1)S(1)} %fusion.52), channel_id=1, source_target_pairs={{0,8},{4,12},{8,0},{12,4},{1,9},{5,13},{9,1},{13,5},{2,10},{6,14},... | collective-permute-start | bytes 589832 | tf_op jit(solution)/shard_map/ppermute | solution.py:477
  263.9 16.1 %copy-start.8 = (f32[128,2048]{1,0:T(8,128)S(1)}, f32[128,2048]{1,0:T(8,128)}, u32[]{:S(2)}) copy-start(f32[128,2048]{1,0:T(8,128)} %copy-done.7) | copy-start | bytes 3145732
  263.9 16.1 %copy-start.27 = (f32[1024]{0:T(1024)S(1)}, f32[1024]{0:T(1024)}, u32[]{:S(2)}) copy-start(f32[1024]{0:T(1024)} %param.19) | copy-start | bytes 12292
  263.9 13.0 %collective-permute-start.32 = (bf16[33,1024]{1,0:T(8,128)(2,1)S(1)}, bf16[33,1024]{1,0:T(8,128)(2,1)S(1)}, u32[]{:S(2)}, u32[]{:S(2)}) collective-permute-start(bf16[33,1024]{1,0:T(8,128)(2,1)S(1)} %fusion.56), channel_id=1, source_target_pairs={{0,8},{4,12},{8,0},{12,4},{1,9},{5,13},{9,1},{13,5},{2,10},{6,14},... | collective-permute-start | bytes 202760 | tf_op jit(solution)/shard_map/ppermute | solution.py:477
  275.7 10.2 %collective-permute-start.25 = (bf16[768,256]{1,0:T(8,128)(2,1)S(1)}, bf16[768,256]{1,0:T(8,128)(2,1)S(1)}, u32[]{:S(2)}, u32[]{:S(2)}) collective-permute-start(bf16[768,256]{1,0:T(8,128)(2,1)S(1)} %fusion.49), channel_id=1, source_target_pairs={{0,4},{4,0},{8,12},{12,8},{1,5},{5,1},{9,13},{13,9},{2,6},{6,2},{1... | collective-permute-start | bytes 1179656 | tf_op jit(solution)/shard_map/ppermute | solution.py:477
  276.9 11.7 %collective-permute-start.33 = (bf16[66,1024]{1,0:T(8,128)(2,1)S(1)}, bf16[66,1024]{1,0:T(8,128)(2,1)S(1)}, u32[]{:S(2)}, u32[]{:S(2)}) collective-permute-start(bf16[66,1024]{1,0:T(8,128)(2,1)S(1)} %fusion.54), channel_id=1, source_target_pairs={{0,4},{4,0},{8,12},{12,8},{1,5},{5,1},{9,13},{13,9},{2,6},{6,2},{1... | collective-permute-start | bytes 405512 | tf_op jit(solution)/shard_map/ppermute | solution.py:477
  281.9 14.9 %collective-permute-start.8 = (bf16[128,2048]{1,0:T(8,128)(2,1)S(1)}, bf16[128,2048]{1,0:T(8,128)(2,1)S(1)}, u32[]{:S(2)}, u32[]{:S(2)}) collective-permute-start(bf16[128,2048]{1,0:T(8,128)(2,1)S(1)} %pad_maximum_fusion.1), channel_id=1, source_target_pairs={{0,2},{1,3},{2,0},{3,1},{4,6},{5,7},{6,4},{7,5},{8,10},{9,11},{10,... | collective-permute-start | bytes 1572872 | tf_op jit(solution)/shard_map/ppermute | solution.py:477
  283.5 20.6 %collective-permute-start.18 = (bf16[128,2048]{1,0:T(8,128)(2,1)S(1)}, bf16[128,2048]{1,0:T(8,128)(2,1)S(1)}, u32[]{:S(2)}, u32[]{:S(2)}) collective-permute-start(bf16[128,2048]{1,0:T(8,128)(2,1)S(1)} %pad_maximum_fusion.2), channel_id=1, source_target_pairs={{0,2},{1,3},{2,0},{3,1},{4,6},{5,7},{6,4},{7,5},{8,10},{9,11},{10,... | collective-permute-start | bytes 1572872 | tf_op jit(solution)/shard_map/ppermute | solution.py:477
  286.7 24.0 %collective-permute-start.26 = (bf16[1536,256]{1,0:T(8,128)(2,1)S(1)}, bf16[1536,256]{1,0:T(8,128)(2,1)}, u32[]{:S(2)}, u32[]{:S(2)}) collective-permute-start(bf16[1536,256]{1,0:T(8,128)(2,1)S(1)} %fusion.1), channel_id=1, source_target_pairs={{0,16},{16,0},{1,17},{17,1},{2,18},{18,2},{3,19},{19,3},{4,20},{20... | collective-permute-start | bytes 2359304 | tf_op jit(solution)/shard_map/ppermute | solution.py:477
  288.8 18.8 %collective-permute-start.34 = (bf16[132,1024]{1,0:T(8,128)(2,1)S(1)}, bf16[132,1024]{1,0:T(8,128)(2,1)S(1)}, u32[]{:S(2)}, u32[]{:S(2)}) collective-permute-start(bf16[132,1024]{1,0:T(8,128)(2,1)S(1)} %fusion.51), channel_id=1, source_target_pairs={{0,16},{16,0},{1,17},{17,1},{2,18},{18,2},{3,19},{19,3},{4,20},{20... | collective-permute-start | bytes 811016 | tf_op jit(solution)/shard_map/ppermute | solution.py:477
  297.1 17.3 %collective-permute-start.9 = (bf16[256,2048]{1,0:T(8,128)(2,1)S(1)}, bf16[256,2048]{1,0:T(8,128)(2,1)}, u32[]{:S(2)}, u32[]{:S(2)}) collective-permute-start(bf16[256,2048]{1,0:T(8,128)(2,1)S(1)} %maximum_select_fusion.2), channel_id=1, source_target_pairs={{0,1},{1,0},{2,3},{3,2},{4,5},{5,4},{6,7},{7,6},{8,9},{9,8},{10,11... | collective-permute-start | bytes 3145736 | tf_op jit(solution)/shard_map/ppermute | solution.py:477
  304.4 13.5 %collective-permute-start.19 = (bf16[256,2048]{1,0:T(8,128)(2,1)S(1)}, bf16[256,2048]{1,0:T(8,128)(2,1)}, u32[]{:S(2)}, u32[]{:S(2)}) collective-permute-start(bf16[256,2048]{1,0:T(8,128)(2,1)S(1)} %maximum_select_fusion.3), channel_id=1, source_target_pairs={{0,1},{1,0},{2,3},{3,2},{4,5},{5,4},{6,7},{7,6},{8,9},{9,8},{10,11... | collective-permute-start | bytes 3145736 | tf_op jit(solution)/shard_map/ppermute | solution.py:477
  312.5 2.4 copy-start.17
  (6 other events, 6.9 us)
Sparse Core Ops, SparseCore 0:
  48.9 138.5 all-reduce.5
  190.5 63.9 all-reduce.3

commit v4 on v3

--- a/solution.py
+++ b/solution.py
@@ -663,7 +663,7 @@
         for chain in branches[::-1]:
             chain.step()
         last = params[0].at == 2 * len(batch_steps) - 1
-        params[0].step(grad_contract if last else expand_sum.sent if turn > 1 else None)
+        params[0].step(grad_contract if last else None)
         if not params[1].done():
             params[1].step(params[0].sent)
         turn += 1

time: 330 us -> 329 us (level)
  no operation moved by 1% of the time
where the time goes in v4:
time: 329 us; the launch traced here: 328 us
  waiting for transfers between devices  94 us (29%)
  Pallas kernels  72.7 us (22%)
  local copies, waits for them, and re-layouts  46.4 us (14%)
  starting transfers between devices  43.5 us (13%)
  other arithmetic  35.5 us (11%)
  between operations  20.5 us (6%)
  matrix products  15.3 us (5%)
    pallas_call x2, Pallas kernels, attention(): pl.pallas_call(functools.partial(attention_kernel, n, per_device), in_spe...  36.2 us
    psum x1, waiting for transfers between devices, on_device(): lax.psum(x.astype(low), 'seq')  25.2 us
    ppermute x11, waiting for transfers between devices, step(): got = lax.ppermute(sent, axis, perm)  23 us
    ppermute x11, waiting for transfers between devices, step(): got = lax.ppermute(x, axis, perm)  21.2 us
    ppermute x6, waiting for transfers between devices, on_device(): piece = lax.ppermute(piece, 'seq', [(s, (s - k) % n) for s in range(n)])  20 us
    dot_general x6, matrix products, dot_tn(): lax.dot_general(a, b, (((0,), (0,)), ((), ())), preferred_element_type=wide)  15.3 us
    pallas_call x1, Pallas kernels, feed_forward(): pl.pallas_call(feed_kernel, grid=(tokens // span,), in_specs=[rows(model)...  14.5 us
    ppermute x11, starting transfers between devices, step(): got = lax.ppermute(sent, axis, perm)  14.3 us
  transfers between devices with their start and end apart: 38, of which 15 were waited for; matrix products, arithmetic and copies ran while one was open for 24% of the time, Pallas kernels for 19%

profile of v4, /device:TPU:0, one launch (start us, length us, event | category | flops | bytes accessed | tf_op | source)
XLA Modules:
  0.0 328.1 jit_solution(1542963175589135303)
XLA Ops:
  8.6 9.6 %shard_map.221 = (bf16[8,2,2,256,128]{4,3,2,1,0:T(8,128)(2,1)}, bf16[4,256,1024]{2,1,0:T(8,128)(2,1)}, bf16[4,256,1024]{2,1,0:T(8,128)(2,1)}) custom-call(s32[4]{0:T(128)} %reshape.205.places, bf16[4,256,1024]{2,1,0:T(8,128)(2,1)} %bitcast.179, bf16[4,256,1024]{2,1,0:T(8,128)(2,1)} %bitcast.182, bf16[3,1024,256]{2,1,0:T(8,128)(2,1)} %proj.5, f32[3,256]{1,0:T(4,128)} %offs.1, ...), custom_call_target="tpu_custom_call" | custom-call | flops 2147483648 | bytes 12582912 | tf_op jit(solution)/shard_map/pallas_call | solution.py:119
  18.2 2.7 dynamic-slice_bitcast_fusion
  20.9 3.0 collective-permute-start
  23.9 2.6 collective-permute-start.1
  26.5 1.3 collective-permute-start.2
  28.9 14.5 %shard_map.223 = (bf16[1024,1024]{1,0:T(8,128)(2,1)}, bf16[1024,1024]{1,0:T(8,128)(2,1)}, f32[1024,1024]{1,0:T(8,128)}, f32[1024,1024]{1,0:T(8,128)}, f32[8,1024]{1,0:T(8,128)}) custom-call(bf16[1024,1024]{1,0:T(8,128)(2,1)} %bitcast.194, bf16[1024,1024]{1,0:T(8,128)(2,1)} %bitcast.183, bf16[1024,1024]{1,0:T(8,128)(2,1)} %expand.1, f32[1,1024]{1,0:T(1,128)} %bitcast.196, ...), custom_call_target="tpu_custom_call" | custom-call | flops 8589934592 | bytes 20971520 | tf_op jit(solution)/shard_map/pallas_call | solution.py:181
  43.4 5.3 %convolution_convert_fusion = bf16[1024,1024]{1,0:T(8,128)(2,1)} fusion(bf16[1024,1024]{1,0:T(8,128)(2,1)} %get-tuple-element.54, bf16[1024,1024]{1,0:T(8,128)(2,1)S(1)} %bitcast.184), kind=kOutput, calls=%fused_computation.7 | convolution fusion | flops 2148532224 | bytes 6291456 | tf_op jit(solution)/shard_map/dot_general | solution.py:571
  48.9 1.4 copy-done.2
  50.3 1.6 fusion.64
  52.7 1.5 fusion.63
  55.0 6.1 %fusion.68 = f32[1024,1024]{1,0:T(8,128)} fusion(bf16[1024,1024]{1,0:T(8,128)(2,1)S(1)} %bitcast.195, bf16[1024,1024]{1,0:T(8,128)(2,1)} %get-tuple-element.62), kind=kOutput, calls=%fused_computation.176 | convolution fusion | flops 2147483648 | bytes 8388608 | tf_op jit(solution)/shard_map/dot_general | solution.py:571
  61.1 1.4 convert_reduce_fusion
  65.0 2.7 dynamic-slice_convert_fusion
  68.8 3.4 %collective-permute-start.12 = (bf16[2,2,256,128]{3,2,1,0:T(8,128)(2,1)}, bf16[2,2,256,128]{3,2,1,0:T(8,128)(2,1)S(1)}, u32[]{:S(2)}, u32[]{:S(2)}) collective-permute-start(bf16[2,2,256,128]{3,2,1,0:T(8,128)(2,1)} %get-tuple-element.75), channel_id=1, source_target_pairs={{0,12},{4,0},{8,4},{12,8},{1,13},{5,1},{9,5},{13,9},{2,14},{6,2},{... | collective-permute-start | bytes 786440 | tf_op jit(solution)/shard_map/ppermute | solution.py:552
  72.2 1.5 collective-permute-start.34
  73.8 18.5 %shard_map.222 = (bf16[2,2,256,128]{3,2,1,0:T(8,128)(2,1)S(1)}, bf16[2,2,256,128]{3,2,1,0:T(8,128)(2,1)S(1)}, bf16[2,2,256,128]{3,2,1,0:T(8,128)(2,1)S(1)}, bf16[2,2,256,128]{3,2,1,0:T(8,128)(2,1)S(1)}) custom-call(s32[8]{0:T(128)S(1)} %get-tuple-element.68.slots, bf16[2,2,256,128]{3,2,1,0:T(8,128)(2,1)S(1)} %get-tuple-element.82.refs_0_, ...), custom_call_target="tpu_custom_call" | custom-call | flops 16106127360 | bytes 8388608 | tf_op jit(solution)/shard_map/pallas_call | solution.py:337
  94.1 1.9 collective-permute-start.5
  96.1 17.6 %shard_map.225 = (bf16[2,2,256,128]{3,2,1,0:T(8,128)(2,1)S(1)}, bf16[2,2,256,128]{3,2,1,0:T(8,128)(2,1)S(1)}, bf16[2,2,256,128]{3,2,1,0:T(8,128)(2,1)S(1)}, bf16[2,2,256,128]{3,2,1,0:T(8,128)(2,1)S(1)}) custom-call(s32[8]{0:T(128)S(1)} %get-tuple-element.67.slots, bf16[2,2,256,128]{3,2,1,0:T(8,128)(2,1)S(1)} %get-tuple-element.78.refs_0_, ...), custom_call_target="tpu_custom_call" | custom-call | flops 16106127360 | bytes 8388608 | tf_op jit(solution)/shard_map/pallas_call | solution.py:337
  113.7 1.9 collective-permute-start.13
  116.4 7.4 %collective-permute-done.4 = bf16[2,2,256,128]{3,2,1,0:T(8,128)(2,1)S(1)} collective-permute-done((bf16[2,2,256,128]{3,2,1,0:T(8,128)(2,1)S(1)}, bf16[2,2,256,128]{3,2,1,0:T(8,128)(2,1)S(1)}, u32[]{:S(2)}, u32[]{:S(2)}) %collective-permute-start.4) | collective-permute-done | bytes 262176 | tf_op jit(solution)/shard_map/ppermute | solution.py:589
  124.9 6.1 %shard_map.224 = (bf16[512,2048]{1,0:T(8,128)(2,1)}, bf16[512,256]{1,0:T(8,128)(2,1)}, bf16[3,512,256]{2,1,0:T(8,128)(2,1)}, f32[8,1024]{1,0:T(8,128)}, f32[8,256]{1,0:T(8,128)}) custom-call(bf16[4,2,2,256,128]{4,3,2,1,0:T(8,128)(2,1)} %copy-done.12, bf16[256,1024]{1,0:T(8,128)(2,1)} %mix.5, bf16[3,1024,256]{2,1,0:T(8,128)(2,1)} %proj.5, ...), custom_call_target="tpu_custom_call" | custom-call | flops 1073741824 | bytes 12582912 | tf_op jit(solution)/shard_map/pallas_call | solution.py:397
  131.0 1.4 constant_dynamic-slice_fusion.2
  132.9 12.6 %collective-permute-done.14 = bf16[2,2,256,128]{3,2,1,0:T(8,128)(2,1)S(1)} collective-permute-done((bf16[2,2,256,128]{3,2,1,0:T(8,128)(2,1)S(1)}, bf16[2,2,256,128]{3,2,1,0:T(8,128)(2,1)S(1)}, u32[]{:S(2)}, u32[]{:S(2)}) %collective-permute-start.14) | collective-permute-done | bytes 262176 | tf_op jit(solution)/shard_map/ppermute | solution.py:589
  146.5 1.3 copy-done.9
  151.1 6.3 %shard_map.226 = (bf16[512,2048]{1,0:T(8,128)(2,1)}, bf16[512,256]{1,0:T(8,128)(2,1)}, bf16[3,512,256]{2,1,0:T(8,128)(2,1)}, f32[8,1024]{1,0:T(8,128)}, f32[8,256]{1,0:T(8,128)}) custom-call(bf16[4,2,2,256,128]{4,3,2,1,0:T(8,128)(2,1)} %copy-done.11, bf16[256,1024]{1,0:T(8,128)(2,1)} %mix.5, bf16[3,1024,256]{2,1,0:T(8,128)(2,1)} %proj.5, ...), custom_call_target="tpu_custom_call" | custom-call | flops 1073741824 | bytes 12582912 | tf_op jit(solution)/shard_map/pallas_call | solution.py:397
  160.1 1.6 collective-permute-start.7
  162.8 1.5 copy-done.5
  164.3 1.7 fusion.45
  169.6 3.6 %collective-permute-done.27 = f32[4,1024]{1,0:T(4,128)S(1)} collective-permute-done((f32[4,1024]{1,0:T(4,128)S(1)}, f32[4,1024]{1,0:T(4,128)S(1)}, u32[]{:S(2)}, u32[]{:S(2)}) %collective-permute-start.27) | collective-permute-done | bytes 16416 | tf_op jit(solution)/shard_map/ppermute | solution.py:499
  173.2 1.9 fusion.49
  175.2 2.6 collective-permute-start.28
  177.7 3.2 add_convert_fusion
  181.1 2.4 constant_dynamic-slice_fusion
  183.5 1.7 collective-permute-done.28
  188.9 4.2 %convert_element_type.236 = f32[1024,1024]{1,0:T(8,128)} convert(bf16[1024,1024]{1,0:T(8,128)(2,1)} %all-reduce.4.cloned.1.call-done) | non-fusion elementwise | flops 1048576 | bytes 6291456 | tf_op jit(solution)/shard_map/convert_element_type | solution.py:660
  196.5 4.0 %collective-permute-done.20 = bf16[1536,256]{1,0:T(8,128)(2,1)} collective-permute-done((bf16[1536,256]{1,0:T(8,128)(2,1)}, bf16[1536,256]{1,0:T(8,128)(2,1)}, u32[]{:S(2)}, u32[]{:S(2)}) %collective-permute-start.20) | collective-permute-done | bytes 786464 | tf_op jit(solution)/shard_map/ppermute | solution.py:469
  200.5 1.3 convert_add_fusion.2
  203.2 2.0 collective-permute-start.21
  205.2 11.7 %collective-permute-done.29 = bf16[66,1024]{1,0:T(8,128)(2,1)S(1)} collective-permute-done((bf16[66,1024]{1,0:T(8,128)(2,1)S(1)}, bf16[66,1024]{1,0:T(8,128)(2,1)S(1)}, u32[]{:S(2)}, u32[]{:S(2)}) %collective-permute-start.29) | collective-permute-done | bytes 135200 | tf_op jit(solution)/shard_map/ppermute | solution.py:469
  217.0 1.6 convert_add_fusion
  219.4 1.5 collective-permute-start.17
  220.9 4.7 %collective-permute-done.21 = bf16[768,256]{1,0:T(8,128)(2,1)S(1)} collective-permute-done((bf16[768,256]{1,0:T(8,128)(2,1)S(1)}, bf16[768,256]{1,0:T(8,128)(2,1)S(1)}, u32[]{:S(2)}, u32[]{:S(2)}) %collective-permute-start.21) | collective-permute-done | bytes 393248 | tf_op jit(solution)/shard_map/ppermute | solution.py:469
  226.2 2.4 collective-permute-start.22
  229.3 25.2 %all-reduce.6.cloned.1.call-done = bf16[512,1024]{1,0:T(8,128)(2,1)} async-done(((bf16[512,1024]{1,0:T(8,128)(2,1)}), bf16[512,1024]{1,0:T(8,128)(2,1)}) %all-reduce.6.cloned.1.call-update) | async-done | bytes 1048592 | tf_op jit(solution)/shard_map/psum | solution.py:577
  254.5 1.3 broadcast_add_fusion
  255.8 1.4 collective-permute-start.35
  257.3 2.6 collective-permute-start.30
  263.4 2.5 collective-permute-start.31
  266.0 8.4 %collective-permute-done.23 = bf16[384,256]{1,0:T(8,128)(2,1)S(1)} collective-permute-done((bf16[384,256]{1,0:T(8,128)(2,1)S(1)}, bf16[384,256]{1,0:T(8,128)(2,1)S(1)}, u32[]{:S(2)}, u32[]{:S(2)}) %collective-permute-start.23) | collective-permute-done | bytes 196640 | tf_op jit(solution)/shard_map/ppermute | solution.py:477
  276.5 1.4 collective-permute-start.32
  279.4 1.8 fusion.33
  281.3 1.5 collective-permute-start.8
  283.5 2.3 collective-permute-done.24
  288.0 1.5 collective-permute-start.33
  289.4 6.8 %collective-permute-done.8 = bf16[128,2048]{1,0:T(8,128)(2,1)S(1)} collective-permute-done((bf16[128,2048]{1,0:T(8,128)(2,1)S(1)}, bf16[128,2048]{1,0:T(8,128)(2,1)S(1)}, u32[]{:S(2)}, u32[]{:S(2)}) %collective-permute-start.8) | collective-permute-done | bytes 524320 | tf_op jit(solution)/shard_map/ppermute | solution.py:477
  296.5 1.6 broadcast_in_dim.84.clone.1
  299.3 1.3 copy-done.16
  300.6 3.3 %collective-permute-done.18 = bf16[128,2048]{1,0:T(8,128)(2,1)S(1)} collective-permute-done((bf16[128,2048]{1,0:T(8,128)(2,1)S(1)}, bf16[128,2048]{1,0:T(8,128)(2,1)S(1)}, u32[]{:S(2)}, u32[]{:S(2)}) %collective-permute-start.18) | collective-permute-done | bytes 524320 | tf_op jit(solution)/shard_map/ppermute | solution.py:477
  304.3 2.9 fusion
  310.7 1.8 maximum_select_fusion.1
  312.5 1.9 convert.5
  314.9 2.1 fusion.39
  317.8 2.1 fusion.37
  319.9 1.3 copy-done.18
  (193 shorter events, 45.2 us)
Async XLA Ops:
  7.2 179.9 %all-reduce.4.cloned.1.call-start = ((), (), s32[]{:S(2)}) async-start(), calls=%async_computation | async-start | bytes 4194304 | tf_op jit(solution)/shard_map/psum | solution.py:573
  20.9 48.0 %collective-permute-start = (bf16[2,2,256,128]{3,2,1,0:T(8,128)(2,1)}, bf16[2,2,256,128]{3,2,1,0:T(8,128)(2,1)S(1)}, u32[]{:S(2)}, u32[]{:S(2)}) collective-permute-start(bf16[2,2,256,128]{3,2,1,0:T(8,128)(2,1)} %get-tuple-element.81), channel_id=1, source_target_pairs={{0,4},{4,8},{8,12},{12,0},{1,5},{5,9},{9,13},{13,1},{2,6},{6,10},{... | collective-permute-start | bytes 786440 | tf_op jit(solution)/shard_map/ppermute | solution.py:552
  23.9 48.3 %collective-permute-start.1 = (bf16[2,2,256,128]{3,2,1,0:T(8,128)(2,1)}, bf16[2,2,256,128]{3,2,1,0:T(8,128)(2,1)}, u32[]{:S(2)}, u32[]{:S(2)}) collective-permute-start(bf16[2,2,256,128]{3,2,1,0:T(8,128)(2,1)} %get-tuple-element.80), channel_id=1, source_target_pairs={{0,8},{4,12},{8,0},{12,4},{1,9},{5,13},{9,1},{13,5},{2,10},{6,14},... | collective-permute-start | bytes 786440 | tf_op jit(solution)/shard_map/ppermute | solution.py:552
  26.5 47.3 %collective-permute-start.2 = (bf16[2,2,256,128]{3,2,1,0:T(8,128)(2,1)}, bf16[2,2,256,128]{3,2,1,0:T(8,128)(2,1)}, u32[]{:S(2)}, u32[]{:S(2)}) collective-permute-start(bf16[2,2,256,128]{3,2,1,0:T(8,128)(2,1)} %get-tuple-element.79), channel_id=1, source_target_pairs={{0,12},{4,0},{8,4},{12,8},{1,13},{5,1},{9,5},{13,9},{2,14},{6,2},{... | collective-permute-start | bytes 786440 | tf_op jit(solution)/shard_map/ppermute | solution.py:552
  27.8 65.5 %collective-permute-start.10 = (bf16[2,2,256,128]{3,2,1,0:T(8,128)(2,1)}, bf16[2,2,256,128]{3,2,1,0:T(8,128)(2,1)S(1)}, u32[]{:S(2)}, u32[]{:S(2)}) collective-permute-start(bf16[2,2,256,128]{3,2,1,0:T(8,128)(2,1)} %get-tuple-element.77), channel_id=1, source_target_pairs={{0,4},{4,8},{8,12},{12,0},{1,5},{5,9},{9,13},{13,1},{2,6},{6,10},{... | collective-permute-start | bytes 786440 | tf_op jit(solution)/shard_map/ppermute | solution.py:552
  28.5 65.6 %collective-permute-start.11 = (bf16[2,2,256,128]{3,2,1,0:T(8,128)(2,1)}, bf16[2,2,256,128]{3,2,1,0:T(8,128)(2,1)S(1)}, u32[]{:S(2)}, u32[]{:S(2)}) collective-permute-start(bf16[2,2,256,128]{3,2,1,0:T(8,128)(2,1)} %get-tuple-element.76), channel_id=1, source_target_pairs={{0,8},{4,12},{8,0},{12,4},{1,9},{5,13},{9,1},{13,5},{2,10},{6,14},... | collective-permute-start | bytes 786440 | tf_op jit(solution)/shard_map/ppermute | solution.py:552
  28.8 14.5 %copy-start.3 = (bf16[2,512,1024]{2,1,0:T(8,128)(2,1)S(1)}, bf16[2,512,1024]{2,1,0:T(8,128)(2,1)}, u32[]{:S(2)}) copy-start(bf16[2,512,1024]{2,1,0:T(8,128)(2,1)} %param.25) | copy-start | bytes 6291460
  48.7 1.6 copy-start.2
  48.8 205.7 %all-reduce.6.cloned.1.call-start = ((), (), s32[]{:S(2)}) async-start(), calls=%async_computation.1 | async-start | bytes 2097152 | tf_op jit(solution)/shard_map/psum | solution.py:577
  50.3 2.3 copy-start.4
  52.7 2.3 copy-start.31
  55.0 9.9 %copy-start.26 = (s32[2,8]{1,0:T(2,128)S(1)}, s32[2,8]{1,0:T(2,128)}, u32[]{:S(2)}) copy-start(s32[2,8]{1,0:T(2,128)} %param.15) | copy-start | bytes 196
  61.1 12.6 %copy-start = (f32[2048,128]{1,0:T(8,128)S(1)}, f32[2048,128]{1,0:T(8,128)}, u32[]{:S(2)}) copy-start(f32[2048,128]{1,0:T(8,128)} %constant.432.clone.cosine.refs_4_) | copy-start | bytes 3145732
  61.1 12.6 %copy-start.1 = (f32[2048,128]{1,0:T(8,128)S(1)}, f32[2048,128]{1,0:T(8,128)}, u32[]{:S(2)}) copy-start(f32[2048,128]{1,0:T(8,128)} %constant.433.clone.sine.refs_5_) | copy-start | bytes 3145732
  68.8 27.2 %collective-permute-start.12 = (bf16[2,2,256,128]{3,2,1,0:T(8,128)(2,1)}, bf16[2,2,256,128]{3,2,1,0:T(8,128)(2,1)S(1)}, u32[]{:S(2)}, u32[]{:S(2)}) collective-permute-start(bf16[2,2,256,128]{3,2,1,0:T(8,128)(2,1)} %get-tuple-element.75), channel_id=1, source_target_pairs={{0,12},{4,0},{8,4},{12,8},{1,13},{5,1},{9,5},{13,9},{2,14},{6,2},{... | collective-permute-start | bytes 786440 | tf_op jit(solution)/shard_map/ppermute | solution.py:552
  72.2 105.5 %collective-permute-start.34 = (bf16[512,1024]{1,0:T(8,128)(2,1)}, bf16[512,1024]{1,0:T(8,128)(2,1)}, u32[]{:S(2)}, u32[]{:S(2)}) collective-permute-start(bf16[512,1024]{1,0:T(8,128)(2,1)} %dynamic-slice_convert_fusion), channel_id=1, source_target_pairs={{0,16},{16,0},{1,17},{17,1},{2,18},{18,2},{3,19},{19,3},{4,20},{20... | collective-permute-start | bytes 3145736 | tf_op jit(solution)/shard_map/ppermute | solution.py:469
  92.3 23.6 %collective-permute-start.3 = (bf16[2,2,256,128]{3,2,1,0:T(8,128)(2,1)S(1)}, bf16[2,2,256,128]{3,2,1,0:T(8,128)(2,1)S(1)}, u32[]{:S(2)}, u32[]{:S(2)}) collective-permute-start(bf16[2,2,256,128]{3,2,1,0:T(8,128)(2,1)S(1)} %get-tuple-element.39), channel_id=1, source_target_pairs={{0,12},{4,0},{8,4},{12,8},{1,13},{5,1},{9,5},{13,9},{2,14},{6,2},{... | collective-permute-start | bytes 786440 | tf_op jit(solution)/shard_map/ppermute | solution.py:589
  93.4 30.5 %collective-permute-start.4 = (bf16[2,2,256,128]{3,2,1,0:T(8,128)(2,1)S(1)}, bf16[2,2,256,128]{3,2,1,0:T(8,128)(2,1)S(1)}, u32[]{:S(2)}, u32[]{:S(2)}) collective-permute-start(bf16[2,2,256,128]{3,2,1,0:T(8,128)(2,1)S(1)} %get-tuple-element.40), channel_id=1, source_target_pairs={{0,8},{4,12},{8,0},{12,4},{1,9},{5,13},{9,1},{13,5},{2,10},{6,14},... | collective-permute-start | bytes 786440 | tf_op jit(solution)/shard_map/ppermute | solution.py:589
  94.1 29.7 %collective-permute-start.5 = (bf16[2,2,256,128]{3,2,1,0:T(8,128)(2,1)S(1)}, bf16[2,2,256,128]{3,2,1,0:T(8,128)(2,1)S(1)}, u32[]{:S(2)}, u32[]{:S(2)}) collective-permute-start(bf16[2,2,256,128]{3,2,1,0:T(8,128)(2,1)S(1)} %get-tuple-element.41), channel_id=1, source_target_pairs={{0,4},{4,8},{8,12},{12,0},{1,5},{5,9},{9,13},{13,1},{2,6},{6,10},{... | collective-permute-start | bytes 786440 | tf_op jit(solution)/shard_map/ppermute | solution.py:589
  113.7 19.0 %collective-permute-start.13 = (bf16[2,2,256,128]{3,2,1,0:T(8,128)(2,1)S(1)}, bf16[2,2,256,128]{3,2,1,0:T(8,128)(2,1)S(1)}, u32[]{:S(2)}, u32[]{:S(2)}) collective-permute-start(bf16[2,2,256,128]{3,2,1,0:T(8,128)(2,1)S(1)} %get-tuple-element.47), channel_id=1, source_target_pairs={{0,12},{4,0},{8,4},{12,8},{1,13},{5,1},{9,5},{13,9},{2,14},{6,2},{... | collective-permute-start | bytes 786440 | tf_op jit(solution)/shard_map/ppermute | solution.py:589
  115.9 29.5 %collective-permute-start.14 = (bf16[2,2,256,128]{3,2,1,0:T(8,128)(2,1)S(1)}, bf16[2,2,256,128]{3,2,1,0:T(8,128)(2,1)S(1)}, u32[]{:S(2)}, u32[]{:S(2)}) collective-permute-start(bf16[2,2,256,128]{3,2,1,0:T(8,128)(2,1)S(1)} %get-tuple-element.48), channel_id=1, source_target_pairs={{0,8},{4,12},{8,0},{12,4},{1,9},{5,13},{9,1},{13,5},{2,10},{6,14},... | collective-permute-start | bytes 786440 | tf_op jit(solution)/shard_map/ppermute | solution.py:589
  123.8 21.6 %collective-permute-start.15 = (bf16[2,2,256,128]{3,2,1,0:T(8,128)(2,1)S(1)}, bf16[2,2,256,128]{3,2,1,0:T(8,128)(2,1)S(1)}, u32[]{:S(2)}, u32[]{:S(2)}) collective-permute-start(bf16[2,2,256,128]{3,2,1,0:T(8,128)(2,1)S(1)} %get-tuple-element.49), channel_id=1, source_target_pairs={{0,4},{4,8},{8,12},{12,0},{1,5},{5,9},{9,13},{13,1},{2,6},{6,10},{... | collective-permute-start | bytes 786440 | tf_op jit(solution)/shard_map/ppermute | solution.py:589
  131.0 1.8 copy-start.20
  132.4 13.2 %collective-permute-start.6 = (bf16[256,2048]{1,0:T(8,128)(2,1)S(1)}, bf16[256,2048]{1,0:T(8,128)(2,1)S(1)}, u32[]{:S(2)}, u32[]{:S(2)}) collective-permute-start(bf16[256,2048]{1,0:T(8,128)(2,1)S(1)} %constant_dynamic-slice_fusion.2), channel_id=1, source_target_pairs={{0,1},{1,0},{2,3},{3,2},{4,5},{5,4},{6,7},{7,6},{8,9},{9,8},{10,11... | collective-permute-start | bytes 3145736 | tf_op jit(solution)/shard_map/ppermute | solution.py:469
  132.7 12.9 %copy-start.15 = (bf16[512,2048]{1,0:T(8,128)(2,1)S(1)}, bf16[512,2048]{1,0:T(8,128)(2,1)}, u32[]{:S(2)}) copy-start(bf16[512,2048]{1,0:T(8,128)(2,1)} %get-tuple-element.45) | copy-start | bytes 6291460
  145.5 5.0 %copy-start.23 = (f32[2,1024]{1,0:T(2,128)S(1)}, f32[2,1024]{1,0:T(2,128)}, u32[]{:S(2)}) copy-start(f32[2,1024]{1,0:T(2,128)} %scale.3) | copy-start | bytes 24580
  151.1 7.5 %copy-start.30 = (bf16[4,256,1024]{2,1,0:T(8,128)(2,1)S(1)}, bf16[4,256,1024]{2,1,0:T(8,128)(2,1)}, u32[]{:S(2)}) copy-start(bf16[4,256,1024]{2,1,0:T(8,128)(2,1)} %get-tuple-element.51) | copy-start | bytes 6291460
  159.4 2.3 copy-start.24
  159.4 2.3 copy-start.25
  160.1 33.0 %collective-permute-start.7 = (bf16[128,2048]{1,0:T(8,128)(2,1)}, bf16[128,2048]{1,0:T(8,128)(2,1)}, u32[]{:S(2)}, u32[]{:S(2)}) collective-permute-start(bf16[128,2048]{1,0:T(8,128)(2,1)} %dynamic-slice_convert_fusion.3), channel_id=1, source_target_pairs={{0,2},{1,3},{2,0},{3,1},{4,6},{5,7},{6,4},{7,5},{8,10},{9,11},{10,... | collective-permute-start | bytes 1572872 | tf_op jit(solution)/shard_map/ppermute | solution.py:469
  161.7 5.3 %collective-permute-start.26 = (f32[4,1024]{1,0:T(4,128)S(1)}, f32[4,1024]{1,0:T(4,128)S(1)}, u32[]{:S(2)}, u32[]{:S(2)}) collective-permute-start(f32[4,1024]{1,0:T(4,128)S(1)} %slice_add_fusion), channel_id=1, source_target_pairs={{0,1},{1,0},{2,3},{3,2},{4,5},{5,4},{6,7},{7,6},{8,9},{9,8},{10,11... | collective-permute-start | bytes 49160 | tf_op jit(solution)/shard_map/ppermute | solution.py:499
  162.5 1.7 copy-start.5
  162.6 1.7 copy-start.21
  162.6 1.8 copy-start.22
  164.3 3.4 %copy-start.28 = (f32[8,256]{1,0:T(8,128)S(1)}, f32[8,256]{1,0:T(8,128)}, u32[]{:S(2)}) copy-start(f32[8,256]{1,0:T(8,128)} %get-tuple-element.59) | copy-start | bytes 24580
  164.3 3.4 %copy-start.29 = (f32[8,256]{1,0:T(8,128)S(1)}, f32[8,256]{1,0:T(8,128)}, u32[]{:S(2)}) copy-start(f32[8,256]{1,0:T(8,128)} %get-tuple-element.60) | copy-start | bytes 24580
  167.0 6.2 %collective-permute-start.27 = (f32[4,1024]{1,0:T(4,128)S(1)}, f32[4,1024]{1,0:T(4,128)S(1)}, u32[]{:S(2)}, u32[]{:S(2)}) collective-permute-start(f32[4,1024]{1,0:T(4,128)S(1)} %add.480), channel_id=1, source_target_pairs={{0,2},{1,3},{2,0},{3,1},{4,6},{5,7},{6,4},{7,5},{8,10},{9,11},{10,... | collective-permute-start | bytes 49160 | tf_op jit(solution)/shard_map/ppermute | solution.py:499
  175.2 10.0 %collective-permute-start.28 = (bf16[132,1024]{1,0:T(8,128)(2,1)}, bf16[132,1024]{1,0:T(8,128)(2,1)S(1)}, u32[]{:S(2)}, u32[]{:S(2)}) collective-permute-start(bf16[132,1024]{1,0:T(8,128)(2,1)} %fusion.49), channel_id=1, source_target_pairs={{0,16},{16,0},{1,17},{17,1},{2,18},{18,2},{3,19},{19,3},{4,20},{20... | collective-permute-start | bytes 811016 | tf_op jit(solution)/shard_map/ppermute | solution.py:469
  181.0 4.2 %copy-start.6 = (f32[256,1024]{1,0:T(8,128)S(1)}, f32[256,1024]{1,0:T(8,128)}, u32[]{:S(2)}) copy-start(f32[256,1024]{1,0:T(8,128)} %fusion.45) | copy-start | bytes 3145732
  181.0 19.5 %collective-permute-start.20 = (bf16[1536,256]{1,0:T(8,128)(2,1)}, bf16[1536,256]{1,0:T(8,128)(2,1)}, u32[]{:S(2)}, u32[]{:S(2)}) collective-permute-start(bf16[1536,256]{1,0:T(8,128)(2,1)} %dynamic-slice_convert_fusion.1), channel_id=1, source_target_pairs={{0,16},{16,0},{1,17},{17,1},{2,18},{18,2},{3,19},{19,3},{4,20},{20... | collective-permute-start | bytes 2359304 | tf_op jit(solution)/shard_map/ppermute | solution.py:469
  183.5 33.5 %collective-permute-start.16 = (bf16[256,2048]{1,0:T(8,128)(2,1)}, bf16[256,2048]{1,0:T(8,128)(2,1)}, u32[]{:S(2)}, u32[]{:S(2)}) collective-permute-start(bf16[256,2048]{1,0:T(8,128)(2,1)} %constant_dynamic-slice_fusion), channel_id=1, source_target_pairs={{0,1},{1,0},{2,3},{3,2},{4,5},{5,4},{6,7},{7,6},{8,9},{9,8},{10,11... | collective-permute-start | bytes 3145736 | tf_op jit(solution)/shard_map/ppermute | solution.py:469
  188.9 4.2 %copy-start.10 = (f32[256,2048]{1,0:T(8,128)S(1)}, f32[256,2048]{1,0:T(8,128)}, u32[]{:S(2)}) copy-start(f32[256,2048]{1,0:T(8,128)} %copy-done.9) | copy-start | bytes 6291460
  196.5 6.5 %copy-start.19 = (f32[132,1024]{1,0:T(8,128)S(1)}, f32[132,1024]{1,0:T(8,128)}, u32[]{:S(2)}) copy-start(f32[132,1024]{1,0:T(8,128)} %fusion.17) | copy-start | bytes 1622020
  196.5 20.4 %copy-start.14 = (bf16[512,2048]{1,0:T(8,128)(2,1)S(1)}, bf16[512,2048]{1,0:T(8,128)(2,1)}, u32[]{:S(2)}) copy-start(bf16[512,2048]{1,0:T(8,128)(2,1)} %get-tuple-element.50) | copy-start | bytes 6291460
  203.1 13.8 %collective-permute-start.29 = (bf16[66,1024]{1,0:T(8,128)(2,1)S(1)}, bf16[66,1024]{1,0:T(8,128)(2,1)S(1)}, u32[]{:S(2)}, u32[]{:S(2)}) collective-permute-start(bf16[66,1024]{1,0:T(8,128)(2,1)S(1)} %fusion.51), channel_id=1, source_target_pairs={{0,4},{4,0},{8,12},{12,8},{1,5},{5,1},{9,13},{13,9},{2,6},{6,2},{1... | collective-permute-start | bytes 405512 | tf_op jit(solution)/shard_map/ppermute | solution.py:469
  203.2 22.4 %collective-permute-start.21 = (bf16[768,256]{1,0:T(8,128)(2,1)S(1)}, bf16[768,256]{1,0:T(8,128)(2,1)S(1)}, u32[]{:S(2)}, u32[]{:S(2)}) collective-permute-start(bf16[768,256]{1,0:T(8,128)(2,1)S(1)} %dynamic-slice_convert_fusion.4), channel_id=1, source_target_pairs={{0,4},{4,0},{8,12},{12,8},{1,5},{5,1},{9,13},{13,9},{2,6},{6,2},{1... | collective-permute-start | bytes 1179656 | tf_op jit(solution)/shard_map/ppermute | solution.py:469
  219.4 58.5 %collective-permute-start.17 = (bf16[128,2048]{1,0:T(8,128)(2,1)}, bf16[128,2048]{1,0:T(8,128)(2,1)}, u32[]{:S(2)}, u32[]{:S(2)}) collective-permute-start(bf16[128,2048]{1,0:T(8,128)(2,1)} %dynamic-slice_convert_fusion.2), channel_id=1, source_target_pairs={{0,2},{1,3},{2,0},{3,1},{4,6},{5,7},{6,4},{7,5},{8,10},{9,11},{10,... | collective-permute-start | bytes 1572872 | tf_op jit(solution)/shard_map/ppermute | solution.py:469
  226.2 33.7 %collective-permute-start.22 = (bf16[384,256]{1,0:T(8,128)(2,1)S(1)}, bf16[384,256]{1,0:T(8,128)(2,1)}, u32[]{:S(2)}, u32[]{:S(2)}) collective-permute-start(bf16[384,256]{1,0:T(8,128)(2,1)S(1)} %dynamic-slice_convert_fusion.5), channel_id=1, source_target_pairs={{0,8},{4,12},{8,0},{12,4},{1,9},{5,13},{9,1},{13,5},{2,10},{6,14},... | collective-permute-start | bytes 589832 | tf_op jit(solution)/shard_map/ppermute | solution.py:469
  255.8 48.5 %collective-permute-start.35 = (bf16[512,1024]{1,0:T(8,128)(2,1)S(1)}, bf16[512,1024]{1,0:T(8,128)(2,1)S(1)}, u32[]{:S(2)}, u32[]{:S(2)}) collective-permute-start(bf16[512,1024]{1,0:T(8,128)(2,1)S(1)} %broadcast_add_fusion), channel_id=1, source_target_pairs={{0,16},{16,0},{1,17},{17,1},{2,18},{18,2},{3,19},{19,3},{4,20},{20... | collective-permute-start | bytes 3145736 | tf_op jit(solution)/shard_map/ppermute | solution.py:477
  257.3 6.1 %collective-permute-start.30 = (bf16[33,1024]{1,0:T(8,128)(2,1)S(1)}, bf16[33,1024]{1,0:T(8,128)(2,1)S(1)}, u32[]{:S(2)}, u32[]{:S(2)}) collective-permute-start(bf16[33,1024]{1,0:T(8,128)(2,1)S(1)} %fusion.53), channel_id=1, source_target_pairs={{0,8},{4,12},{8,0},{12,4},{1,9},{5,13},{9,1},{13,5},{2,10},{6,14},... | collective-permute-start | bytes 202760 | tf_op jit(solution)/shard_map/ppermute | solution.py:469
  260.9 18.3 %copy-start.13 = (bf16[1,512,1024]{2,1,0:T(8,128)(2,1)S(1)}, bf16[1,512,1024]{2,1,0:T(8,128)(2,1)}, u32[]{:S(2)}) copy-start(bf16[1,512,1024]{2,1,0:T(8,128)(2,1)} %get-tuple-element.73) | copy-start | bytes 3145732
  261.4 13.0 %collective-permute-start.23 = (bf16[384,256]{1,0:T(8,128)(2,1)S(1)}, bf16[384,256]{1,0:T(8,128)(2,1)S(1)}, u32[]{:S(2)}, u32[]{:S(2)}) collective-permute-start(bf16[384,256]{1,0:T(8,128)(2,1)S(1)} %add_convert_fusion.1), channel_id=1, source_target_pairs={{0,8},{4,12},{8,0},{12,4},{1,9},{5,13},{9,1},{13,5},{2,10},{6,14},... | collective-permute-start | bytes 589832 | tf_op jit(solution)/shard_map/ppermute | solution.py:477
  263.4 16.0 %copy-start.8 = (f32[128,2048]{1,0:T(8,128)S(1)}, f32[128,2048]{1,0:T(8,128)}, u32[]{:S(2)}) copy-start(f32[128,2048]{1,0:T(8,128)} %copy-done.7) | copy-start | bytes 3145732
  263.4 16.0 %copy-start.27 = (f32[1024]{0:T(1024)S(1)}, f32[1024]{0:T(1024)}, u32[]{:S(2)}) copy-start(f32[1024]{0:T(1024)} %param.19) | copy-start | bytes 12292
  263.4 13.0 %collective-permute-start.31 = (bf16[33,1024]{1,0:T(8,128)(2,1)S(1)}, bf16[33,1024]{1,0:T(8,128)(2,1)S(1)}, u32[]{:S(2)}, u32[]{:S(2)}) collective-permute-start(bf16[33,1024]{1,0:T(8,128)(2,1)S(1)} %fusion.54), channel_id=1, source_target_pairs={{0,8},{4,12},{8,0},{12,4},{1,9},{5,13},{9,1},{13,5},{2,10},{6,14},... | collective-permute-start | bytes 202760 | tf_op jit(solution)/shard_map/ppermute | solution.py:477
  275.1 10.7 %collective-permute-start.24 = (bf16[768,256]{1,0:T(8,128)(2,1)S(1)}, bf16[768,256]{1,0:T(8,128)(2,1)S(1)}, u32[]{:S(2)}, u32[]{:S(2)}) collective-permute-start(bf16[768,256]{1,0:T(8,128)(2,1)S(1)} %maximum_select_fusion.6), channel_id=1, source_target_pairs={{0,4},{4,0},{8,12},{12,8},{1,5},{5,1},{9,13},{13,9},{2,6},{6,2},{1... | collective-permute-start | bytes 1179656 | tf_op jit(solution)/shard_map/ppermute | solution.py:477
  276.5 11.3 %collective-permute-start.32 = (bf16[66,1024]{1,0:T(8,128)(2,1)S(1)}, bf16[66,1024]{1,0:T(8,128)(2,1)S(1)}, u32[]{:S(2)}, u32[]{:S(2)}) collective-permute-start(bf16[66,1024]{1,0:T(8,128)(2,1)S(1)} %fusion.52), channel_id=1, source_target_pairs={{0,4},{4,0},{8,12},{12,8},{1,5},{5,1},{9,13},{13,9},{2,6},{6,2},{1... | collective-permute-start | bytes 405512 | tf_op jit(solution)/shard_map/ppermute | solution.py:477
  281.3 14.9 %collective-permute-start.8 = (bf16[128,2048]{1,0:T(8,128)(2,1)S(1)}, bf16[128,2048]{1,0:T(8,128)(2,1)S(1)}, u32[]{:S(2)}, u32[]{:S(2)}) collective-permute-start(bf16[128,2048]{1,0:T(8,128)(2,1)S(1)} %pad_maximum_fusion.1), channel_id=1, source_target_pairs={{0,2},{1,3},{2,0},{3,1},{4,6},{5,7},{6,4},{7,5},{8,10},{9,11},{10,... | collective-permute-start | bytes 1572872 | tf_op jit(solution)/shard_map/ppermute | solution.py:477
  282.9 21.1 %collective-permute-start.18 = (bf16[128,2048]{1,0:T(8,128)(2,1)S(1)}, bf16[128,2048]{1,0:T(8,128)(2,1)S(1)}, u32[]{:S(2)}, u32[]{:S(2)}) collective-permute-start(bf16[128,2048]{1,0:T(8,128)(2,1)S(1)} %pad_maximum_fusion.2), channel_id=1, source_target_pairs={{0,2},{1,3},{2,0},{3,1},{4,6},{5,7},{6,4},{7,5},{8,10},{9,11},{10,... | collective-permute-start | bytes 1572872 | tf_op jit(solution)/shard_map/ppermute | solution.py:477
  286.6 24.1 %collective-permute-start.25 = (bf16[1536,256]{1,0:T(8,128)(2,1)S(1)}, bf16[1536,256]{1,0:T(8,128)(2,1)}, u32[]{:S(2)}, u32[]{:S(2)}) collective-permute-start(bf16[1536,256]{1,0:T(8,128)(2,1)S(1)} %fusion.1), channel_id=1, source_target_pairs={{0,16},{16,0},{1,17},{17,1},{2,18},{18,2},{3,19},{19,3},{4,20},{20... | collective-permute-start | bytes 2359304 | tf_op jit(solution)/shard_map/ppermute | solution.py:477
  288.0 19.6 %collective-permute-start.33 = (bf16[132,1024]{1,0:T(8,128)(2,1)S(1)}, bf16[132,1024]{1,0:T(8,128)(2,1)S(1)}, u32[]{:S(2)}, u32[]{:S(2)}) collective-permute-start(bf16[132,1024]{1,0:T(8,128)(2,1)S(1)} %fusion.50), channel_id=1, source_target_pairs={{0,16},{16,0},{1,17},{17,1},{2,18},{18,2},{3,19},{19,3},{4,20},{20... | collective-permute-start | bytes 811016 | tf_op jit(solution)/shard_map/ppermute | solution.py:477
  296.5 17.9 %collective-permute-start.9 = (bf16[256,2048]{1,0:T(8,128)(2,1)S(1)}, bf16[256,2048]{1,0:T(8,128)(2,1)}, u32[]{:S(2)}, u32[]{:S(2)}) collective-permute-start(bf16[256,2048]{1,0:T(8,128)(2,1)S(1)} %maximum_select_fusion.2), channel_id=1, source_target_pairs={{0,1},{1,0},{2,3},{3,2},{4,5},{5,4},{6,7},{7,6},{8,9},{9,8},{10,11... | collective-permute-start | bytes 3145736 | tf_op jit(solution)/shard_map/ppermute | solution.py:477
  304.2 13.7 %collective-permute-start.19 = (bf16[256,2048]{1,0:T(8,128)(2,1)S(1)}, bf16[256,2048]{1,0:T(8,128)(2,1)}, u32[]{:S(2)}, u32[]{:S(2)}) collective-permute-start(bf16[256,2048]{1,0:T(8,128)(2,1)S(1)} %maximum_select_fusion.3), channel_id=1, source_target_pairs={{0,1},{1,0},{2,3},{3,2},{4,5},{5,4},{6,7},{7,6},{8,9},{9,8},{10,11... | collective-permute-start | bytes 3145736 | tf_op jit(solution)/shard_map/ppermute | solution.py:477
  312.5 2.4 copy-start.17
  (6 other events, 6.9 us)
Sparse Core Ops, SparseCore 0:
  48.9 138.1 all-reduce.3
  190.0 64.4 all-reduce.5
